TPU v7x, 32 devices: a whole 2x2x4 slice. The times are simulated.
32 devices in a mesh: dp: 4 (over y, core), frame: 4 (over z), mp: 2 (over x).
Axes of the slice: x: 2, y: 2, z: 4, core: 2. Of those that a mesh axis runs over, the one named last changes fastest.
Arguments:
- projected: bfloat16 [6, 4, 16, 128, 5120], P(None, 'dp', 'frame', None, 'mp'), may hold values from -6 to 6
- codes: float32 [4, 16, 32], P('dp'), may hold values from -6 to 6
- action_weight: float32 [32, 5120], P(None, 'mp'), may hold values from -1 to 1
- clip_ids: int32 [4], replicated, may hold values from 0 to 3, each once
- frame_map: int32 [16], replicated, may hold values from 0 to 15, each once
- segments: int32 [4, 16], P('dp'), may hold values from 0 to 2, never falling along the last dimension, each value on 1 to 8 neighbouring positions
Outputs:
- mixed: bfloat16 [4, 16, 128, 5120], P('dp', 'frame', None, 'mp')
Inputs may be any that keep to these rules, and one draw needn't show every extreme that they name: `clip_ids`: each clip id appears once. `frame_map`: each time appears once. `segments`: episode numbers never fall along time.
All inputs are finite; a program needn't handle non-finite values.
Results may differ from a plain program's by a relative error of at most 0.0085.
Values may be sent and summed in bfloat16 or wider, within the bound.
No kernel may reach another device: no remote copies, remote signals or barrier semaphores. Data moves between devices by JAX's collectives and lax.ppermute only.
A program may use at most 128 MiB of HBM per device.

v0:
```python
import jax
import jax.numpy as jnp
from jax import lax
from jax.sharding import PartitionSpec as P

E = 128


def masked_softmax(spatial_scores, allowed):
    peak = jnp.max(jnp.where(allowed, spatial_scores, -1e30), axis=-1, keepdims=True)
    weights = jnp.where(allowed, jnp.exp(spatial_scores - peak), 0.0)
    return (weights / jnp.sum(weights, axis=-1, keepdims=True)).astype(jnp.bfloat16)


def local(projected, codes, action_weight, clip_ids, frame_map, segments):
    clip_dev, frames_dev, patches, width = projected.shape[1:]
    heads_dev = width // E
    frames_all = frame_map.shape[0]
    score_scale = 1.0 / E**0.5
    head_patches = lax.Precision.HIGHEST
    reshaped_rows = projected.reshape(6, clip_dev, frames_dev, patches, heads_dev, E)
    all_codes = lax.all_gather(codes, "dp", axis=0, tiled=True)
    owned = lax.axis_index("dp") * clip_dev + jnp.arange(clip_dev, dtype=jnp.int32)
    select = (clip_ids[:, None] == owned[None, :]).astype(jnp.float32)
    by_clip = jnp.einsum("ic,ifa->cfa", select, all_codes, precision=head_patches)
    local_times = lax.dynamic_slice_in_dim(
        frame_map, lax.axis_index("frame") * frames_dev, frames_dev
    )
    pick = (local_times[:, None] == jnp.arange(frames_all, dtype=jnp.int32)[None, :]).astype(
        jnp.float32
    )
    codes_slot = jnp.einsum("st,cta->csa", pick, by_clip, precision=head_patches)
    action_rows = jnp.einsum("csa,ad->csd", codes_slot, action_weight, precision=head_patches)
    values_t = (
        reshaped_rows[5].astype(jnp.float32)
        + action_rows.reshape(clip_dev, frames_dev, 1, heads_dev, E)
    ).astype(jnp.bfloat16)
    temporal_in = jnp.stack([reshaped_rows[3], reshaped_rows[4], values_t])
    match = frame_map[:, None] == jnp.arange(frames_all, dtype=jnp.int32)[None, :]
    seg_slot = jnp.sum(jnp.where(match[None], segments[:, None, :], 0), axis=-1)
    allowed = (frame_map[None, :] <= frame_map[:, None])[None] & (
        seg_slot[:, None, :] == seg_slot[:, :, None]
    )
    gathered = lax.all_to_all(temporal_in, "frame", split_axis=3, concat_axis=2, tiled=True)
    tscores = (
        jnp.einsum(
            "csphe,ctphe->cphst", gathered[0], gathered[1], preferred_element_type=jnp.float32
        )
        * score_scale
    )
    tprobs = masked_softmax(tscores, allowed[:, None, None])
    finished = jnp.einsum(
        "cphst,ctphe->csphe", tprobs, gathered[2], preferred_element_type=jnp.float32
    ).astype(jnp.bfloat16)
    temporal = lax.all_to_all(finished, "frame", split_axis=1, concat_axis=2, tiled=True)
    spatial_scores = (
        jnp.einsum(
            "cfphe,cfqhe->cfhpq",
            reshaped_rows[0],
            reshaped_rows[1],
            preferred_element_type=jnp.float32,
        )
        * score_scale
    )
    probs = masked_softmax(spatial_scores, jnp.ones((1, 1, 1, 1, 1), bool))
    spatial = jnp.einsum(
        "cfhpq,cfqhe->cfphe", probs, reshaped_rows[2], preferred_element_type=jnp.float32
    ).astype(jnp.bfloat16)
    mixed = (spatial.astype(jnp.float32) + temporal.astype(jnp.float32)).astype(jnp.bfloat16)
    return mixed.reshape(clip_dev, frames_dev, patches, width)


def solution(mesh):
    return jax.shard_map(
        local,
        mesh=mesh,
        in_specs=(
            P(None, "dp", "frame", None, "mp"),
            P("dp", None, None),
            P(None, "mp"),
            P(),
            P(),
            P("dp", None),
        ),
        out_specs=P("dp", "frame", None, "mp"),
        check_vma=False,
    )
```

profile of v0, /device:TPU:0, one launch (start us, length us, event | category | flops | bytes accessed | tf_op | source)
XLA Modules:
  0.0 351.8 jit_solution(15035384974300789328)
XLA Ops:
  0.0 6.5 %all_gather.3 = f32[4,16,32]{2,1,0:T(8,128)S(1)} all-gather(f32[1,16,32]{2,1,0:T(8,128)} %param.7), channel_id=1, replica_groups=mesh['dp'=4,'frame'=4,'mp'=2] {'dp'}, dimensions={0}, use_global_device_ids=true | all-gather | bytes 10240 | tf_op jit(solution)/shard_map/all_gather | solution.py:22
  8.6 11.6 %fusion.33 = (bf16[1,1,4,128,2560]{4,3,2,1,0:T(8,128)(2,1)}, bf16[1,1,4,128,2560]{4,3,2,1,0:T(8,128)(2,1)}, bf16[1,1,4,128,2560]{4,3,2,1,0:T(8,128)(2,1)}, bf16[...) fusion(bf16[6,1,4,128,2560]{4,3,2,1,0:T(8,128)(2,1)} %param.6), kind=kLoop, calls=%fused_computation.44 | loop fusion | bytes 31457280 | tf_op jit(solution)/shard_map/slice | solution.py:60
  20.1 3.2 copy.129
  23.4 4.4 %copy.127 = bf16[1,1,4,128,2560]{3,4,2,1,0:T(8,128)(2,1)} copy(bf16[1,1,4,128,2560]{4,3,2,1,0:T(8,128)(2,1)} %get-tuple-element.7) | data formatting | bytes 5242880
  27.8 4.4 %copy.128 = bf16[1,1,4,128,2560]{3,4,2,1,0:T(8,128)(2,1)} copy(bf16[1,1,4,128,2560]{4,3,2,1,0:T(8,128)(2,1)} %get-tuple-element.6) | data formatting | bytes 5242880
  34.7 3.7 %pad_maximum_fusion = bf16[3,1,4,128,20,128]{3,5,4,2,1,0:T(8,128)(2,1)} fusion(bf16[1,1,4,128,20,128]{3,5,4,2,1,0:T(8,128)(2,1)S(1)} %fusion.2, bf16[1,1,4,128,20,128]{3,5,4,2,1,0:T(8,128)(2,1)S(1)} %bitcast.73, bf16[1,1,4,128,20,128]{3,5,4,2,1,0:T(8,128)(2,1)S(1)} %bitcast.72), kind=kLoop, calls=%fused_computation.2 | loop fusion | flops 7864320 | bytes 15728640 | tf_op jit(solution)/shard_map/stack | solution.py:38
  38.4 14.0 %copy.108 = bf16[3,1,4,128,20,128]{5,2,4,1,0,3:T(4,128)(2,1)} copy(bf16[3,1,4,128,20,128]{3,5,4,2,1,0:T(8,128)(2,1)} %pad_maximum_fusion) | data formatting | bytes 15728640 | tf_op jit(solution)/shard_map/stack | solution.py:38
  52.4 5.7 %all-to-all-start = ((bf16[3,1,4,128,20,128]{5,2,4,1,0,3:T(4,128)(2,1)}), bf16[3,1,4,128,20,128]{5,2,4,1,0,3:T(4,128)(2,1)}, u32[]{:S(2)}, u32[]{:S(2)}) async-start(bf16[3,1,4,128,20,128]{5,2,4,1,0,3:T(4,128)(2,1)} %copy.108), calls=%async_computation | async-start | bytes 15728640 | tf_op jit(solution)/shard_map/all_to_all | solution.py:44
  58.4 172.8 %all-to-all-done = bf16[3,1,4,128,20,128]{5,2,4,1,0,3:T(4,128)(2,1)} async-done(((bf16[3,1,4,128,20,128]{5,2,4,1,0,3:T(4,128)(2,1)}), bf16[3,1,4,128,20,128]{5,2,4,1,0,3:T(4,128)(2,1)}, u32[]{:S(2)}, u32[]{:S(2)}) %all-to-all-start) | async-done | bytes 7864352 | tf_op jit(solution)/shard_map/all_to_all | solution.py:44
  231.2 5.3 %copy.109 = bf16[3,1,4,128,20,128]{5,3,4,2,0,1:T(8,128)(2,1)S(1)} copy(bf16[3,1,4,128,20,128]{5,2,4,1,0,3:T(4,128)(2,1)} %all-to-all-done) | data formatting | bytes 15728640 | tf_op jit(solution)/shard_map/all_to_all | solution.py:44
  241.7 3.6 %copy.112 = bf16[1,1,4,4,32,20,128]{6,3,2,5,4,1,0:T(4,128)(2,1)} copy(bf16[1,1,4,4,32,20,128]{6,4,2,5,3,0,1:T(8,128)(2,1)S(1)} %get-tuple-element.11) | data formatting | bytes 5242880 | tf_op jit(solution)/shard_map/slice | solution.py:47
  245.2 3.5 %copy.110 = bf16[1,1,4,4,32,20,128]{6,3,2,5,4,1,0:T(4,128)(2,1)} copy(bf16[1,1,4,4,32,20,128]{6,4,2,5,3,0,1:T(8,128)(2,1)S(1)} %get-tuple-element.13) | data formatting | bytes 5242880 | tf_op jit(solution)/shard_map/slice | solution.py:53
  248.8 8.4 %fusion.35 = (f32[32,20,16]{2,1,0:T(8,128)S(1)}, f32[32,20,16,16]{2,3,1,0:T(8,128)}) fusion(pred[16,16]{0,1:T(8,128)(4,1)S(1)} %compare_and_fusion, bf16[16,32,20,128]{3,0,2,1:T(8,128)(2,1)S(1)} %bitcast.75, bf16[16,32,20,128]{3,0,2,1:T(8,128)(2,1)} %bitcast.76), kind=kOutput, calls=%fused_computation.46 | convolution fusion | flops 84869136 | bytes 5939456 | tf_op jit(solution)/shard_map/sub | solution.py:11
  257.1 4.3 %convert_bitcast_fusion.1 = bf16[1,16,32,20,128]{4,1,3,2,0:T(8,128)(2,1)S(1)} fusion(bf16[16,32,20,128]{3,0,2,1:T(8,128)(2,1)} %bitcast.77, f32[32,20,16,16]{2,3,1,0:T(8,128)} %get-tuple-element.15, f32[32,20,16]{2,1,0:T(8,128)S(1)} %get-tuple-element.14), kind=kOutput, calls=%fused_computation.19 | convolution fusion | flops 43581440 | bytes 5939200 | tf_op jit(solution)/shard_map/cphst,ctphe->csphe/dot_general | solution.py:52
  261.5 3.5 copy.114
  264.9 4.6 %all-to-all-start.1 = ((bf16[1,16,32,20,128]{4,2,3,0,1:T(8,128)(2,1)}), bf16[1,16,32,20,128]{4,2,3,0,1:T(8,128)(2,1)}, u32[]{:S(2)}, u32[]{:S(2)}) async-start(bf16[1,16,32,20,128]{4,2,3,0,1:T(8,128)(2,1)} %copy.114), calls=%async_computation.1 | async-start | bytes 5242880 | tf_op jit(solution)/shard_map/all_to_all | solution.py:55
  269.5 3.2 copy.125
  272.7 4.4 %copy.126 = bf16[1,1,4,128,2560]{3,4,2,1,0:T(8,128)(2,1)} copy(bf16[1,1,4,128,2560]{4,3,2,1,0:T(8,128)(2,1)} %get-tuple-element.5) | data formatting | bytes 5242880
  277.2 4.4 %copy.101 = bf16[1,1,4,128,2560]{3,4,2,1,0:T(8,128)(2,1)} copy(bf16[1,1,4,128,2560]{4,3,2,1,0:T(8,128)(2,1)} %get-tuple-element.10) | data formatting | bytes 5242880 | tf_op jit(solution)/shard_map/slice | solution.py:67
  281.6 6.1 %fusion.36 = (f32[4,20,128]{2,1,0:T(8,128)S(1)}, f32[4,20,128,128]{2,3,1,0:T(8,128)}) fusion(bf16[4,128,20,128]{1,3,2,0:T(8,128)(2,1)S(1)} %bitcast.69, bf16[4,128,20,128]{1,3,2,0:T(8,128)(2,1)} %bitcast.70), kind=kOutput, calls=%fused_computation.47 | convolution fusion | flops 339476608 | bytes 10526720 | tf_op jit(solution)/shard_map/sub | solution.py:11
  287.7 41.6 %all-to-all-done.1 = bf16[1,16,32,20,128]{4,2,3,0,1:T(8,128)(2,1)} async-done(((bf16[1,16,32,20,128]{4,2,3,0,1:T(8,128)(2,1)}), bf16[1,16,32,20,128]{4,2,3,0,1:T(8,128)(2,1)}, u32[]{:S(2)}, u32[]{:S(2)}) %all-to-all-start.1) | async-done | bytes 2621472 | tf_op jit(solution)/shard_map/all_to_all | solution.py:55
  334.8 6.1 %copy.117 = f32[1,4,128,20,128]{2,4,3,1,0:T(8,128)} copy(f32[1,4,128,20,128]{4,2,3,1,0:T(8,128)} %bitcast.68) | data formatting | bytes 10485760 | tf_op jit(solution)/shard_map/convert_element_type | solution.py:69
  340.9 6.5 %fusion.3 = bf16[1,4,128,20,128]{2,4,3,1,0:T(8,128)(2,1)} fusion(f32[1,4,128,20,128]{2,4,3,1,0:T(8,128)} %copy.117, bf16[4,128,20,128]{1,3,2,0:T(8,128)(2,1)S(1)} %bitcast.74, f32[4,20,128,128]{2,3,1,0:T(8,128)} %get-tuple-element.17, f32[4,20,128]{2,1,0:T(8,128)S(1)} %get-tuple-element.16), kind=kOutput, calls=%fused_computation.7 | convolution fusion | flops 343408640 | bytes 15769600 | tf_op jit(solution)/shard_map/cfhpq,cfqhe->cfphe/dot_general | solution.py:66
  347.4 4.4 %copy.118 = bf16[1,4,128,2560]{3,2,1,0:T(8,128)(2,1)} copy(bf16[1,4,128,2560]{2,3,1,0:T(8,128)(2,1)} %bitcast.78) | data formatting | bytes 5242880 | tf_op jit(solution)/shard_map/reshape | solution.py:70
  (26 shorter events, 15.4 us)
Async XLA Ops:
  0.0 8.3 %copy-start = (f32[32,2560]{1,0:T(8,128)S(1)}, f32[32,2560]{1,0:T(8,128)}, u32[]{:S(2)}) copy-start(f32[32,2560]{1,0:T(8,128)} %param.8) | copy-start | bytes 983044
  32.2 1.7 copy-start.2
  32.2 2.5 copy-start.3
  52.4 5.7 %copy-start.5 = (s32[16]{0:T(128)S(1)}, s32[16]{0:T(128)}, u32[]{:S(2)}) copy-start(s32[16]{0:T(128)} %param.10) | copy-start | bytes 196
  52.4 5.8 %copy-start.6 = (s32[1,16]{1,0:T(1,128)S(1)}, s32[1,16]{1,0:T(1,128)}, u32[]{:S(2)}) copy-start(s32[1,16]{1,0:T(1,128)} %param.11) | copy-start | bytes 196
  52.4 178.8 %all-to-all-start = ((bf16[3,1,4,128,20,128]{5,2,4,1,0,3:T(4,128)(2,1)}), bf16[3,1,4,128,20,128]{5,2,4,1,0,3:T(4,128)(2,1)}, u32[]{:S(2)}, u32[]{:S(2)}) async-start(bf16[3,1,4,128,20,128]{5,2,4,1,0,3:T(4,128)(2,1)} %copy.108), calls=%async_computation | async-start | bytes 15728640 | tf_op jit(solution)/shard_map/all_to_all | solution.py:44
  264.9 64.3 %all-to-all-start.1 = ((bf16[1,16,32,20,128]{4,2,3,0,1:T(8,128)(2,1)}), bf16[1,16,32,20,128]{4,2,3,0,1:T(8,128)(2,1)}, u32[]{:S(2)}, u32[]{:S(2)}) async-start(bf16[1,16,32,20,128]{4,2,3,0,1:T(8,128)(2,1)} %copy.114), calls=%async_computation.1 | async-start | bytes 5242880 | tf_op jit(solution)/shard_map/all_to_all | solution.py:55
  334.8 6.1 %copy-start.4 = (bf16[1,1,4,128,2560]{3,4,2,1,0:T(8,128)(2,1)S(1)}, bf16[1,1,4,128,2560]{3,4,2,1,0:T(8,128)(2,1)}, u32[]{:S(2)}) copy-start(bf16[1,1,4,128,2560]{3,4,2,1,0:T(8,128)(2,1)} %copy.101) | copy-start | bytes 7864324
  347.4 4.4 %copy-start.1 = (f32[32,2560]{1,0:T(8,128)S(1)}, f32[32,2560]{1,0:T(8,128)}, u32[]{:S(2)}) copy-start(f32[32,2560]{1,0:T(8,128)} %param.8) | copy-start | bytes 983044
where the time goes:
time: 353 us; the launch traced here: 352 us
  waiting for transfers between devices  214 us (61%)
  local copies, waits for them, and re-layouts  85.8 us (24%)
  matrix products  26.6 us (8%)
  starting transfers between devices  10.3 us (3%)
  other arithmetic  8.06 us (2%)
  blocking collectives  6.53 us (2%)
    all_to_all x1, waiting for transfers between devices, local(): lax.all_to_all(temporal_in, 'frame', split_axis=3, concat_axis=2, tiled=T...  173 us
    all_to_all x1, waiting for transfers between devices, local(): lax.all_to_all(finished, 'frame', split_axis=1, concat_axis=2, tiled=True)  41.6 us
    unnamed x19, local copies, waits for them, and re-layouts  20.6 us
    sub x2, matrix products, masked_softmax(): weights = jnp.where(allowed, jnp.exp(spatial_scores - peak), 0.0)  14.5 us
    another operation x1, local copies, waits for them, and re-layouts, local(): temporal_in = jnp.stack([reshaped_rows[3], reshaped_rows[4], values_t])  14 us
    slice x1, local copies, waits for them, and re-layouts, local(): reshaped_rows[1]  11.6 us
    convert_element_type x2, local copies, waits for them, and re-layouts, local(): temporal.astype(jnp.float32)  9.09 us
  transfers between devices with their start and end apart: 2, of which 2 were waited for; matrix products, arithmetic and copies ran while one was open for 5% of the time, Pallas kernels for 0%

commit v1 on v0

v1 whole, which is shorter than its diff:
```python
import functools

import jax
import jax.numpy as jnp
from jax import lax
from jax.experimental import pallas as pl
from jax.experimental.pallas import tpu as pltpu
from jax.sharding import PartitionSpec as P

E = 128
GROUP = 16
CHUNKS = 5
HIGHEST = lax.Precision.HIGHEST
VMEM = 48 * 1024 * 1024


def params():
    return pltpu.CompilerParams(vmem_limit_bytes=VMEM)


def spatial_kernel(q_ref, k_ref, v_ref, o_ref):
    heads = q_ref.shape[-1] // E
    for h in range(heads):
        cols = slice(h * E, (h + 1) * E)
        q, k, v = q_ref[0, 0, 0, :, cols], k_ref[0, 0, 0, :, cols], v_ref[0, 0, 0, :, cols]
        s = lax.dot_general(q, k, (((1,), (1,)), ((), ())), preferred_element_type=jnp.float32)
        s = s * (1.0 / E**0.5)
        w = jnp.exp(s - jnp.max(s, axis=-1, keepdims=True))
        p = (w * (1.0 / jnp.sum(w, axis=-1, keepdims=True))).astype(jnp.bfloat16)
        o = jnp.dot(p, v, preferred_element_type=jnp.float32)
        o_ref[0, 0, :, cols] = o.astype(jnp.bfloat16)


def spatial_attention(projected, step):
    _, clips, frames, patches, width = projected.shape
    spec = lambda which: pl.BlockSpec(
        (1, 1, 1, patches, step), lambda c, f, j: (which, c, f, 0, j)
    )
    return pl.pallas_call(
        spatial_kernel,
        grid=(clips, frames, width // step),
        in_specs=[spec(0), spec(1), spec(2)],
        out_specs=pl.BlockSpec((1, 1, patches, step), lambda c, f, j: (c, f, 0, j)),
        out_shape=jax.ShapeDtypeStruct((clips, frames, patches, width), jnp.bfloat16),
        compiler_params=params(),
        cost_estimate=pl.CostEstimate(
            flops=4 * clips * frames * patches * patches * width,
            bytes_accessed=8 * clips * frames * patches * width,
            transcendentals=clips * frames * patches * patches * (width // E),
        ),
        name="spatial",
    )(projected, projected, projected)


def pack_kernel(n, me_ref, *refs):
    for x, y in zip(refs[: n - 1], refs[n - 1 :]):
        y[...] = x[...]


def pack(projected, me, n, shifts, chunk, cols):
    _, clips, frames, patches, _ = projected.shape
    rows = patches // n
    block = (1, 1, frames, rows, cols)

    def spec(d):
        return pl.BlockSpec(
            block, lambda a, c, me_ref: (a + 3, c, 0, lax.rem(me_ref[0] + d, n), chunk)
        )

    shape = (3, clips, frames, rows, cols)
    return pl.pallas_call(
        functools.partial(pack_kernel, n),
        grid_spec=pltpu.PrefetchScalarGridSpec(
            num_scalar_prefetch=1,
            grid=(3, clips),
            in_specs=[spec(d) for d in shifts],
            out_specs=[pl.BlockSpec(block, lambda a, c, me_ref: (a, c, 0, 0, 0)) for _ in shifts],
        ),
        out_shape=[jax.ShapeDtypeStruct(shape, jnp.bfloat16) for _ in shifts],
        compiler_params=params(),
        cost_estimate=pl.CostEstimate(
            flops=0,
            bytes_accessed=12 * (n - 1) * clips * frames * rows * cols,
            transcendentals=0,
        ),
        name="pack",
    )(me, *([projected] * (n - 1)))


def temporal_kernel(n, me_ref, bias_ref, action_ref, *refs):
    ins, outs = refs[:n], refs[n:]
    frames, _, cols = ins[0].shape[2:]
    slots = n * frames
    bias = bias_ref[0]
    for h in range(cols // E):
        cut = slice(h * E, (h + 1) * E)

        def slots_of(which):
            return jnp.concatenate([x[which, 0, :, :, cut] for x in ins], axis=0)

        q = slots_of(0).reshape(slots * GROUP, E)
        k = slots_of(1).reshape(slots * GROUP, E)
        action = action_ref[0, :, cut].reshape(slots, 1, E)
        v = (slots_of(2).astype(jnp.float32) + action).astype(jnp.bfloat16)
        v = v.reshape(slots * GROUP, E)
        s = lax.dot_general(q, k, (((1,), (1,)), ((), ())), preferred_element_type=jnp.float32)
        s = s * (1.0 / E**0.5) + bias
        w = jnp.exp(s - jnp.max(s, axis=-1, keepdims=True))
        p = (w * (1.0 / jnp.sum(w, axis=-1, keepdims=True))).astype(jnp.bfloat16)
        o = jnp.dot(p, v, preferred_element_type=jnp.float32).astype(jnp.bfloat16)
        o = o.reshape(n, frames, GROUP, E)
        for i in range(n):
            outs[i][0, :, :, cut] = o[i]


def temporal_attention(projected, arrived, bias, action, me, n, chunk, cols):
    _, clips, frames, patches, _ = projected.shape
    rows = patches // n
    groups = rows // GROUP
    slots = n * frames
    block = (3, 1, frames, GROUP, cols)
    own = pl.BlockSpec(block, lambda c, g, me_ref: (1, c, 0, me_ref[0] * groups + g, chunk))
    other = pl.BlockSpec(block, lambda c, g, me_ref: (0, c, 0, g, 0))
    return pl.pallas_call(
        functools.partial(temporal_kernel, n),
        grid_spec=pltpu.PrefetchScalarGridSpec(
            num_scalar_prefetch=1,
            grid=(clips, groups),
            in_specs=[
                pl.BlockSpec((1, slots * GROUP, slots * GROUP), lambda c, g, me_ref: (c, 0, 0)),
                pl.BlockSpec((1, slots, cols), lambda c, g, me_ref: (c, 0, chunk)),
                own,
            ]
            + [other] * (n - 1),
            out_specs=[
                pl.BlockSpec((1, frames, GROUP, cols), lambda c, g, me_ref: (c, 0, g, 0))
            ]
            * n,
        ),
        out_shape=[jax.ShapeDtypeStruct((clips, frames, rows, cols), jnp.bfloat16)] * n,
        compiler_params=params(),
        cost_estimate=pl.CostEstimate(
            flops=4 * clips * groups * (slots * GROUP) ** 2 * cols,
            bytes_accessed=8 * clips * slots * rows * cols,
            transcendentals=clips * groups * (slots * GROUP) ** 2 * (cols // E),
        ),
        name="temporal",
    )(me, bias, action, projected, *arrived)


def combine_kernel(n, me_ref, spatial_ref, *refs):
    parts, out_ref = refs[:n], refs[n]
    rows = parts[0].shape[2]
    for d in range(n):
        at = pl.ds(pl.multiple_of(lax.rem(me_ref[0] + d, n) * rows, rows), rows)
        total = spatial_ref[0, :, at, :].astype(jnp.float32) + parts[d][0].astype(jnp.float32)
        out_ref[0, :, at, :] = total.astype(jnp.bfloat16)


def combine(mixed, parts, me, n, chunk, cols):
    clips, frames, patches, width = mixed.shape
    rows = patches // n
    whole = pl.BlockSpec((1, frames, patches, cols), lambda c, me_ref: (c, 0, 0, chunk))
    part = pl.BlockSpec((1, frames, rows, cols), lambda c, me_ref: (c, 0, 0, 0))
    return pl.pallas_call(
        functools.partial(combine_kernel, n),
        grid_spec=pltpu.PrefetchScalarGridSpec(
            num_scalar_prefetch=1,
            grid=(clips,),
            in_specs=[whole] + [part] * n,
            out_specs=whole,
        ),
        out_shape=jax.ShapeDtypeStruct(mixed.shape, mixed.dtype),
        input_output_aliases={1: 0},
        compiler_params=params(),
        cost_estimate=pl.CostEstimate(
            flops=clips * frames * patches * cols,
            bytes_accessed=6 * clips * frames * patches * cols,
            transcendentals=0,
        ),
        name="combine",
    )(me, mixed, *parts)


def local(n, projected, codes, action_weight, clip_ids, frame_map, segments):
    _, clips, frames, patches, width = projected.shape
    slots = frame_map.shape[0]
    heads = width // E
    chunks = max(c for c in range(1, CHUNKS + 1) if heads % c == 0)
    cols = width // chunks
    me_scalar = lax.axis_index("frame")
    me = me_scalar.astype(jnp.int32)[None]
    far_first = sorted(range(1, n), key=lambda d: abs(d - n // 2))

    def send(x, d):
        return lax.ppermute(x, "frame", [(i, (i + d) % n) for i in range(n)])

    arrived = []
    for j in range(chunks):
        packed = pack(projected, me, n, far_first, j, cols)
        got = {d: send(x, d) for d, x in zip(far_first, packed)}
        arrived.append([got[d] for d in range(1, n)])

    source = lax.rem(me_scalar - jnp.arange(n) + n, n)
    order = (source[:, None] * frames + jnp.arange(frames)[None, :]).reshape(-1)
    time_of = jnp.sum(
        jnp.where(order[:, None] == jnp.arange(slots)[None, :], frame_map[None, :], 0), axis=-1
    )
    at_time = time_of[:, None] == jnp.arange(slots, dtype=jnp.int32)[None, :]
    seg_slot = jnp.sum(jnp.where(at_time[None], segments[:, None, :], 0), axis=-1)
    allowed = (time_of[None, :] <= time_of[:, None])[None] & (
        seg_slot[:, None, :] == seg_slot[:, :, None]
    )
    row = jnp.arange(slots * GROUP)
    same_patch = (row[:, None] % GROUP) == (row[None, :] % GROUP)
    wide = jnp.repeat(jnp.repeat(allowed, GROUP, axis=1), GROUP, axis=2)
    bias = jnp.where(wide & same_patch[None], 0.0, -1e30).astype(jnp.float32)

    all_codes = lax.all_gather(codes, "dp", axis=0, tiled=True)
    owned = lax.axis_index("dp") * clips + jnp.arange(clips, dtype=jnp.int32)
    select = (clip_ids[:, None] == owned[None, :]).astype(jnp.float32)
    by_clip = jnp.einsum("ic,ifa->cfa", select, all_codes, precision=HIGHEST)
    codes_slot = jnp.einsum(
        "st,cta->csa", at_time.astype(jnp.float32), by_clip, precision=HIGHEST
    )
    action = jnp.einsum("csa,ad->csd", codes_slot, action_weight, precision=HIGHEST)

    mixed = spatial_attention(projected, cols)
    for j in range(chunks):
        done = temporal_attention(projected, arrived[j], bias, action, me, n, j, cols)
        back = {d: send(done[d], -d) for d in far_first}
        mixed = combine(mixed, [done[0]] + [back[d] for d in range(1, n)], me, n, j, cols)
    return mixed


def solution(mesh):
    return jax.shard_map(
        functools.partial(local, mesh.shape["frame"]),
        mesh=mesh,
        in_specs=(
            P(None, "dp", "frame", None, "mp"),
            P("dp", None, None),
            P(None, "mp"),
            P(),
            P(),
            P("dp", None),
        ),
        out_specs=P("dp", "frame", None, "mp"),
        check_vma=False,
    )
```

time: 353 us -> 266 us (0.75)
  waiting for transfers between devices: 214 us -> 76.3 us
  starting transfers between devices: 10.3 us -> 105 us
  local copies, waits for them, and re-layouts: 85.8 us -> 7.22 us
  Pallas kernels: 0 us -> 70.4 us
  matrix products: 26.6 us -> 0.64 us
  other arithmetic: 8.06 us -> 0.64 us
    all_to_all x2 -> x0, waiting for transfers between devices: 214 us -> none  [the longest x1 173 us: local(): lax.all_to_all(temporal_in, 'frame', split_axis=3, concat_axis=2, tiled=T...]
    ppermute x0 -> x30, starting transfers between devices: none -> 105 us  [send(): return lax.ppermute(x, 'frame', [(i, (i + d) % n) for i in range(n)])]
    ppermute x0 -> x30, waiting for transfers between devices: none -> 76.3 us  [send(): return lax.ppermute(x, 'frame', [(i, (i + d) % n) for i in range(n)])]
    pallas_call x0 -> x16, Pallas kernels: none -> 70.4 us  [the longest x1 30.3 us: spatial_attention(): pl.pallas_call(spatial_kernel, grid=(clips, frames, width // step), in_sp...]
    slice x6 -> x0, local copies, waits for them, and re-layouts: 28.1 us -> none  [the longest x1 11.6 us: local(): reshaped_rows[1]]
    unnamed x19 -> x24, local copies, waits for them, and re-layouts: 20.6 us -> 5.26 us
    sub x2 -> x0, matrix products: 14.5 us -> none  [masked_softmax(): weights = jnp.where(allowed, jnp.exp(spatial_scores - peak), 0.0)]
    another operation x1 -> x0, local copies, waits for them, and re-layouts: 14 us -> none  [local(): temporal_in = jnp.stack([reshaped_rows[3], reshaped_rows[4], values_t])]
  transfers between devices with their start and end apart: 2 -> 30, of which waited for: 2 -> 6; matrix products, arithmetic and copies ran while one was open for 5% -> 1% of each run, Pallas kernels for 0% -> 25%
where the time goes in v1:
time: 266 us; the launch traced here: 265 us
  starting transfers between devices  105 us (39%)
  waiting for transfers between devices  76.3 us (29%)
  Pallas kernels  70.4 us (26%)
  local copies, waits for them, and re-layouts  7.22 us (3%)
  blocking collectives  5.18 us (2%)
    ppermute x30, starting transfers between devices, send(): return lax.ppermute(x, 'frame', [(i, (i + d) % n) for i in range(n)])  105 us
    ppermute x30, waiting for transfers between devices, send(): return lax.ppermute(x, 'frame', [(i, (i + d) % n) for i in range(n)])  76.3 us
    pallas_call x1, Pallas kernels, spatial_attention(): pl.pallas_call(spatial_kernel, grid=(clips, frames, width // step), in_sp...  30.3 us
    pallas_call x5, Pallas kernels, temporal_attention(): pl.pallas_call(functools.partial(temporal_kernel, n), grid_spec=pltpu.Pre...  16.8 us
    pallas_call x5, Pallas kernels, pack(): pl.pallas_call(functools.partial(pack_kernel, n), grid_spec=pltpu.Prefetc...  13.5 us
    pallas_call x5, Pallas kernels, combine(): pl.pallas_call(functools.partial(combine_kernel, n), grid_spec=pltpu.Pref...  9.78 us
  transfers between devices with their start and end apart: 30, of which 6 were waited for; matrix products, arithmetic and copies ran while one was open for 1% of the time, Pallas kernels for 25%

profile of v1, /device:TPU:0, one launch (start us, length us, event | category | flops | bytes accessed | tf_op | source)
XLA Modules:
  0.0 265.2 jit_solution(17611454017912073146)
XLA Ops:
  22.7 5.2 %all_gather.3 = f32[4,16,32]{2,1,0:T(8,128)S(1)} all-gather(f32[1,16,32]{2,1,0:T(8,128)S(1)} %copy-done.8), channel_id=1, replica_groups=mesh['dp'=4,'frame'=4,'mp'=2] {'dp'}, dimensions={0}, use_global_device_ids=true | all-gather | bytes 10240 | tf_op jit(solution)/shard_map/all_gather | solution.py:219
  31.1 19.4 %collective-permute-done.1.refs_2_ = bf16[3,1,4,32,512]{4,3,2,1,0:T(8,128)(2,1)S(1)} collective-permute-done((bf16[3,1,4,32,512]{4,3,2,1,0:T(8,128)(2,1)S(1)}, bf16[3,1,4,32,512]{4,3,2,1,0:T(8,128)(2,1)S(1)}, u32[]{:S(2)}, u32[]{:S(2)}) %collective-permute-start.1) | collective-permute-done | bytes 393248 | tf_op jit(solution)/shard_map/ppermute | solution.py:196
  50.5 8.5 %collective-permute-start.12 = (bf16[3,1,4,32,512]{4,3,2,1,0:T(8,128)(2,1)}, bf16[3,1,4,32,512]{4,3,2,1,0:T(8,128)(2,1)S(1)}, u32[]{:S(2)}, u32[]{:S(2)}) collective-permute-start(bf16[3,1,4,32,512]{4,3,2,1,0:T(8,128)(2,1)} %get-tuple-element.54), channel_id=1, source_target_pairs={{0,2},{2,4},{4,6},{6,0},{1,3},{3,5},{5,7},{7,1},{8,10},{10,12},{12... | collective-permute-start | bytes 1179656 | tf_op jit(solution)/shard_map/ppermute | solution.py:196
  59.0 3.9 %collective-permute-start.13 = (bf16[3,1,4,32,512]{4,3,2,1,0:T(8,128)(2,1)}, bf16[3,1,4,32,512]{4,3,2,1,0:T(8,128)(2,1)S(1)}, u32[]{:S(2)}, u32[]{:S(2)}) collective-permute-start(bf16[3,1,4,32,512]{4,3,2,1,0:T(8,128)(2,1)} %get-tuple-element.55), channel_id=1, source_target_pairs={{0,4},{2,6},{4,0},{6,2},{1,5},{3,7},{5,1},{7,3},{8,12},{10,14},{12... | collective-permute-start | bytes 1179656 | tf_op jit(solution)/shard_map/ppermute | solution.py:196
  63.4 21.5 %collective-permute-done.7.refs_2_ = bf16[3,1,4,32,512]{4,3,2,1,0:T(8,128)(2,1)S(1)} collective-permute-done((bf16[3,1,4,32,512]{4,3,2,1,0:T(8,128)(2,1)}, bf16[3,1,4,32,512]{4,3,2,1,0:T(8,128)(2,1)S(1)}, u32[]{:S(2)}, u32[]{:S(2)}) %collective-permute-start.7) | collective-permute-done | bytes 393248 | tf_op jit(solution)/shard_map/ppermute | solution.py:196
  84.9 8.4 %collective-permute-start.18 = (bf16[3,1,4,32,512]{4,3,2,1,0:T(8,128)(2,1)}, bf16[3,1,4,32,512]{4,3,2,1,0:T(8,128)(2,1)}, u32[]{:S(2)}, u32[]{:S(2)}) collective-permute-start(bf16[3,1,4,32,512]{4,3,2,1,0:T(8,128)(2,1)} %copy-done.4), channel_id=1, source_target_pairs={{0,2},{2,4},{4,6},{6,0},{1,3},{3,5},{5,7},{7,1},{8,10},{10,12},{12... | collective-permute-start | bytes 1179656 | tf_op jit(solution)/shard_map/ppermute | solution.py:196
  100.2 3.3 %collective-permute-start.19 = (bf16[3,1,4,32,512]{4,3,2,1,0:T(8,128)(2,1)}, bf16[3,1,4,32,512]{4,3,2,1,0:T(8,128)(2,1)S(1)}, u32[]{:S(2)}, u32[]{:S(2)}) collective-permute-start(bf16[3,1,4,32,512]{4,3,2,1,0:T(8,128)(2,1)} %copy-done.2), channel_id=1, source_target_pairs={{0,4},{2,6},{4,0},{6,2},{1,5},{3,7},{5,1},{7,3},{8,12},{10,14},{12... | collective-permute-start | bytes 1179656 | tf_op jit(solution)/shard_map/ppermute | solution.py:196
  103.6 15.1 %collective-permute-done.13.refs_2_ = bf16[3,1,4,32,512]{4,3,2,1,0:T(8,128)(2,1)S(1)} collective-permute-done((bf16[3,1,4,32,512]{4,3,2,1,0:T(8,128)(2,1)}, bf16[3,1,4,32,512]{4,3,2,1,0:T(8,128)(2,1)S(1)}, u32[]{:S(2)}, u32[]{:S(2)}) %collective-permute-start.13) | collective-permute-done | bytes 393248 | tf_op jit(solution)/shard_map/ppermute | solution.py:196
  118.7 8.4 %collective-permute-start.24 = (bf16[3,1,4,32,512]{4,3,2,1,0:T(8,128)(2,1)}, bf16[3,1,4,32,512]{4,3,2,1,0:T(8,128)(2,1)S(1)}, u32[]{:S(2)}, u32[]{:S(2)}) collective-permute-start(bf16[3,1,4,32,512]{4,3,2,1,0:T(8,128)(2,1)} %copy-done.7), channel_id=1, source_target_pairs={{0,2},{2,4},{4,6},{6,0},{1,3},{3,5},{5,7},{7,1},{8,10},{10,12},{12... | collective-permute-start | bytes 1179656 | tf_op jit(solution)/shard_map/ppermute | solution.py:196
  127.1 3.3 %collective-permute-start.25 = (bf16[3,1,4,32,512]{4,3,2,1,0:T(8,128)(2,1)}, bf16[3,1,4,32,512]{4,3,2,1,0:T(8,128)(2,1)S(1)}, u32[]{:S(2)}, u32[]{:S(2)}) collective-permute-start(bf16[3,1,4,32,512]{4,3,2,1,0:T(8,128)(2,1)} %copy-done.6), channel_id=1, source_target_pairs={{0,4},{2,6},{4,0},{6,2},{1,5},{3,7},{5,1},{7,3},{8,12},{10,14},{12... | collective-permute-start | bytes 1179656 | tf_op jit(solution)/shard_map/ppermute | solution.py:196
  130.5 3.3 %temporal.5 = (bf16[1,4,32,512]{3,2,1,0:T(8,128)(2,1)S(1)}, bf16[1,4,32,512]{3,2,1,0:T(8,128)(2,1)S(1)}, bf16[1,4,32,512]{3,2,1,0:T(8,128)(2,1)S(1)}, bf16[1,4,32,512]{3,2,1,0:T(8,128)(2,1)S(1)}) custom-call(s32[1]{0:T(128)} %bitcast.me_ref, f32[1,256,256]{2,1,0:T(8,128)S(1)} %and_select_fusion.bias_ref, ...), custom_call_target="tpu_custom_call" | custom-call | flops 268435456 | bytes 2097152 | tf_op jit(solution)/shard_map/temporal/pallas_call | solution.py:124
  133.8 3.4 %temporal.6 = (bf16[1,4,32,512]{3,2,1,0:T(8,128)(2,1)S(1)}, bf16[1,4,32,512]{3,2,1,0:T(8,128)(2,1)S(1)}, bf16[1,4,32,512]{3,2,1,0:T(8,128)(2,1)S(1)}, bf16[1,4,32,512]{3,2,1,0:T(8,128)(2,1)S(1)}) custom-call(s32[1]{0:T(128)} %bitcast.me_ref, f32[1,256,256]{2,1,0:T(8,128)S(1)} %and_select_fusion.bias_ref, ...), custom_call_target="tpu_custom_call" | custom-call | flops 268435456 | bytes 2097152 | tf_op jit(solution)/shard_map/temporal/pallas_call | solution.py:124
  137.3 15.2 %collective-permute-done.19.refs_2_ = bf16[3,1,4,32,512]{4,3,2,1,0:T(8,128)(2,1)S(1)} collective-permute-done((bf16[3,1,4,32,512]{4,3,2,1,0:T(8,128)(2,1)}, bf16[3,1,4,32,512]{4,3,2,1,0:T(8,128)(2,1)S(1)}, u32[]{:S(2)}, u32[]{:S(2)}) %collective-permute-start.19) | collective-permute-done | bytes 393248 | tf_op jit(solution)/shard_map/ppermute | solution.py:196
  152.4 11.0 %collective-permute-start.3 = (bf16[1,4,32,512]{3,2,1,0:T(8,128)(2,1)S(1)}, bf16[1,4,32,512]{3,2,1,0:T(8,128)(2,1)S(1)}, u32[]{:S(2)}, u32[]{:S(2)}) collective-permute-start(bf16[1,4,32,512]{3,2,1,0:T(8,128)(2,1)S(1)} %get-tuple-element.44), channel_id=1, source_target_pairs={{0,6},{2,0},{4,2},{6,4},{1,7},{3,1},{5,3},{7,5},{8,14},{10,8},{12,... | collective-permute-start | bytes 393224 | tf_op jit(solution)/shard_map/ppermute | solution.py:196
  163.5 11.3 %collective-permute-start.5 = (bf16[1,4,32,512]{3,2,1,0:T(8,128)(2,1)S(1)}, bf16[1,4,32,512]{3,2,1,0:T(8,128)(2,1)S(1)}, u32[]{:S(2)}, u32[]{:S(2)}) collective-permute-start(bf16[1,4,32,512]{3,2,1,0:T(8,128)(2,1)S(1)} %get-tuple-element.46), channel_id=1, source_target_pairs={{0,2},{2,4},{4,6},{6,0},{1,3},{3,5},{5,7},{7,1},{8,10},{10,12},{12... | collective-permute-start | bytes 393224 | tf_op jit(solution)/shard_map/ppermute | solution.py:196
  176.6 12.7 %collective-permute-start.11 = (bf16[1,4,32,512]{3,2,1,0:T(8,128)(2,1)S(1)}, bf16[1,4,32,512]{3,2,1,0:T(8,128)(2,1)S(1)}, u32[]{:S(2)}, u32[]{:S(2)}) collective-permute-start(bf16[1,4,32,512]{3,2,1,0:T(8,128)(2,1)S(1)} %get-tuple-element.53), channel_id=1, source_target_pairs={{0,2},{2,4},{4,6},{6,0},{1,3},{3,5},{5,7},{7,1},{8,10},{10,12},{12... | collective-permute-start | bytes 393224 | tf_op jit(solution)/shard_map/ppermute | solution.py:196
  189.4 3.3 %temporal.7 = (bf16[1,4,32,512]{3,2,1,0:T(8,128)(2,1)S(1)}, bf16[1,4,32,512]{3,2,1,0:T(8,128)(2,1)S(1)}, bf16[1,4,32,512]{3,2,1,0:T(8,128)(2,1)S(1)}, bf16[1,4,32,512]{3,2,1,0:T(8,128)(2,1)S(1)}) custom-call(s32[1]{0:T(128)} %bitcast.me_ref, f32[1,256,256]{2,1,0:T(8,128)S(1)} %and_select_fusion.bias_ref, ...), custom_call_target="tpu_custom_call" | custom-call | flops 268435456 | bytes 2097152 | tf_op jit(solution)/shard_map/temporal/pallas_call | solution.py:124
  192.7 3.4 %temporal.8 = (bf16[1,4,32,512]{3,2,1,0:T(8,128)(2,1)S(1)}, bf16[1,4,32,512]{3,2,1,0:T(8,128)(2,1)S(1)}, bf16[1,4,32,512]{3,2,1,0:T(8,128)(2,1)S(1)}, bf16[1,4,32,512]{3,2,1,0:T(8,128)(2,1)S(1)}) custom-call(s32[1]{0:T(128)} %bitcast.me_ref, f32[1,256,256]{2,1,0:T(8,128)S(1)} %and_select_fusion.bias_ref, ...), custom_call_target="tpu_custom_call" | custom-call | flops 268435456 | bytes 2097152 | tf_op jit(solution)/shard_map/temporal/pallas_call | solution.py:124
  199.7 3.8 %collective-permute-start.21 = (bf16[1,4,32,512]{3,2,1,0:T(8,128)(2,1)S(1)}, bf16[1,4,32,512]{3,2,1,0:T(8,128)(2,1)S(1)}, u32[]{:S(2)}, u32[]{:S(2)}) collective-permute-start(bf16[1,4,32,512]{3,2,1,0:T(8,128)(2,1)S(1)} %get-tuple-element.65), channel_id=1, source_target_pairs={{0,6},{2,0},{4,2},{6,4},{1,7},{3,1},{5,3},{7,5},{8,14},{10,8},{12,... | collective-permute-start | bytes 393224 | tf_op jit(solution)/shard_map/ppermute | solution.py:196
  203.5 3.3 %temporal.9 = (bf16[1,4,32,512]{3,2,1,0:T(8,128)(2,1)S(1)}, bf16[1,4,32,512]{3,2,1,0:T(8,128)(2,1)S(1)}, bf16[1,4,32,512]{3,2,1,0:T(8,128)(2,1)S(1)}, bf16[1,4,32,512]{3,2,1,0:T(8,128)(2,1)S(1)}) custom-call(s32[1]{0:T(128)} %bitcast.me_ref, f32[1,256,256]{2,1,0:T(8,128)S(1)} %and_select_fusion.bias_ref, ...), custom_call_target="tpu_custom_call" | custom-call | flops 268435456 | bytes 2097152 | tf_op jit(solution)/shard_map/temporal/pallas_call | solution.py:124
  208.3 5.7 %collective-permute-start.23 = (bf16[1,4,32,512]{3,2,1,0:T(8,128)(2,1)S(1)}, bf16[1,4,32,512]{3,2,1,0:T(8,128)(2,1)S(1)}, u32[]{:S(2)}, u32[]{:S(2)}) collective-permute-start(bf16[1,4,32,512]{3,2,1,0:T(8,128)(2,1)S(1)} %get-tuple-element.67), channel_id=1, source_target_pairs={{0,2},{2,4},{4,6},{6,0},{1,3},{3,5},{5,7},{7,1},{8,10},{10,12},{12... | collective-permute-start | bytes 393224 | tf_op jit(solution)/shard_map/ppermute | solution.py:196
  214.0 4.9 %collective-permute-done.16.refs_2_ = bf16[1,4,32,512]{3,2,1,0:T(8,128)(2,1)S(1)} collective-permute-done((bf16[1,4,32,512]{3,2,1,0:T(8,128)(2,1)S(1)}, bf16[1,4,32,512]{3,2,1,0:T(8,128)(2,1)S(1)}, u32[]{:S(2)}, u32[]{:S(2)}) %collective-permute-start.16) | collective-permute-done | bytes 131104 | tf_op jit(solution)/shard_map/ppermute | solution.py:196
  219.7 5.4 %collective-permute-start.29 = (bf16[1,4,32,512]{3,2,1,0:T(8,128)(2,1)S(1)}, bf16[1,4,32,512]{3,2,1,0:T(8,128)(2,1)S(1)}, u32[]{:S(2)}, u32[]{:S(2)}) collective-permute-start(bf16[1,4,32,512]{3,2,1,0:T(8,128)(2,1)S(1)} %get-tuple-element.74), channel_id=1, source_target_pairs={{0,2},{2,4},{4,6},{6,0},{1,3},{3,5},{5,7},{7,1},{8,10},{10,12},{12... | collective-permute-start | bytes 393224 | tf_op jit(solution)/shard_map/ppermute | solution.py:196
  225.1 30.3 %spatial.1.spatial_ref = bf16[1,4,128,2560]{3,2,1,0:T(8,128)(2,1)} custom-call(bf16[6,1,4,128,2560]{4,3,2,1,0:T(8,128)(2,1)} %refs_0_.19, bf16[6,1,4,128,2560]{4,3,2,1,0:T(8,128)(2,1)} %refs_0_.19, bf16[6,1,4,128,2560]{4,3,2,1,0:T(8,128)(2,1)} %refs_0_.19), custom_call_target="tpu_custom_call" | custom-call | flops 671088640 | bytes 10485760 | tf_op jit(solution)/shard_map/spatial/pallas_call | solution.py:39
  (92 shorter events, 50.8 us)
Async XLA Ops:
  3.0 25.3 %collective-permute-start = (bf16[3,1,4,32,512]{4,3,2,1,0:T(8,128)(2,1)}, bf16[3,1,4,32,512]{4,3,2,1,0:T(8,128)(2,1)S(1)}, u32[]{:S(2)}, u32[]{:S(2)}) collective-permute-start(bf16[3,1,4,32,512]{4,3,2,1,0:T(8,128)(2,1)} %get-tuple-element.40), channel_id=1, source_target_pairs={{0,2},{2,4},{4,6},{6,0},{1,3},{3,5},{5,7},{7,1},{8,10},{10,12},{12... | collective-permute-start | bytes 1179656 | tf_op jit(solution)/shard_map/ppermute | solution.py:196
  6.0 44.5 %collective-permute-start.1 = (bf16[3,1,4,32,512]{4,3,2,1,0:T(8,128)(2,1)S(1)}, bf16[3,1,4,32,512]{4,3,2,1,0:T(8,128)(2,1)S(1)}, u32[]{:S(2)}, u32[]{:S(2)}) collective-permute-start(bf16[3,1,4,32,512]{4,3,2,1,0:T(8,128)(2,1)S(1)} %get-tuple-element.41), channel_id=1, source_target_pairs={{0,4},{2,6},{4,0},{6,2},{1,5},{3,7},{5,1},{7,3},{8,12},{10,14},{12... | collective-permute-start | bytes 1179656 | tf_op jit(solution)/shard_map/ppermute | solution.py:196
  8.6 50.4 %collective-permute-start.2 = (bf16[3,1,4,32,512]{4,3,2,1,0:T(8,128)(2,1)S(1)}, bf16[3,1,4,32,512]{4,3,2,1,0:T(8,128)(2,1)S(1)}, u32[]{:S(2)}, u32[]{:S(2)}) collective-permute-start(bf16[3,1,4,32,512]{4,3,2,1,0:T(8,128)(2,1)S(1)} %get-tuple-element.42), channel_id=1, source_target_pairs={{0,6},{2,0},{4,2},{6,4},{1,7},{3,1},{5,3},{7,5},{8,14},{10,8},{12,... | collective-permute-start | bytes 1179656 | tf_op jit(solution)/shard_map/ppermute | solution.py:196
  13.0 49.9 %collective-permute-start.6 = (bf16[3,1,4,32,512]{4,3,2,1,0:T(8,128)(2,1)S(1)}, bf16[3,1,4,32,512]{4,3,2,1,0:T(8,128)(2,1)S(1)}, u32[]{:S(2)}, u32[]{:S(2)}) collective-permute-start(bf16[3,1,4,32,512]{4,3,2,1,0:T(8,128)(2,1)S(1)} %get-tuple-element.47), channel_id=1, source_target_pairs={{0,2},{2,4},{4,6},{6,0},{1,3},{3,5},{5,7},{7,1},{8,10},{10,12},{12... | collective-permute-start | bytes 1179656 | tf_op jit(solution)/shard_map/ppermute | solution.py:196
  13.7 71.3 %collective-permute-start.7 = (bf16[3,1,4,32,512]{4,3,2,1,0:T(8,128)(2,1)}, bf16[3,1,4,32,512]{4,3,2,1,0:T(8,128)(2,1)S(1)}, u32[]{:S(2)}, u32[]{:S(2)}) collective-permute-start(bf16[3,1,4,32,512]{4,3,2,1,0:T(8,128)(2,1)} %get-tuple-element.48), channel_id=1, source_target_pairs={{0,4},{2,6},{4,0},{6,2},{1,5},{3,7},{5,1},{7,3},{8,12},{10,14},{12... | collective-permute-start | bytes 1179656 | tf_op jit(solution)/shard_map/ppermute | solution.py:196
  28.3 72.0 %collective-permute-start.8 = (bf16[3,1,4,32,512]{4,3,2,1,0:T(8,128)(2,1)}, bf16[3,1,4,32,512]{4,3,2,1,0:T(8,128)(2,1)}, u32[]{:S(2)}, u32[]{:S(2)}) collective-permute-start(bf16[3,1,4,32,512]{4,3,2,1,0:T(8,128)(2,1)} %get-tuple-element.49), channel_id=1, source_target_pairs={{0,6},{2,0},{4,2},{6,4},{1,7},{3,1},{5,3},{7,5},{8,14},{10,8},{12,... | collective-permute-start | bytes 1179656 | tf_op jit(solution)/shard_map/ppermute | solution.py:196
  50.5 53.1 %collective-permute-start.12 = (bf16[3,1,4,32,512]{4,3,2,1,0:T(8,128)(2,1)}, bf16[3,1,4,32,512]{4,3,2,1,0:T(8,128)(2,1)S(1)}, u32[]{:S(2)}, u32[]{:S(2)}) collective-permute-start(bf16[3,1,4,32,512]{4,3,2,1,0:T(8,128)(2,1)} %get-tuple-element.54), channel_id=1, source_target_pairs={{0,2},{2,4},{4,6},{6,0},{1,3},{3,5},{5,7},{7,1},{8,10},{10,12},{12... | collective-permute-start | bytes 1179656 | tf_op jit(solution)/shard_map/ppermute | solution.py:196
  59.0 59.7 %collective-permute-start.13 = (bf16[3,1,4,32,512]{4,3,2,1,0:T(8,128)(2,1)}, bf16[3,1,4,32,512]{4,3,2,1,0:T(8,128)(2,1)S(1)}, u32[]{:S(2)}, u32[]{:S(2)}) collective-permute-start(bf16[3,1,4,32,512]{4,3,2,1,0:T(8,128)(2,1)} %get-tuple-element.55), channel_id=1, source_target_pairs={{0,4},{2,6},{4,0},{6,2},{1,5},{3,7},{5,1},{7,3},{8,12},{10,14},{12... | collective-permute-start | bytes 1179656 | tf_op jit(solution)/shard_map/ppermute | solution.py:196
  62.9 64.2 %collective-permute-start.14 = (bf16[3,1,4,32,512]{4,3,2,1,0:T(8,128)(2,1)}, bf16[3,1,4,32,512]{4,3,2,1,0:T(8,128)(2,1)S(1)}, u32[]{:S(2)}, u32[]{:S(2)}) collective-permute-start(bf16[3,1,4,32,512]{4,3,2,1,0:T(8,128)(2,1)} %copy-done.5), channel_id=1, source_target_pairs={{0,6},{2,0},{4,2},{6,4},{1,7},{3,1},{5,3},{7,5},{8,14},{10,8},{12,... | collective-permute-start | bytes 1179656 | tf_op jit(solution)/shard_map/ppermute | solution.py:196
  84.9 45.4 %collective-permute-start.18 = (bf16[3,1,4,32,512]{4,3,2,1,0:T(8,128)(2,1)}, bf16[3,1,4,32,512]{4,3,2,1,0:T(8,128)(2,1)}, u32[]{:S(2)}, u32[]{:S(2)}) collective-permute-start(bf16[3,1,4,32,512]{4,3,2,1,0:T(8,128)(2,1)} %copy-done.4), channel_id=1, source_target_pairs={{0,2},{2,4},{4,6},{6,0},{1,3},{3,5},{5,7},{7,1},{8,10},{10,12},{12... | collective-permute-start | bytes 1179656 | tf_op jit(solution)/shard_map/ppermute | solution.py:196
  100.2 52.2 %collective-permute-start.19 = (bf16[3,1,4,32,512]{4,3,2,1,0:T(8,128)(2,1)}, bf16[3,1,4,32,512]{4,3,2,1,0:T(8,128)(2,1)S(1)}, u32[]{:S(2)}, u32[]{:S(2)}) collective-permute-start(bf16[3,1,4,32,512]{4,3,2,1,0:T(8,128)(2,1)} %copy-done.2), channel_id=1, source_target_pairs={{0,4},{2,6},{4,0},{6,2},{1,5},{3,7},{5,1},{7,3},{8,12},{10,14},{12... | collective-permute-start | bytes 1179656 | tf_op jit(solution)/shard_map/ppermute | solution.py:196
  103.6 59.9 %collective-permute-start.20 = (bf16[3,1,4,32,512]{4,3,2,1,0:T(8,128)(2,1)}, bf16[3,1,4,32,512]{4,3,2,1,0:T(8,128)(2,1)S(1)}, u32[]{:S(2)}, u32[]{:S(2)}) collective-permute-start(bf16[3,1,4,32,512]{4,3,2,1,0:T(8,128)(2,1)} %copy-done.1), channel_id=1, source_target_pairs={{0,6},{2,0},{4,2},{6,4},{1,7},{3,1},{5,3},{7,5},{8,14},{10,8},{12,... | collective-permute-start | bytes 1179656 | tf_op jit(solution)/shard_map/ppermute | solution.py:196
  118.7 44.8 %collective-permute-start.24 = (bf16[3,1,4,32,512]{4,3,2,1,0:T(8,128)(2,1)}, bf16[3,1,4,32,512]{4,3,2,1,0:T(8,128)(2,1)S(1)}, u32[]{:S(2)}, u32[]{:S(2)}) collective-permute-start(bf16[3,1,4,32,512]{4,3,2,1,0:T(8,128)(2,1)} %copy-done.7), channel_id=1, source_target_pairs={{0,2},{2,4},{4,6},{6,0},{1,3},{3,5},{5,7},{7,1},{8,10},{10,12},{12... | collective-permute-start | bytes 1179656 | tf_op jit(solution)/shard_map/ppermute | solution.py:196
  127.1 47.9 %collective-permute-start.25 = (bf16[3,1,4,32,512]{4,3,2,1,0:T(8,128)(2,1)}, bf16[3,1,4,32,512]{4,3,2,1,0:T(8,128)(2,1)S(1)}, u32[]{:S(2)}, u32[]{:S(2)}) collective-permute-start(bf16[3,1,4,32,512]{4,3,2,1,0:T(8,128)(2,1)} %copy-done.6), channel_id=1, source_target_pairs={{0,4},{2,6},{4,0},{6,2},{1,5},{3,7},{5,1},{7,3},{8,12},{10,14},{12... | collective-permute-start | bytes 1179656 | tf_op jit(solution)/shard_map/ppermute | solution.py:196
  130.3 46.3 %collective-permute-start.26 = (bf16[3,1,4,32,512]{4,3,2,1,0:T(8,128)(2,1)}, bf16[3,1,4,32,512]{4,3,2,1,0:T(8,128)(2,1)S(1)}, u32[]{:S(2)}, u32[]{:S(2)}) collective-permute-start(bf16[3,1,4,32,512]{4,3,2,1,0:T(8,128)(2,1)} %copy-done.3), channel_id=1, source_target_pairs={{0,6},{2,0},{4,2},{6,4},{1,7},{3,1},{5,3},{7,5},{8,14},{10,8},{12,... | collective-permute-start | bytes 1179656 | tf_op jit(solution)/shard_map/ppermute | solution.py:196
  152.4 43.7 %collective-permute-start.3 = (bf16[1,4,32,512]{3,2,1,0:T(8,128)(2,1)S(1)}, bf16[1,4,32,512]{3,2,1,0:T(8,128)(2,1)S(1)}, u32[]{:S(2)}, u32[]{:S(2)}) collective-permute-start(bf16[1,4,32,512]{3,2,1,0:T(8,128)(2,1)S(1)} %get-tuple-element.44), channel_id=1, source_target_pairs={{0,6},{2,0},{4,2},{6,4},{1,7},{3,1},{5,3},{7,5},{8,14},{10,8},{12,... | collective-permute-start | bytes 393224 | tf_op jit(solution)/shard_map/ppermute | solution.py:196
  163.5 32.7 %collective-permute-start.4 = (bf16[1,4,32,512]{3,2,1,0:T(8,128)(2,1)S(1)}, bf16[1,4,32,512]{3,2,1,0:T(8,128)(2,1)S(1)}, u32[]{:S(2)}, u32[]{:S(2)}) collective-permute-start(bf16[1,4,32,512]{3,2,1,0:T(8,128)(2,1)S(1)} %get-tuple-element.45), channel_id=1, source_target_pairs={{0,4},{2,6},{4,0},{6,2},{1,5},{3,7},{5,1},{7,3},{8,12},{10,14},{12... | collective-permute-start | bytes 393224 | tf_op jit(solution)/shard_map/ppermute | solution.py:196
  163.5 34.2 %collective-permute-start.5 = (bf16[1,4,32,512]{3,2,1,0:T(8,128)(2,1)S(1)}, bf16[1,4,32,512]{3,2,1,0:T(8,128)(2,1)S(1)}, u32[]{:S(2)}, u32[]{:S(2)}) collective-permute-start(bf16[1,4,32,512]{3,2,1,0:T(8,128)(2,1)S(1)} %get-tuple-element.46), channel_id=1, source_target_pairs={{0,2},{2,4},{4,6},{6,0},{1,3},{3,5},{5,7},{7,1},{8,10},{10,12},{12... | collective-permute-start | bytes 393224 | tf_op jit(solution)/shard_map/ppermute | solution.py:196
  175.0 24.7 %collective-permute-start.10 = (bf16[1,4,32,512]{3,2,1,0:T(8,128)(2,1)S(1)}, bf16[1,4,32,512]{3,2,1,0:T(8,128)(2,1)S(1)}, u32[]{:S(2)}, u32[]{:S(2)}) collective-permute-start(bf16[1,4,32,512]{3,2,1,0:T(8,128)(2,1)S(1)} %get-tuple-element.52), channel_id=1, source_target_pairs={{0,4},{2,6},{4,0},{6,2},{1,5},{3,7},{5,1},{7,3},{8,12},{10,14},{12... | collective-permute-start | bytes 393224 | tf_op jit(solution)/shard_map/ppermute | solution.py:196
  206.8 54.4 %collective-permute-start.22 = (bf16[1,4,32,512]{3,2,1,0:T(8,128)(2,1)S(1)}, bf16[1,4,32,512]{3,2,1,0:T(8,128)(2,1)S(1)}, u32[]{:S(2)}, u32[]{:S(2)}) collective-permute-start(bf16[1,4,32,512]{3,2,1,0:T(8,128)(2,1)S(1)} %get-tuple-element.66), channel_id=1, source_target_pairs={{0,4},{2,6},{4,0},{6,2},{1,5},{3,7},{5,1},{7,3},{8,12},{10,14},{12... | collective-permute-start | bytes 393224 | tf_op jit(solution)/shard_map/ppermute | solution.py:196
  208.3 53.0 %collective-permute-start.23 = (bf16[1,4,32,512]{3,2,1,0:T(8,128)(2,1)S(1)}, bf16[1,4,32,512]{3,2,1,0:T(8,128)(2,1)S(1)}, u32[]{:S(2)}, u32[]{:S(2)}) collective-permute-start(bf16[1,4,32,512]{3,2,1,0:T(8,128)(2,1)S(1)} %get-tuple-element.67), channel_id=1, source_target_pairs={{0,2},{2,4},{4,6},{6,0},{1,3},{3,5},{5,7},{7,1},{8,10},{10,12},{12... | collective-permute-start | bytes 393224 | tf_op jit(solution)/shard_map/ppermute | solution.py:196
  218.9 44.3 %collective-permute-start.27 = (bf16[1,4,32,512]{3,2,1,0:T(8,128)(2,1)S(1)}, bf16[1,4,32,512]{3,2,1,0:T(8,128)(2,1)S(1)}, u32[]{:S(2)}, u32[]{:S(2)}) collective-permute-start(bf16[1,4,32,512]{3,2,1,0:T(8,128)(2,1)S(1)} %get-tuple-element.72), channel_id=1, source_target_pairs={{0,6},{2,0},{4,2},{6,4},{1,7},{3,1},{5,3},{7,5},{8,14},{10,8},{12,... | collective-permute-start | bytes 393224 | tf_op jit(solution)/shard_map/ppermute | solution.py:196
  218.9 44.3 %collective-permute-start.28 = (bf16[1,4,32,512]{3,2,1,0:T(8,128)(2,1)S(1)}, bf16[1,4,32,512]{3,2,1,0:T(8,128)(2,1)S(1)}, u32[]{:S(2)}, u32[]{:S(2)}) collective-permute-start(bf16[1,4,32,512]{3,2,1,0:T(8,128)(2,1)S(1)} %get-tuple-element.73), channel_id=1, source_target_pairs={{0,4},{2,6},{4,0},{6,2},{1,5},{3,7},{5,1},{7,3},{8,12},{10,14},{12... | collective-permute-start | bytes 393224 | tf_op jit(solution)/shard_map/ppermute | solution.py:196
  219.7 43.6 %collective-permute-start.29 = (bf16[1,4,32,512]{3,2,1,0:T(8,128)(2,1)S(1)}, bf16[1,4,32,512]{3,2,1,0:T(8,128)(2,1)S(1)}, u32[]{:S(2)}, u32[]{:S(2)}) collective-permute-start(bf16[1,4,32,512]{3,2,1,0:T(8,128)(2,1)S(1)} %get-tuple-element.74), channel_id=1, source_target_pairs={{0,2},{2,4},{4,6},{6,0},{1,3},{3,5},{5,7},{7,1},{8,10},{10,12},{12... | collective-permute-start | bytes 393224 | tf_op jit(solution)/shard_map/ppermute | solution.py:196
  (18 other events, 241.1 us)

commit v2 on v1

--- a/solution.py
+++ b/solution.py
@@ -10,6 +10,7 @@
 E = 128
 GROUP = 16
 CHUNKS = 5
+AHEAD = 2
 HIGHEST = lax.Precision.HIGHEST
 VMEM = 48 * 1024 * 1024
 
@@ -31,22 +32,22 @@
         o_ref[0, 0, :, cols] = o.astype(jnp.bfloat16)
 
 
-def spatial_attention(projected, step):
-    _, clips, frames, patches, width = projected.shape
+def spatial_attention(projected, chunk, cols):
+    _, clips, frames, patches, _ = projected.shape
     spec = lambda which: pl.BlockSpec(
-        (1, 1, 1, patches, step), lambda c, f, j: (which, c, f, 0, j)
+        (1, 1, 1, patches, cols), lambda c, f: (which, c, f, 0, chunk)
     )
     return pl.pallas_call(
         spatial_kernel,
-        grid=(clips, frames, width // step),
+        grid=(clips, frames),
         in_specs=[spec(0), spec(1), spec(2)],
-        out_specs=pl.BlockSpec((1, 1, patches, step), lambda c, f, j: (c, f, 0, j)),
-        out_shape=jax.ShapeDtypeStruct((clips, frames, patches, width), jnp.bfloat16),
-        compiler_params=params(),
-        cost_estimate=pl.CostEstimate(
-            flops=4 * clips * frames * patches * patches * width,
-            bytes_accessed=8 * clips * frames * patches * width,
-            transcendentals=clips * frames * patches * patches * (width // E),
+        out_specs=pl.BlockSpec((1, 1, patches, cols), lambda c, f: (c, f, 0, 0)),
+        out_shape=jax.ShapeDtypeStruct((clips, frames, patches, cols), jnp.bfloat16),
+        compiler_params=params(),
+        cost_estimate=pl.CostEstimate(
+            flops=4 * clips * frames * patches * patches * cols,
+            bytes_accessed=8 * clips * frames * patches * cols,
+            transcendentals=clips * frames * patches * patches * (cols // E),
         ),
         name="spatial",
     )(projected, projected, projected)
@@ -149,7 +150,7 @@
 
 
 def combine_kernel(n, me_ref, spatial_ref, *refs):
-    parts, out_ref = refs[:n], refs[n]
+    parts, out_ref = refs[:n], refs[-1]
     rows = parts[0].shape[2]
     for d in range(n):
         at = pl.ds(pl.multiple_of(lax.rem(me_ref[0] + d, n) * rows, rows), rows)
@@ -157,21 +158,23 @@
         out_ref[0, :, at, :] = total.astype(jnp.bfloat16)
 
 
-def combine(mixed, parts, me, n, chunk, cols):
-    clips, frames, patches, width = mixed.shape
+def combine(mixed, spatial, parts, me, n, chunk, width):
+    clips, frames, patches, cols = spatial.shape
     rows = patches // n
-    whole = pl.BlockSpec((1, frames, patches, cols), lambda c, me_ref: (c, 0, 0, chunk))
     part = pl.BlockSpec((1, frames, rows, cols), lambda c, me_ref: (c, 0, 0, 0))
+    before = [] if mixed is None else [mixed]
     return pl.pallas_call(
         functools.partial(combine_kernel, n),
         grid_spec=pltpu.PrefetchScalarGridSpec(
             num_scalar_prefetch=1,
             grid=(clips,),
-            in_specs=[whole] + [part] * n,
-            out_specs=whole,
-        ),
-        out_shape=jax.ShapeDtypeStruct(mixed.shape, mixed.dtype),
-        input_output_aliases={1: 0},
+            in_specs=[pl.BlockSpec((1, frames, patches, cols), lambda c, me_ref: (c, 0, 0, 0))]
+            + [part] * n
+            + [pl.BlockSpec(memory_space=pl.ANY)] * len(before),
+            out_specs=pl.BlockSpec((1, frames, patches, cols), lambda c, me_ref: (c, 0, 0, chunk)),
+        ),
+        out_shape=jax.ShapeDtypeStruct((clips, frames, patches, width), jnp.bfloat16),
+        input_output_aliases={n + 2: 0} if before else {},
         compiler_params=params(),
         cost_estimate=pl.CostEstimate(
             flops=clips * frames * patches * cols,
@@ -179,7 +182,11 @@
             transcendentals=0,
         ),
         name="combine",
-    )(me, mixed, *parts)
+    )(me, spatial, *parts, *before)
+
+
+def after(x, *others):
+    return lax.optimization_barrier((x, *others))[0]
 
 
 def local(n, projected, codes, action_weight, clip_ids, frame_map, segments):
@@ -195,11 +202,14 @@
     def send(x, d):
         return lax.ppermute(x, "frame", [(i, (i + d) % n) for i in range(n)])
 
-    arrived = []
-    for j in range(chunks):
+    def forward(j, *others):
         packed = pack(projected, me, n, far_first, j, cols)
+        if others:
+            packed = lax.optimization_barrier((*packed, *others))[: n - 1]
         got = {d: send(x, d) for d, x in zip(far_first, packed)}
-        arrived.append([got[d] for d in range(1, n)])
+        return [got[d] for d in range(1, n)]
+
+    arrived = [forward(j) for j in range(min(AHEAD, chunks))]
 
     source = lax.rem(me_scalar - jnp.arange(n) + n, n)
     order = (source[:, None] * frames + jnp.arange(frames)[None, :]).reshape(-1)
@@ -225,11 +235,17 @@
     )
     action = jnp.einsum("csa,ad->csd", codes_slot, action_weight, precision=HIGHEST)
 
-    mixed = spatial_attention(projected, cols)
+    mixed = None
     for j in range(chunks):
-        done = temporal_attention(projected, arrived[j], bias, action, me, n, j, cols)
+        spatial = spatial_attention(projected, j, cols)
+        done = temporal_attention(
+            projected, arrived[j], bias, action, after(me, spatial), n, j, cols
+        )
         back = {d: send(done[d], -d) for d in far_first}
-        mixed = combine(mixed, [done[0]] + [back[d] for d in range(1, n)], me, n, j, cols)
+        if j + AHEAD < chunks:
+            arrived.append(forward(j + AHEAD, done[1]))
+        parts = [done[0]] + [back[d] for d in range(1, n)]
+        mixed = combine(mixed, spatial, parts, me, n, j, width)
     return mixed
 
 

time: 266 us -> 238 us (0.89)
  waiting for transfers between devices: 76.3 us -> 50.5 us
  starting transfers between devices: 105 us -> 111 us
  local copies, waits for them, and re-layouts: 7.22 us -> 1.29 us
    ppermute x30, waiting for transfers between devices: 76.3 us -> 50.5 us  [send(): return lax.ppermute(x, 'frame', [(i, (i + d) % n) for i in range(n)])]
    ppermute x30, starting transfers between devices: 105 us -> 111 us  [send(): return lax.ppermute(x, 'frame', [(i, (i + d) % n) for i in range(n)])]
    pallas_call x5, Pallas kernels: 9.78 us -> 4.59 us  [combine(): pl.pallas_call(functools.partial(combine_kernel, n), grid_spec=pltpu.Pref...]
    unnamed x24 -> x22, local copies, waits for them, and re-layouts: 5.26 us -> 0.79 us
    pallas_call x1 -> x5, Pallas kernels: 30.3 us -> 33.9 us  [spatial_attention(): pl.pallas_call(spatial_kernel, grid=(clips, frames), in_specs=[spec(0), s...]
  transfers between devices with their start and end apart: 30 -> 30, of which waited for: 6 -> 7; matrix products, arithmetic and copies ran while one was open for 1% -> 1% of each run, Pallas kernels for 25% -> 27%
where the time goes in v2:
time: 238 us; the launch traced here: 237 us
  starting transfers between devices  111 us (47%)
  Pallas kernels  68.1 us (29%)
  waiting for transfers between devices  50.5 us (21%)
  blocking collectives  5.18 us (2%)
    ppermute x30, starting transfers between devices, send(): return lax.ppermute(x, 'frame', [(i, (i + d) % n) for i in range(n)])  111 us
    ppermute x30, waiting for transfers between devices, send(): return lax.ppermute(x, 'frame', [(i, (i + d) % n) for i in range(n)])  50.5 us
    pallas_call x5, Pallas kernels, spatial_attention(): pl.pallas_call(spatial_kernel, grid=(clips, frames), in_specs=[spec(0), s...  33.9 us
    pallas_call x5, Pallas kernels, temporal_attention(): pl.pallas_call(functools.partial(temporal_kernel, n), grid_spec=pltpu.Pre...  16.6 us
    pallas_call x5, Pallas kernels, pack(): pl.pallas_call(functools.partial(pack_kernel, n), grid_spec=pltpu.Prefetc...  12.9 us
    all_gather x1, blocking collectives, local(): all_codes = lax.all_gather(codes, 'dp', axis=0, tiled=True)  5.18 us
  transfers between devices with their start and end apart: 30, of which 7 were waited for; matrix products, arithmetic and copies ran while one was open for 1% of the time, Pallas kernels for 27%

profile of v2, /device:TPU:0, one launch (start us, length us, event | category | flops | bytes accessed | tf_op | source)
XLA Modules:
  0.0 237.5 jit_solution(11985531865903023539)
XLA Ops:
  14.5 5.2 %all_gather.3 = f32[4,16,32]{2,1,0:T(8,128)S(1)} all-gather(f32[1,16,32]{2,1,0:T(8,128)S(1)} %copy-done.7), channel_id=1, replica_groups=mesh['dp'=4,'frame'=4,'mp'=2] {'dp'}, dimensions={0}, use_global_device_ids=true | all-gather | bytes 10240 | tf_op jit(solution)/shard_map/all_gather | solution.py:229
  26.7 7.0 %spatial.7.spatial_ref = bf16[1,4,128,512]{3,2,1,0:T(8,128)(2,1)S(1)} custom-call(bf16[6,1,4,128,2560]{4,3,2,1,0:T(8,128)(2,1)} %refs_0_.19, bf16[6,1,4,128,2560]{4,3,2,1,0:T(8,128)(2,1)} %refs_0_.19, bf16[6,1,4,128,2560]{4,3,2,1,0:T(8,128)(2,1)} %refs_0_.19), custom_call_target="tpu_custom_call" | custom-call | flops 134217728 | bytes 2097152 | tf_op jit(solution)/shard_map/spatial/pallas_call | solution.py:40
  35.2 3.3 %temporal.5 = (bf16[1,4,32,512]{3,2,1,0:T(8,128)(2,1)S(1)}, bf16[1,4,32,512]{3,2,1,0:T(8,128)(2,1)S(1)}, bf16[1,4,32,512]{3,2,1,0:T(8,128)(2,1)S(1)}, bf16[1,4,32,512]{3,2,1,0:T(8,128)(2,1)S(1)}) custom-call(s32[1]{0:T(128)} %bitcast.me_ref, f32[1,256,256]{2,1,0:T(8,128)S(1)} %and_select_fusion.bias_ref, ...), custom_call_target="tpu_custom_call" | custom-call | flops 268435456 | bytes 2097152 | tf_op jit(solution)/shard_map/temporal/pallas_call | solution.py:125
  38.5 25.9 %collective-permute-start.3 = (bf16[3,1,4,32,512]{4,3,2,1,0:T(8,128)(2,1)S(1)}, bf16[3,1,4,32,512]{4,3,2,1,0:T(8,128)(2,1)S(1)}, u32[]{:S(2)}, u32[]{:S(2)}) collective-permute-start(bf16[3,1,4,32,512]{4,3,2,1,0:T(8,128)(2,1)S(1)} %copy-done.6), channel_id=1, source_target_pairs={{0,2},{2,4},{4,6},{6,0},{1,3},{3,5},{5,7},{7,1},{8,10},{10,12},{12... | collective-permute-start | bytes 1179656 | tf_op jit(solution)/shard_map/ppermute | solution.py:203
  66.8 6.7 %spatial.9.spatial_ref = bf16[1,4,128,512]{3,2,1,0:T(8,128)(2,1)S(1)} custom-call(bf16[6,1,4,128,2560]{4,3,2,1,0:T(8,128)(2,1)} %refs_0_.19, bf16[6,1,4,128,2560]{4,3,2,1,0:T(8,128)(2,1)} %refs_0_.19, bf16[6,1,4,128,2560]{4,3,2,1,0:T(8,128)(2,1)} %refs_0_.19), custom_call_target="tpu_custom_call" | custom-call | flops 134217728 | bytes 2097152 | tf_op jit(solution)/shard_map/spatial/pallas_call | solution.py:40
  75.8 9.1 %collective-permute-done.13.refs_2_ = bf16[3,1,4,32,512]{4,3,2,1,0:T(8,128)(2,1)S(1)} collective-permute-done((bf16[3,1,4,32,512]{4,3,2,1,0:T(8,128)(2,1)}, bf16[3,1,4,32,512]{4,3,2,1,0:T(8,128)(2,1)S(1)}, u32[]{:S(2)}, u32[]{:S(2)}) %collective-permute-start.13) | collective-permute-done | bytes 393248 | tf_op jit(solution)/shard_map/ppermute | solution.py:203
  84.9 12.5 %collective-permute-start.27 = (bf16[1,4,32,512]{3,2,1,0:T(8,128)(2,1)S(1)}, bf16[1,4,32,512]{3,2,1,0:T(8,128)(2,1)S(1)}, u32[]{:S(2)}, u32[]{:S(2)}) collective-permute-start(bf16[1,4,32,512]{3,2,1,0:T(8,128)(2,1)S(1)} %get-tuple-element.66), channel_id=1, source_target_pairs={{0,6},{2,0},{4,2},{6,4},{1,7},{3,1},{5,3},{7,5},{8,14},{10,8},{12,... | collective-permute-start | bytes 393224 | tf_op jit(solution)/shard_map/ppermute | solution.py:203
  97.4 3.3 %temporal.8 = (bf16[1,4,32,512]{3,2,1,0:T(8,128)(2,1)S(1)}, bf16[1,4,32,512]{3,2,1,0:T(8,128)(2,1)S(1)}, bf16[1,4,32,512]{3,2,1,0:T(8,128)(2,1)S(1)}, bf16[1,4,32,512]{3,2,1,0:T(8,128)(2,1)S(1)}) custom-call(s32[1]{0:T(128)} %bitcast.me_ref, f32[1,256,256]{2,1,0:T(8,128)S(1)} %and_select_fusion.bias_ref, ...), custom_call_target="tpu_custom_call" | custom-call | flops 268435456 | bytes 2097152 | tf_op jit(solution)/shard_map/temporal/pallas_call | solution.py:125
  101.5 9.5 %collective-permute-done.27.refs_1_ = bf16[1,4,32,512]{3,2,1,0:T(8,128)(2,1)S(1)} collective-permute-done((bf16[1,4,32,512]{3,2,1,0:T(8,128)(2,1)S(1)}, bf16[1,4,32,512]{3,2,1,0:T(8,128)(2,1)S(1)}, u32[]{:S(2)}, u32[]{:S(2)}) %collective-permute-start.27) | collective-permute-done | bytes 131104 | tf_op jit(solution)/shard_map/ppermute | solution.py:203
  111.0 9.9 %collective-permute-start.28 = (bf16[1,4,32,512]{3,2,1,0:T(8,128)(2,1)S(1)}, bf16[1,4,32,512]{3,2,1,0:T(8,128)(2,1)S(1)}, u32[]{:S(2)}, u32[]{:S(2)}) collective-permute-start(bf16[1,4,32,512]{3,2,1,0:T(8,128)(2,1)S(1)} %get-tuple-element.101), channel_id=1, source_target_pairs={{0,4},{2,6},{4,0},{6,2},{1,5},{3,7},{5,1},{7,3},{8,12},{10,14},{12... | collective-permute-start | bytes 393224 | tf_op jit(solution)/shard_map/ppermute | solution.py:203
  120.8 3.7 %collective-permute-done.28.refs_2_ = bf16[1,4,32,512]{3,2,1,0:T(8,128)(2,1)S(1)} collective-permute-done((bf16[1,4,32,512]{3,2,1,0:T(8,128)(2,1)S(1)}, bf16[1,4,32,512]{3,2,1,0:T(8,128)(2,1)S(1)}, u32[]{:S(2)}, u32[]{:S(2)}) %collective-permute-start.28) | collective-permute-done | bytes 131104 | tf_op jit(solution)/shard_map/ppermute | solution.py:203
  127.3 4.0 %collective-permute-start.29 = (bf16[1,4,32,512]{3,2,1,0:T(8,128)(2,1)S(1)}, bf16[1,4,32,512]{3,2,1,0:T(8,128)(2,1)S(1)}, u32[]{:S(2)}, u32[]{:S(2)}) collective-permute-start(bf16[1,4,32,512]{3,2,1,0:T(8,128)(2,1)S(1)} %get-tuple-element.102), channel_id=1, source_target_pairs={{0,2},{2,4},{4,6},{6,0},{1,3},{3,5},{5,7},{7,1},{8,10},{10,12},{12... | collective-permute-start | bytes 393224 | tf_op jit(solution)/shard_map/ppermute | solution.py:203
  133.5 6.7 %spatial.6.spatial_ref = bf16[1,4,128,512]{3,2,1,0:T(8,128)(2,1)S(1)} custom-call(bf16[6,1,4,128,2560]{4,3,2,1,0:T(8,128)(2,1)} %refs_0_.19, bf16[6,1,4,128,2560]{4,3,2,1,0:T(8,128)(2,1)} %refs_0_.19, bf16[6,1,4,128,2560]{4,3,2,1,0:T(8,128)(2,1)} %refs_0_.19), custom_call_target="tpu_custom_call" | custom-call | flops 134217728 | bytes 2097152 | tf_op jit(solution)/shard_map/spatial/pallas_call | solution.py:40
  141.8 3.3 %temporal.6 = (bf16[1,4,32,512]{3,2,1,0:T(8,128)(2,1)S(1)}, bf16[1,4,32,512]{3,2,1,0:T(8,128)(2,1)S(1)}, bf16[1,4,32,512]{3,2,1,0:T(8,128)(2,1)S(1)}, bf16[1,4,32,512]{3,2,1,0:T(8,128)(2,1)S(1)}) custom-call(s32[1]{0:T(128)} %bitcast.me_ref, f32[1,256,256]{2,1,0:T(8,128)S(1)} %and_select_fusion.bias_ref, ...), custom_call_target="tpu_custom_call" | custom-call | flops 268435456 | bytes 2097152 | tf_op jit(solution)/shard_map/temporal/pallas_call | solution.py:125
  145.1 13.7 %collective-permute-start.6 = (bf16[3,1,4,32,512]{4,3,2,1,0:T(8,128)(2,1)S(1)}, bf16[3,1,4,32,512]{4,3,2,1,0:T(8,128)(2,1)S(1)}, u32[]{:S(2)}, u32[]{:S(2)}) collective-permute-start(bf16[3,1,4,32,512]{4,3,2,1,0:T(8,128)(2,1)S(1)} %get-tuple-element.71), channel_id=1, source_target_pairs={{0,2},{2,4},{4,6},{6,0},{1,3},{3,5},{5,7},{7,1},{8,10},{10,12},{12... | collective-permute-start | bytes 1179656 | tf_op jit(solution)/shard_map/ppermute | solution.py:203
  163.7 6.7 %spatial.8.spatial_ref = bf16[1,4,128,512]{3,2,1,0:T(8,128)(2,1)S(1)} custom-call(bf16[6,1,4,128,2560]{4,3,2,1,0:T(8,128)(2,1)} %refs_0_.19, bf16[6,1,4,128,2560]{4,3,2,1,0:T(8,128)(2,1)} %refs_0_.19, bf16[6,1,4,128,2560]{4,3,2,1,0:T(8,128)(2,1)} %refs_0_.19), custom_call_target="tpu_custom_call" | custom-call | flops 134217728 | bytes 2097152 | tf_op jit(solution)/shard_map/spatial/pallas_call | solution.py:40
  170.5 6.9 %collective-permute-start.26 = (bf16[1,4,32,512]{3,2,1,0:T(8,128)(2,1)S(1)}, bf16[1,4,32,512]{3,2,1,0:T(8,128)(2,1)S(1)}, u32[]{:S(2)}, u32[]{:S(2)}) collective-permute-start(bf16[1,4,32,512]{3,2,1,0:T(8,128)(2,1)S(1)} %get-tuple-element.99), channel_id=1, source_target_pairs={{0,2},{2,4},{4,6},{6,0},{1,3},{3,5},{5,7},{7,1},{8,10},{10,12},{12... | collective-permute-start | bytes 393224 | tf_op jit(solution)/shard_map/ppermute | solution.py:203
  177.4 3.3 %temporal.9 = (bf16[1,4,32,512]{3,2,1,0:T(8,128)(2,1)S(1)}, bf16[1,4,32,512]{3,2,1,0:T(8,128)(2,1)S(1)}, bf16[1,4,32,512]{3,2,1,0:T(8,128)(2,1)S(1)}, bf16[1,4,32,512]{3,2,1,0:T(8,128)(2,1)S(1)}) custom-call(s32[1]{0:T(128)} %bitcast.me_ref, f32[1,256,256]{2,1,0:T(8,128)S(1)} %and_select_fusion.bias_ref, ...), custom_call_target="tpu_custom_call" | custom-call | flops 268435456 | bytes 2097152 | tf_op jit(solution)/shard_map/temporal/pallas_call | solution.py:125
  180.7 20.0 %collective-permute-done.25.refs_2_ = bf16[1,4,32,512]{3,2,1,0:T(8,128)(2,1)S(1)} collective-permute-done((bf16[1,4,32,512]{3,2,1,0:T(8,128)(2,1)S(1)}, bf16[1,4,32,512]{3,2,1,0:T(8,128)(2,1)S(1)}, u32[]{:S(2)}, u32[]{:S(2)}) %collective-permute-start.25) | collective-permute-done | bytes 131104 | tf_op jit(solution)/shard_map/ppermute | solution.py:203
  200.7 3.9 %collective-permute-start.21 = (bf16[1,4,32,512]{3,2,1,0:T(8,128)(2,1)S(1)}, bf16[1,4,32,512]{3,2,1,0:T(8,128)(2,1)S(1)}, u32[]{:S(2)}, u32[]{:S(2)}) collective-permute-start(bf16[1,4,32,512]{3,2,1,0:T(8,128)(2,1)S(1)} %get-tuple-element.70), channel_id=1, source_target_pairs={{0,6},{2,0},{4,2},{6,4},{1,7},{3,1},{5,3},{7,5},{8,14},{10,8},{12,... | collective-permute-start | bytes 393224 | tf_op jit(solution)/shard_map/ppermute | solution.py:203
  205.2 3.3 %collective-permute-start.18 = (bf16[1,4,32,512]{3,2,1,0:T(8,128)(2,1)S(1)}, bf16[1,4,32,512]{3,2,1,0:T(8,128)(2,1)S(1)}, u32[]{:S(2)}, u32[]{:S(2)}) collective-permute-start(bf16[1,4,32,512]{3,2,1,0:T(8,128)(2,1)S(1)} %get-tuple-element.91), channel_id=1, source_target_pairs={{0,6},{2,0},{4,2},{6,4},{1,7},{3,1},{5,3},{7,5},{8,14},{10,8},{12,... | collective-permute-start | bytes 393224 | tf_op jit(solution)/shard_map/ppermute | solution.py:203
  208.5 6.7 %spatial.5.spatial_ref = bf16[1,4,128,512]{3,2,1,0:T(8,128)(2,1)S(1)} custom-call(bf16[6,1,4,128,2560]{4,3,2,1,0:T(8,128)(2,1)} %refs_0_.19, bf16[6,1,4,128,2560]{4,3,2,1,0:T(8,128)(2,1)} %refs_0_.19, bf16[6,1,4,128,2560]{4,3,2,1,0:T(8,128)(2,1)} %refs_0_.19), custom_call_target="tpu_custom_call" | custom-call | flops 134217728 | bytes 2097152 | tf_op jit(solution)/shard_map/spatial/pallas_call | solution.py:40
  215.2 3.3 %temporal.7 = (bf16[1,4,32,512]{3,2,1,0:T(8,128)(2,1)S(1)}, bf16[1,4,32,512]{3,2,1,0:T(8,128)(2,1)S(1)}, bf16[1,4,32,512]{3,2,1,0:T(8,128)(2,1)S(1)}, bf16[1,4,32,512]{3,2,1,0:T(8,128)(2,1)S(1)}) custom-call(s32[1]{0:T(128)} %bitcast.me_ref, f32[1,256,256]{2,1,0:T(8,128)S(1)} %and_select_fusion.bias_ref, ...), custom_call_target="tpu_custom_call" | custom-call | flops 268435456 | bytes 2097152 | tf_op jit(solution)/shard_map/temporal/pallas_call | solution.py:125
  228.2 5.5 %collective-permute-done.19.refs_2_ = bf16[1,4,32,512]{3,2,1,0:T(8,128)(2,1)S(1)} collective-permute-done((bf16[1,4,32,512]{3,2,1,0:T(8,128)(2,1)S(1)}, bf16[1,4,32,512]{3,2,1,0:T(8,128)(2,1)S(1)}, u32[]{:S(2)}, u32[]{:S(2)}) %collective-permute-start.19) | collective-permute-done | bytes 131104 | tf_op jit(solution)/shard_map/ppermute | solution.py:203
  (94 shorter events, 53.6 us)
Async XLA Ops:
  3.1 17.7 %collective-permute-start = (bf16[3,1,4,32,512]{4,3,2,1,0:T(8,128)(2,1)S(1)}, bf16[3,1,4,32,512]{4,3,2,1,0:T(8,128)(2,1)S(1)}, u32[]{:S(2)}, u32[]{:S(2)}) collective-permute-start(bf16[3,1,4,32,512]{4,3,2,1,0:T(8,128)(2,1)S(1)} %get-tuple-element.63), channel_id=1, source_target_pairs={{0,2},{2,4},{4,6},{6,0},{1,3},{3,5},{5,7},{7,1},{8,10},{10,12},{12... | collective-permute-start | bytes 1179656 | tf_op jit(solution)/shard_map/ppermute | solution.py:203
  6.2 29.0 %collective-permute-start.1 = (bf16[3,1,4,32,512]{4,3,2,1,0:T(8,128)(2,1)}, bf16[3,1,4,32,512]{4,3,2,1,0:T(8,128)(2,1)S(1)}, u32[]{:S(2)}, u32[]{:S(2)}) collective-permute-start(bf16[3,1,4,32,512]{4,3,2,1,0:T(8,128)(2,1)} %get-tuple-element.64), channel_id=1, source_target_pairs={{0,4},{2,6},{4,0},{6,2},{1,5},{3,7},{5,1},{7,3},{8,12},{10,14},{12... | collective-permute-start | bytes 1179656 | tf_op jit(solution)/shard_map/ppermute | solution.py:203
  8.8 26.4 %collective-permute-start.2 = (bf16[3,1,4,32,512]{4,3,2,1,0:T(8,128)(2,1)}, bf16[3,1,4,32,512]{4,3,2,1,0:T(8,128)(2,1)S(1)}, u32[]{:S(2)}, u32[]{:S(2)}) collective-permute-start(bf16[3,1,4,32,512]{4,3,2,1,0:T(8,128)(2,1)} %get-tuple-element.65), channel_id=1, source_target_pairs={{0,6},{2,0},{4,2},{6,4},{1,7},{3,1},{5,3},{7,5},{8,14},{10,8},{12,... | collective-permute-start | bytes 1179656 | tf_op jit(solution)/shard_map/ppermute | solution.py:203
  13.4 52.8 %collective-permute-start.12 = (bf16[3,1,4,32,512]{4,3,2,1,0:T(8,128)(2,1)}, bf16[3,1,4,32,512]{4,3,2,1,0:T(8,128)(2,1)S(1)}, u32[]{:S(2)}, u32[]{:S(2)}) collective-permute-start(bf16[3,1,4,32,512]{4,3,2,1,0:T(8,128)(2,1)} %get-tuple-element.83), channel_id=1, source_target_pairs={{0,2},{2,4},{4,6},{6,0},{1,3},{3,5},{5,7},{7,1},{8,10},{10,12},{12... | collective-permute-start | bytes 1179656 | tf_op jit(solution)/shard_map/ppermute | solution.py:203
  14.0 70.8 %collective-permute-start.13 = (bf16[3,1,4,32,512]{4,3,2,1,0:T(8,128)(2,1)}, bf16[3,1,4,32,512]{4,3,2,1,0:T(8,128)(2,1)S(1)}, u32[]{:S(2)}, u32[]{:S(2)}) collective-permute-start(bf16[3,1,4,32,512]{4,3,2,1,0:T(8,128)(2,1)} %get-tuple-element.84), channel_id=1, source_target_pairs={{0,4},{2,6},{4,0},{6,2},{1,5},{3,7},{5,1},{7,3},{8,12},{10,14},{12... | collective-permute-start | bytes 1179656 | tf_op jit(solution)/shard_map/ppermute | solution.py:203
  20.8 76.5 %collective-permute-start.14 = (bf16[3,1,4,32,512]{4,3,2,1,0:T(8,128)(2,1)}, bf16[3,1,4,32,512]{4,3,2,1,0:T(8,128)(2,1)S(1)}, u32[]{:S(2)}, u32[]{:S(2)}) collective-permute-start(bf16[3,1,4,32,512]{4,3,2,1,0:T(8,128)(2,1)} %get-tuple-element.85), channel_id=1, source_target_pairs={{0,6},{2,0},{4,2},{6,4},{1,7},{3,1},{5,3},{7,5},{8,14},{10,8},{12,... | collective-permute-start | bytes 1179656 | tf_op jit(solution)/shard_map/ppermute | solution.py:203
  38.5 88.8 %collective-permute-start.3 = (bf16[3,1,4,32,512]{4,3,2,1,0:T(8,128)(2,1)S(1)}, bf16[3,1,4,32,512]{4,3,2,1,0:T(8,128)(2,1)S(1)}, u32[]{:S(2)}, u32[]{:S(2)}) collective-permute-start(bf16[3,1,4,32,512]{4,3,2,1,0:T(8,128)(2,1)S(1)} %copy-done.6), channel_id=1, source_target_pairs={{0,2},{2,4},{4,6},{6,0},{1,3},{3,5},{5,7},{7,1},{8,10},{10,12},{12... | collective-permute-start | bytes 1179656 | tf_op jit(solution)/shard_map/ppermute | solution.py:203
  64.4 66.9 %collective-permute-start.4 = (bf16[3,1,4,32,512]{4,3,2,1,0:T(8,128)(2,1)S(1)}, bf16[3,1,4,32,512]{4,3,2,1,0:T(8,128)(2,1)S(1)}, u32[]{:S(2)}, u32[]{:S(2)}) collective-permute-start(bf16[3,1,4,32,512]{4,3,2,1,0:T(8,128)(2,1)S(1)} %copy-done.4), channel_id=1, source_target_pairs={{0,4},{2,6},{4,0},{6,2},{1,5},{3,7},{5,1},{7,3},{8,12},{10,14},{12... | collective-permute-start | bytes 1179656 | tf_op jit(solution)/shard_map/ppermute | solution.py:203
  66.2 74.1 %collective-permute-start.5 = (bf16[3,1,4,32,512]{4,3,2,1,0:T(8,128)(2,1)S(1)}, bf16[3,1,4,32,512]{4,3,2,1,0:T(8,128)(2,1)S(1)}, u32[]{:S(2)}, u32[]{:S(2)}) collective-permute-start(bf16[3,1,4,32,512]{4,3,2,1,0:T(8,128)(2,1)S(1)} %copy-done.2), channel_id=1, source_target_pairs={{0,6},{2,0},{4,2},{6,4},{1,7},{3,1},{5,3},{7,5},{8,14},{10,8},{12,... | collective-permute-start | bytes 1179656 | tf_op jit(solution)/shard_map/ppermute | solution.py:203
  84.9 26.1 %collective-permute-start.27 = (bf16[1,4,32,512]{3,2,1,0:T(8,128)(2,1)S(1)}, bf16[1,4,32,512]{3,2,1,0:T(8,128)(2,1)S(1)}, u32[]{:S(2)}, u32[]{:S(2)}) collective-permute-start(bf16[1,4,32,512]{3,2,1,0:T(8,128)(2,1)S(1)} %get-tuple-element.66), channel_id=1, source_target_pairs={{0,6},{2,0},{4,2},{6,4},{1,7},{3,1},{5,3},{7,5},{8,14},{10,8},{12,... | collective-permute-start | bytes 393224 | tf_op jit(solution)/shard_map/ppermute | solution.py:203
  100.7 60.1 %collective-permute-start.15 = (bf16[3,1,4,32,512]{4,3,2,1,0:T(8,128)(2,1)S(1)}, bf16[3,1,4,32,512]{4,3,2,1,0:T(8,128)(2,1)S(1)}, u32[]{:S(2)}, u32[]{:S(2)}) collective-permute-start(bf16[3,1,4,32,512]{4,3,2,1,0:T(8,128)(2,1)S(1)} %get-tuple-element.87), channel_id=1, source_target_pairs={{0,2},{2,4},{4,6},{6,0},{1,3},{3,5},{5,7},{7,1},{8,10},{10,12},{12... | collective-permute-start | bytes 1179656 | tf_op jit(solution)/shard_map/ppermute | solution.py:203
  124.5 39.2 %collective-permute-start.16 = (bf16[3,1,4,32,512]{4,3,2,1,0:T(8,128)(2,1)S(1)}, bf16[3,1,4,32,512]{4,3,2,1,0:T(8,128)(2,1)S(1)}, u32[]{:S(2)}, u32[]{:S(2)}) collective-permute-start(bf16[3,1,4,32,512]{4,3,2,1,0:T(8,128)(2,1)S(1)} %get-tuple-element.88), channel_id=1, source_target_pairs={{0,4},{2,6},{4,0},{6,2},{1,5},{3,7},{5,1},{7,3},{8,12},{10,14},{12... | collective-permute-start | bytes 1179656 | tf_op jit(solution)/shard_map/ppermute | solution.py:203
  127.3 17.8 %collective-permute-start.29 = (bf16[1,4,32,512]{3,2,1,0:T(8,128)(2,1)S(1)}, bf16[1,4,32,512]{3,2,1,0:T(8,128)(2,1)S(1)}, u32[]{:S(2)}, u32[]{:S(2)}) collective-permute-start(bf16[1,4,32,512]{3,2,1,0:T(8,128)(2,1)S(1)} %get-tuple-element.102), channel_id=1, source_target_pairs={{0,2},{2,4},{4,6},{6,0},{1,3},{3,5},{5,7},{7,1},{8,10},{10,12},{12... | collective-permute-start | bytes 393224 | tf_op jit(solution)/shard_map/ppermute | solution.py:203
  131.3 27.6 %collective-permute-start.24 = (bf16[1,4,32,512]{3,2,1,0:T(8,128)(2,1)S(1)}, bf16[1,4,32,512]{3,2,1,0:T(8,128)(2,1)S(1)}, u32[]{:S(2)}, u32[]{:S(2)}) collective-permute-start(bf16[1,4,32,512]{3,2,1,0:T(8,128)(2,1)S(1)} %get-tuple-element.86), channel_id=1, source_target_pairs={{0,6},{2,0},{4,2},{6,4},{1,7},{3,1},{5,3},{7,5},{8,14},{10,8},{12,... | collective-permute-start | bytes 393224 | tf_op jit(solution)/shard_map/ppermute | solution.py:203
  140.3 30.2 %collective-permute-start.17 = (bf16[3,1,4,32,512]{4,3,2,1,0:T(8,128)(2,1)S(1)}, bf16[3,1,4,32,512]{4,3,2,1,0:T(8,128)(2,1)S(1)}, u32[]{:S(2)}, u32[]{:S(2)}) collective-permute-start(bf16[3,1,4,32,512]{4,3,2,1,0:T(8,128)(2,1)S(1)} %get-tuple-element.89), channel_id=1, source_target_pairs={{0,6},{2,0},{4,2},{6,4},{1,7},{3,1},{5,3},{7,5},{8,14},{10,8},{12,... | collective-permute-start | bytes 1179656 | tf_op jit(solution)/shard_map/ppermute | solution.py:203
  145.1 59.5 %collective-permute-start.6 = (bf16[3,1,4,32,512]{4,3,2,1,0:T(8,128)(2,1)S(1)}, bf16[3,1,4,32,512]{4,3,2,1,0:T(8,128)(2,1)S(1)}, u32[]{:S(2)}, u32[]{:S(2)}) collective-permute-start(bf16[3,1,4,32,512]{4,3,2,1,0:T(8,128)(2,1)S(1)} %get-tuple-element.71), channel_id=1, source_target_pairs={{0,2},{2,4},{4,6},{6,0},{1,3},{3,5},{5,7},{7,1},{8,10},{10,12},{12... | collective-permute-start | bytes 1179656 | tf_op jit(solution)/shard_map/ppermute | solution.py:203
  158.9 45.7 %collective-permute-start.7 = (bf16[3,1,4,32,512]{4,3,2,1,0:T(8,128)(2,1)S(1)}, bf16[3,1,4,32,512]{4,3,2,1,0:T(8,128)(2,1)S(1)}, u32[]{:S(2)}, u32[]{:S(2)}) collective-permute-start(bf16[3,1,4,32,512]{4,3,2,1,0:T(8,128)(2,1)S(1)} %get-tuple-element.72), channel_id=1, source_target_pairs={{0,4},{2,6},{4,0},{6,2},{1,5},{3,7},{5,1},{7,3},{8,12},{10,14},{12... | collective-permute-start | bytes 1179656 | tf_op jit(solution)/shard_map/ppermute | solution.py:203
  160.8 44.4 %collective-permute-start.8 = (bf16[3,1,4,32,512]{4,3,2,1,0:T(8,128)(2,1)S(1)}, bf16[3,1,4,32,512]{4,3,2,1,0:T(8,128)(2,1)S(1)}, u32[]{:S(2)}, u32[]{:S(2)}) collective-permute-start(bf16[3,1,4,32,512]{4,3,2,1,0:T(8,128)(2,1)S(1)} %get-tuple-element.73), channel_id=1, source_target_pairs={{0,6},{2,0},{4,2},{6,4},{1,7},{3,1},{5,3},{7,5},{8,14},{10,8},{12,... | collective-permute-start | bytes 1179656 | tf_op jit(solution)/shard_map/ppermute | solution.py:203
  163.7 37.0 %collective-permute-start.25 = (bf16[1,4,32,512]{3,2,1,0:T(8,128)(2,1)S(1)}, bf16[1,4,32,512]{3,2,1,0:T(8,128)(2,1)S(1)}, u32[]{:S(2)}, u32[]{:S(2)}) collective-permute-start(bf16[1,4,32,512]{3,2,1,0:T(8,128)(2,1)S(1)} %get-tuple-element.98), channel_id=1, source_target_pairs={{0,4},{2,6},{4,0},{6,2},{1,5},{3,7},{5,1},{7,3},{8,12},{10,14},{12... | collective-permute-start | bytes 393224 | tf_op jit(solution)/shard_map/ppermute | solution.py:203
  170.5 48.1 %collective-permute-start.26 = (bf16[1,4,32,512]{3,2,1,0:T(8,128)(2,1)S(1)}, bf16[1,4,32,512]{3,2,1,0:T(8,128)(2,1)S(1)}, u32[]{:S(2)}, u32[]{:S(2)}) collective-permute-start(bf16[1,4,32,512]{3,2,1,0:T(8,128)(2,1)S(1)} %get-tuple-element.99), channel_id=1, source_target_pairs={{0,2},{2,4},{4,6},{6,0},{1,3},{3,5},{5,7},{7,1},{8,10},{10,12},{12... | collective-permute-start | bytes 393224 | tf_op jit(solution)/shard_map/ppermute | solution.py:203
  200.7 19.0 %collective-permute-start.21 = (bf16[1,4,32,512]{3,2,1,0:T(8,128)(2,1)S(1)}, bf16[1,4,32,512]{3,2,1,0:T(8,128)(2,1)S(1)}, u32[]{:S(2)}, u32[]{:S(2)}) collective-permute-start(bf16[1,4,32,512]{3,2,1,0:T(8,128)(2,1)S(1)} %get-tuple-element.70), channel_id=1, source_target_pairs={{0,6},{2,0},{4,2},{6,4},{1,7},{3,1},{5,3},{7,5},{8,14},{10,8},{12,... | collective-permute-start | bytes 393224 | tf_op jit(solution)/shard_map/ppermute | solution.py:203
  204.6 17.1 %collective-permute-start.23 = (bf16[1,4,32,512]{3,2,1,0:T(8,128)(2,1)S(1)}, bf16[1,4,32,512]{3,2,1,0:T(8,128)(2,1)S(1)}, u32[]{:S(2)}, u32[]{:S(2)}) collective-permute-start(bf16[1,4,32,512]{3,2,1,0:T(8,128)(2,1)S(1)} %get-tuple-element.96), channel_id=1, source_target_pairs={{0,2},{2,4},{4,6},{6,0},{1,3},{3,5},{5,7},{7,1},{8,10},{10,12},{12... | collective-permute-start | bytes 393224 | tf_op jit(solution)/shard_map/ppermute | solution.py:203
  205.2 18.9 %collective-permute-start.18 = (bf16[1,4,32,512]{3,2,1,0:T(8,128)(2,1)S(1)}, bf16[1,4,32,512]{3,2,1,0:T(8,128)(2,1)S(1)}, u32[]{:S(2)}, u32[]{:S(2)}) collective-permute-start(bf16[1,4,32,512]{3,2,1,0:T(8,128)(2,1)S(1)} %get-tuple-element.91), channel_id=1, source_target_pairs={{0,6},{2,0},{4,2},{6,4},{1,7},{3,1},{5,3},{7,5},{8,14},{10,8},{12,... | collective-permute-start | bytes 393224 | tf_op jit(solution)/shard_map/ppermute | solution.py:203
  219.8 16.8 %collective-permute-start.10 = (bf16[1,4,32,512]{3,2,1,0:T(8,128)(2,1)S(1)}, bf16[1,4,32,512]{3,2,1,0:T(8,128)(2,1)S(1)}, u32[]{:S(2)}, u32[]{:S(2)}) collective-permute-start(bf16[1,4,32,512]{3,2,1,0:T(8,128)(2,1)S(1)} %get-tuple-element.76), channel_id=1, source_target_pairs={{0,4},{2,6},{4,0},{6,2},{1,5},{3,7},{5,1},{7,3},{8,12},{10,14},{12... | collective-permute-start | bytes 393224 | tf_op jit(solution)/shard_map/ppermute | solution.py:203
  (17 other events, 226.2 us)

commit v3 on v2

--- a/solution.py
+++ b/solution.py
@@ -53,8 +53,9 @@
     )(projected, projected, projected)
 
 
-def pack_kernel(n, me_ref, *refs):
-    for x, y in zip(refs[: n - 1], refs[n - 1 :]):
+def pack_kernel(me_ref, *refs):
+    count = len(refs) // 2
+    for x, y in zip(refs[:count], refs[count:]):
         y[...] = x[...]
 
 
@@ -70,7 +71,7 @@
 
     shape = (3, clips, frames, rows, cols)
     return pl.pallas_call(
-        functools.partial(pack_kernel, n),
+        pack_kernel,
         grid_spec=pltpu.PrefetchScalarGridSpec(
             num_scalar_prefetch=1,
             grid=(3, clips),
@@ -81,11 +82,11 @@
         compiler_params=params(),
         cost_estimate=pl.CostEstimate(
             flops=0,
-            bytes_accessed=12 * (n - 1) * clips * frames * rows * cols,
+            bytes_accessed=12 * len(shifts) * clips * frames * rows * cols,
             transcendentals=0,
         ),
         name="pack",
-    )(me, *([projected] * (n - 1)))
+    )(me, *([projected] * len(shifts)))
 
 
 def temporal_kernel(n, me_ref, bias_ref, action_ref, *refs):
@@ -189,12 +190,24 @@
     return lax.optimization_barrier((x, *others))[0]
 
 
+def chunk_sizes(heads):
+    least, most = max(1, heads // (2 * CHUNKS)), max(1, heads // CHUNKS)
+    sizes, at = [], 0
+    while at < heads:
+        limit = max(least, min(most, (heads - at) // 2)) if at >= most else least
+        limit = min(limit, heads - at)
+        sizes.append(max(c for c in range(1, limit + 1) if at % c == 0))
+        at += sizes[-1]
+    return sizes
+
+
 def local(n, projected, codes, action_weight, clip_ids, frame_map, segments):
     _, clips, frames, patches, width = projected.shape
     slots = frame_map.shape[0]
     heads = width // E
-    chunks = max(c for c in range(1, CHUNKS + 1) if heads % c == 0)
-    cols = width // chunks
+    sizes = chunk_sizes(heads)
+    chunks = len(sizes)
+    starts = [sum(sizes[:j]) for j in range(chunks)]
     me_scalar = lax.axis_index("frame")
     me = me_scalar.astype(jnp.int32)[None]
     far_first = sorted(range(1, n), key=lambda d: abs(d - n // 2))
@@ -203,7 +216,12 @@
         return lax.ppermute(x, "frame", [(i, (i + d) % n) for i in range(n)])
 
     def forward(j, *others):
-        packed = pack(projected, me, n, far_first, j, cols)
+        cols = sizes[j] * E
+        at = starts[j] // sizes[j]
+        if j == 0:
+            packed = [pack(projected, me, n, [d], at, cols)[0] for d in far_first]
+        else:
+            packed = pack(projected, me, n, far_first, at, cols)
         if others:
             packed = lax.optimization_barrier((*packed, *others))[: n - 1]
         got = {d: send(x, d) for d, x in zip(far_first, packed)}
@@ -235,17 +253,21 @@
     )
     action = jnp.einsum("csa,ad->csd", codes_slot, action_weight, precision=HIGHEST)
 
+    spatial = []
     mixed = None
     for j in range(chunks):
-        spatial = spatial_attention(projected, j, cols)
+        cols, at = sizes[j] * E, starts[j] // sizes[j]
+        while len(spatial) < min(j + 2, chunks):
+            i = len(spatial)
+            spatial.append(spatial_attention(projected, starts[i] // sizes[i], sizes[i] * E))
         done = temporal_attention(
-            projected, arrived[j], bias, action, after(me, spatial), n, j, cols
+            projected, arrived[j], bias, action, after(me, *spatial), n, at, cols
         )
         back = {d: send(done[d], -d) for d in far_first}
         if j + AHEAD < chunks:
             arrived.append(forward(j + AHEAD, done[1]))
         parts = [done[0]] + [back[d] for d in range(1, n)]
-        mixed = combine(mixed, spatial, parts, me, n, j, width)
+        mixed = combine(mixed, spatial[j], parts, me, n, at, width)
     return mixed
 
 

time: 238 us -> 259 us (1.088)
  Pallas kernels: 68.1 us -> 81.8 us
  starting transfers between devices: 111 us -> 118 us
    ppermute x30 -> x42, starting transfers between devices: 111 us -> 118 us  [send(): return lax.ppermute(x, 'frame', [(i, (i + d) % n) for i in range(n)])]
    pallas_call x5 -> x7, Pallas kernels: 16.6 us -> 21.5 us  [temporal_attention(): pl.pallas_call(functools.partial(temporal_kernel, n), grid_spec=pltpu.Pre...]
    pallas_call x5 -> x9, Pallas kernels: 12.9 us -> 17.5 us  [pack(): pl.pallas_call(pack_kernel, grid_spec=pltpu.PrefetchScalarGridSpec(num_sc...]
    pallas_call x5 -> x7, Pallas kernels: 33.9 us -> 37 us  [spatial_attention(): pl.pallas_call(spatial_kernel, grid=(clips, frames), in_specs=[spec(0), s...]
    pallas_call x5 -> x7, Pallas kernels: 4.59 us -> 5.8 us  [combine(): pl.pallas_call(functools.partial(combine_kernel, n), grid_spec=pltpu.Pref...]
    ppermute x30 -> x42, waiting for transfers between devices: 50.5 us -> 50 us  [send(): return lax.ppermute(x, 'frame', [(i, (i + d) % n) for i in range(n)])]
  transfers between devices with their start and end apart: 30 -> 42, of which waited for: 7 -> 10; matrix products, arithmetic and copies ran while one was open for 1% -> 1% of each run, Pallas kernels for 27% -> 31%
where the time goes in v3:
time: 259 us; the launch traced here: 258 us
  starting transfers between devices  118 us (46%)
  Pallas kernels  81.8 us (32%)
  waiting for transfers between devices  50 us (19%)
  blocking collectives  5.19 us (2%)
    ppermute x42, starting transfers between devices, send(): return lax.ppermute(x, 'frame', [(i, (i + d) % n) for i in range(n)])  118 us
    ppermute x42, waiting for transfers between devices, send(): return lax.ppermute(x, 'frame', [(i, (i + d) % n) for i in range(n)])  50 us
    pallas_call x7, Pallas kernels, spatial_attention(): pl.pallas_call(spatial_kernel, grid=(clips, frames), in_specs=[spec(0), s...  37 us
    pallas_call x7, Pallas kernels, temporal_attention(): pl.pallas_call(functools.partial(temporal_kernel, n), grid_spec=pltpu.Pre...  21.5 us
    pallas_call x9, Pallas kernels, pack(): pl.pallas_call(pack_kernel, grid_spec=pltpu.PrefetchScalarGridSpec(num_sc...  17.5 us
    pallas_call x7, Pallas kernels, combine(): pl.pallas_call(functools.partial(combine_kernel, n), grid_spec=pltpu.Pref...  5.8 us
    all_gather x1, blocking collectives, local(): all_codes = lax.all_gather(codes, 'dp', axis=0, tiled=True)  5.19 us
  transfers between devices with their start and end apart: 42, of which 10 were waited for; matrix products, arithmetic and copies ran while one was open for 1% of the time, Pallas kernels for 31%

profile of v3, /device:TPU:0, one launch (start us, length us, event | category | flops | bytes accessed | tf_op | source)
XLA Modules:
  0.0 257.7 jit_solution(12863684271524785002)
XLA Ops:
  16.3 5.2 %all_gather.3 = f32[4,16,32]{2,1,0:T(8,128)S(1)} all-gather(f32[1,16,32]{2,1,0:T(8,128)S(1)} %copy-done.1), channel_id=1, replica_groups=mesh['dp'=4,'frame'=4,'mp'=2] {'dp'}, dimensions={0}, use_global_device_ids=true | all-gather | bytes 10240 | tf_op jit(solution)/shard_map/all_gather | solution.py:247
  24.2 4.2 %spatial.8.spatial_ref = bf16[1,4,128,256]{3,2,1,0:T(8,128)(2,1)S(1)} custom-call(bf16[6,1,4,128,2560]{4,3,2,1,0:T(8,128)(2,1)} %refs_0_.31, bf16[6,1,4,128,2560]{4,3,2,1,0:T(8,128)(2,1)} %refs_0_.31, bf16[6,1,4,128,2560]{4,3,2,1,0:T(8,128)(2,1)} %refs_0_.31), custom_call_target="tpu_custom_call" | custom-call | flops 67108864 | bytes 1048576 | tf_op jit(solution)/shard_map/spatial/pallas_call | solution.py:40
  31.3 4.2 %spatial.9.spatial_ref = bf16[1,4,128,256]{3,2,1,0:T(8,128)(2,1)S(1)} custom-call(bf16[6,1,4,128,2560]{4,3,2,1,0:T(8,128)(2,1)} %refs_0_.31, bf16[6,1,4,128,2560]{4,3,2,1,0:T(8,128)(2,1)} %refs_0_.31, bf16[6,1,4,128,2560]{4,3,2,1,0:T(8,128)(2,1)} %refs_0_.31), custom_call_target="tpu_custom_call" | custom-call | flops 67108864 | bytes 1048576 | tf_op jit(solution)/shard_map/spatial/pallas_call | solution.py:40
  45.9 6.7 %spatial.10.spatial_ref = bf16[1,4,128,512]{3,2,1,0:T(8,128)(2,1)S(1)} custom-call(bf16[6,1,4,128,2560]{4,3,2,1,0:T(8,128)(2,1)} %refs_0_.31, bf16[6,1,4,128,2560]{4,3,2,1,0:T(8,128)(2,1)} %refs_0_.31, bf16[6,1,4,128,2560]{4,3,2,1,0:T(8,128)(2,1)} %refs_0_.31), custom_call_target="tpu_custom_call" | custom-call | flops 134217728 | bytes 2097152 | tf_op jit(solution)/shard_map/spatial/pallas_call | solution.py:40
  55.6 3.8 %collective-permute-start.39 = (bf16[1,4,32,256]{3,2,1,0:T(8,128)(2,1)S(1)}, bf16[1,4,32,256]{3,2,1,0:T(8,128)(2,1)S(1)}, u32[]{:S(2)}, u32[]{:S(2)}) collective-permute-start(bf16[1,4,32,256]{3,2,1,0:T(8,128)(2,1)S(1)} %get-tuple-element.85), channel_id=1, source_target_pairs={{0,6},{2,0},{4,2},{6,4},{1,7},{3,1},{5,3},{7,5},{8,14},{10,8},{12,... | collective-permute-start | bytes 196616 | tf_op jit(solution)/shard_map/ppermute | solution.py:216
  59.4 18.5 %collective-permute-done.39.refs_1_ = bf16[1,4,32,256]{3,2,1,0:T(8,128)(2,1)S(1)} collective-permute-done((bf16[1,4,32,256]{3,2,1,0:T(8,128)(2,1)S(1)}, bf16[1,4,32,256]{3,2,1,0:T(8,128)(2,1)S(1)}, u32[]{:S(2)}, u32[]{:S(2)}) %collective-permute-start.39) | collective-permute-done | bytes 65568 | tf_op jit(solution)/shard_map/ppermute | solution.py:216
  77.9 8.1 %collective-permute-start.40 = (bf16[1,4,32,256]{3,2,1,0:T(8,128)(2,1)S(1)}, bf16[1,4,32,256]{3,2,1,0:T(8,128)(2,1)S(1)}, u32[]{:S(2)}, u32[]{:S(2)}) collective-permute-start(bf16[1,4,32,256]{3,2,1,0:T(8,128)(2,1)S(1)} %get-tuple-element.137), channel_id=1, source_target_pairs={{0,4},{2,6},{4,0},{6,2},{1,5},{3,7},{5,1},{7,3},{8,12},{10,14},{12... | collective-permute-start | bytes 196616 | tf_op jit(solution)/shard_map/ppermute | solution.py:216
  88.2 3.9 %collective-permute-start.41 = (bf16[1,4,32,256]{3,2,1,0:T(8,128)(2,1)S(1)}, bf16[1,4,32,256]{3,2,1,0:T(8,128)(2,1)S(1)}, u32[]{:S(2)}, u32[]{:S(2)}) collective-permute-start(bf16[1,4,32,256]{3,2,1,0:T(8,128)(2,1)S(1)} %get-tuple-element.138), channel_id=1, source_target_pairs={{0,2},{2,4},{4,6},{6,0},{1,3},{3,5},{5,7},{7,1},{8,10},{10,12},{12... | collective-permute-start | bytes 196616 | tf_op jit(solution)/shard_map/ppermute | solution.py:216
  101.6 6.7 %spatial.11.spatial_ref = bf16[1,4,128,512]{3,2,1,0:T(8,128)(2,1)S(1)} custom-call(bf16[6,1,4,128,2560]{4,3,2,1,0:T(8,128)(2,1)} %refs_0_.31, bf16[6,1,4,128,2560]{4,3,2,1,0:T(8,128)(2,1)} %refs_0_.31, bf16[6,1,4,128,2560]{4,3,2,1,0:T(8,128)(2,1)} %refs_0_.31), custom_call_target="tpu_custom_call" | custom-call | flops 134217728 | bytes 2097152 | tf_op jit(solution)/shard_map/spatial/pallas_call | solution.py:40
  111.7 3.4 %collective-permute-done.36.refs_1_ = bf16[1,4,32,256]{3,2,1,0:T(8,128)(2,1)S(1)} collective-permute-done((bf16[1,4,32,256]{3,2,1,0:T(8,128)(2,1)S(1)}, bf16[1,4,32,256]{3,2,1,0:T(8,128)(2,1)S(1)}, u32[]{:S(2)}, u32[]{:S(2)}) %collective-permute-start.36) | collective-permute-done | bytes 65568 | tf_op jit(solution)/shard_map/ppermute | solution.py:216
  115.1 18.9 %collective-permute-start.6 = (bf16[3,1,4,32,512]{4,3,2,1,0:T(8,128)(2,1)S(1)}, bf16[3,1,4,32,512]{4,3,2,1,0:T(8,128)(2,1)S(1)}, u32[]{:S(2)}, u32[]{:S(2)}) collective-permute-start(bf16[3,1,4,32,512]{4,3,2,1,0:T(8,128)(2,1)S(1)} %get-tuple-element.90), channel_id=1, source_target_pairs={{0,2},{2,4},{4,6},{6,0},{1,3},{3,5},{5,7},{7,1},{8,10},{10,12},{12... | collective-permute-start | bytes 1179656 | tf_op jit(solution)/shard_map/ppermute | solution.py:216
  141.1 6.7 %spatial.12.spatial_ref = bf16[1,4,128,512]{3,2,1,0:T(8,128)(2,1)S(1)} custom-call(bf16[6,1,4,128,2560]{4,3,2,1,0:T(8,128)(2,1)} %refs_0_.31, bf16[6,1,4,128,2560]{4,3,2,1,0:T(8,128)(2,1)} %refs_0_.31, bf16[6,1,4,128,2560]{4,3,2,1,0:T(8,128)(2,1)} %refs_0_.31), custom_call_target="tpu_custom_call" | custom-call | flops 134217728 | bytes 2097152 | tf_op jit(solution)/shard_map/spatial/pallas_call | solution.py:40
  147.8 3.3 %temporal.12 = (bf16[1,4,32,512]{3,2,1,0:T(8,128)(2,1)S(1)}, bf16[1,4,32,512]{3,2,1,0:T(8,128)(2,1)S(1)}, bf16[1,4,32,512]{3,2,1,0:T(8,128)(2,1)S(1)}, bf16[1,4,32,512]{3,2,1,0:T(8,128)(2,1)S(1)}) custom-call(s32[1]{0:T(128)} %bitcast.me_ref, f32[1,256,256]{2,1,0:T(8,128)S(1)} %and_select_fusion.bias_ref, ...), custom_call_target="tpu_custom_call" | custom-call | flops 268435456 | bytes 2097152 | tf_op jit(solution)/shard_map/temporal/pallas_call | solution.py:126
  151.2 12.4 %collective-permute-done.38.refs_3_ = bf16[1,4,32,256]{3,2,1,0:T(8,128)(2,1)S(1)} collective-permute-done((bf16[1,4,32,256]{3,2,1,0:T(8,128)(2,1)S(1)}, bf16[1,4,32,256]{3,2,1,0:T(8,128)(2,1)S(1)}, u32[]{:S(2)}, u32[]{:S(2)}) %collective-permute-start.38) | collective-permute-done | bytes 65568 | tf_op jit(solution)/shard_map/ppermute | solution.py:216
  163.6 10.7 %collective-permute-start.34 = (bf16[1,4,32,512]{3,2,1,0:T(8,128)(2,1)S(1)}, bf16[1,4,32,512]{3,2,1,0:T(8,128)(2,1)S(1)}, u32[]{:S(2)}, u32[]{:S(2)}) collective-permute-start(bf16[1,4,32,512]{3,2,1,0:T(8,128)(2,1)S(1)} %get-tuple-element.131), channel_id=1, source_target_pairs={{0,4},{2,6},{4,0},{6,2},{1,5},{3,7},{5,1},{7,3},{8,12},{10,14},{12... | collective-permute-start | bytes 393224 | tf_op jit(solution)/shard_map/ppermute | solution.py:216
  180.7 4.2 %spatial.13.spatial_ref = bf16[1,4,128,256]{3,2,1,0:T(8,128)(2,1)S(1)} custom-call(bf16[6,1,4,128,2560]{4,3,2,1,0:T(8,128)(2,1)} %refs_0_.31, bf16[6,1,4,128,2560]{4,3,2,1,0:T(8,128)(2,1)} %refs_0_.31, bf16[6,1,4,128,2560]{4,3,2,1,0:T(8,128)(2,1)} %refs_0_.31), custom_call_target="tpu_custom_call" | custom-call | flops 67108864 | bytes 1048576 | tf_op jit(solution)/shard_map/spatial/pallas_call | solution.py:40
  184.9 3.3 %temporal.9 = (bf16[1,4,32,512]{3,2,1,0:T(8,128)(2,1)S(1)}, bf16[1,4,32,512]{3,2,1,0:T(8,128)(2,1)S(1)}, bf16[1,4,32,512]{3,2,1,0:T(8,128)(2,1)S(1)}, bf16[1,4,32,512]{3,2,1,0:T(8,128)(2,1)S(1)}) custom-call(s32[1]{0:T(128)} %bitcast.me_ref, f32[1,256,256]{2,1,0:T(8,128)S(1)} %and_select_fusion.bias_ref, ...), custom_call_target="tpu_custom_call" | custom-call | flops 268435456 | bytes 2097152 | tf_op jit(solution)/shard_map/temporal/pallas_call | solution.py:126
  192.7 11.4 %collective-permute-start.10 = (bf16[3,1,4,32,256]{4,3,2,1,0:T(8,128)(2,1)S(1)}, bf16[3,1,4,32,256]{4,3,2,1,0:T(8,128)(2,1)S(1)}, u32[]{:S(2)}, u32[]{:S(2)}) collective-permute-start(bf16[3,1,4,32,256]{4,3,2,1,0:T(8,128)(2,1)S(1)} %get-tuple-element.95), channel_id=1, source_target_pairs={{0,4},{2,6},{4,0},{6,2},{1,5},{3,7},{5,1},{7,3},{8,12},{10,14},{12... | collective-permute-start | bytes 589832 | tf_op jit(solution)/shard_map/ppermute | solution.py:216
  204.1 3.7 %collective-permute-start.11 = (bf16[3,1,4,32,256]{4,3,2,1,0:T(8,128)(2,1)S(1)}, bf16[3,1,4,32,256]{4,3,2,1,0:T(8,128)(2,1)S(1)}, u32[]{:S(2)}, u32[]{:S(2)}) collective-permute-start(bf16[3,1,4,32,256]{4,3,2,1,0:T(8,128)(2,1)S(1)} %get-tuple-element.96), channel_id=1, source_target_pairs={{0,6},{2,0},{4,2},{6,4},{1,7},{3,1},{5,3},{7,5},{8,14},{10,8},{12,... | collective-permute-start | bytes 589832 | tf_op jit(solution)/shard_map/ppermute | solution.py:216
  207.8 7.7 %collective-permute-start.32 = (bf16[1,4,32,512]{3,2,1,0:T(8,128)(2,1)S(1)}, bf16[1,4,32,512]{3,2,1,0:T(8,128)(2,1)S(1)}, u32[]{:S(2)}, u32[]{:S(2)}) collective-permute-start(bf16[1,4,32,512]{3,2,1,0:T(8,128)(2,1)S(1)} %get-tuple-element.129), channel_id=1, source_target_pairs={{0,2},{2,4},{4,6},{6,0},{1,3},{3,5},{5,7},{7,1},{8,10},{10,12},{12... | collective-permute-start | bytes 393224 | tf_op jit(solution)/shard_map/ppermute | solution.py:216
  218.4 7.7 %collective-permute-done.10.refs_2_ = bf16[3,1,4,32,256]{4,3,2,1,0:T(8,128)(2,1)S(1)} collective-permute-done((bf16[3,1,4,32,256]{4,3,2,1,0:T(8,128)(2,1)S(1)}, bf16[3,1,4,32,256]{4,3,2,1,0:T(8,128)(2,1)S(1)}, u32[]{:S(2)}, u32[]{:S(2)}) %collective-permute-start.10) | collective-permute-done | bytes 196640 | tf_op jit(solution)/shard_map/ppermute | solution.py:216
  226.1 8.2 %collective-permute-start.29 = (bf16[1,4,32,512]{3,2,1,0:T(8,128)(2,1)S(1)}, bf16[1,4,32,512]{3,2,1,0:T(8,128)(2,1)S(1)}, u32[]{:S(2)}, u32[]{:S(2)}) collective-permute-start(bf16[1,4,32,512]{3,2,1,0:T(8,128)(2,1)S(1)} %get-tuple-element.126), channel_id=1, source_target_pairs={{0,2},{2,4},{4,6},{6,0},{1,3},{3,5},{5,7},{7,1},{8,10},{10,12},{12... | collective-permute-start | bytes 393224 | tf_op jit(solution)/shard_map/ppermute | solution.py:216
  234.3 4.2 %spatial.7.spatial_ref = bf16[1,4,128,256]{3,2,1,0:T(8,128)(2,1)S(1)} custom-call(bf16[6,1,4,128,2560]{4,3,2,1,0:T(8,128)(2,1)} %refs_0_.31, bf16[6,1,4,128,2560]{4,3,2,1,0:T(8,128)(2,1)} %refs_0_.31, bf16[6,1,4,128,2560]{4,3,2,1,0:T(8,128)(2,1)} %refs_0_.31), custom_call_target="tpu_custom_call" | custom-call | flops 67108864 | bytes 1048576 | tf_op jit(solution)/shard_map/spatial/pallas_call | solution.py:40
  247.0 3.8 %collective-permute-start.12 = (bf16[1,4,32,256]{3,2,1,0:T(8,128)(2,1)S(1)}, bf16[1,4,32,256]{3,2,1,0:T(8,128)(2,1)S(1)}, u32[]{:S(2)}, u32[]{:S(2)}) collective-permute-start(bf16[1,4,32,256]{3,2,1,0:T(8,128)(2,1)S(1)} %get-tuple-element.98), channel_id=1, source_target_pairs={{0,6},{2,0},{4,2},{6,4},{1,7},{3,1},{5,3},{7,5},{8,14},{10,8},{12,... | collective-permute-start | bytes 196616 | tf_op jit(solution)/shard_map/ppermute | solution.py:216
  (116 shorter events, 86.1 us)
Async XLA Ops:
  1.8 26.6 %collective-permute-start = (bf16[3,1,4,32,256]{4,3,2,1,0:T(8,128)(2,1)S(1)}, bf16[3,1,4,32,256]{4,3,2,1,0:T(8,128)(2,1)S(1)}, u32[]{:S(2)}, u32[]{:S(2)}) collective-permute-start(bf16[3,1,4,32,256]{4,3,2,1,0:T(8,128)(2,1)S(1)} %pack.12), channel_id=1, source_target_pairs={{0,2},{2,4},{4,6},{6,0},{1,3},{3,5},{5,7},{7,1},{8,10},{10,12},{12... | collective-permute-start | bytes 589832 | tf_op jit(solution)/shard_map/ppermute | solution.py:216
  6.5 29.3 %collective-permute-start.1 = (bf16[3,1,4,32,256]{4,3,2,1,0:T(8,128)(2,1)S(1)}, bf16[3,1,4,32,256]{4,3,2,1,0:T(8,128)(2,1)S(1)}, u32[]{:S(2)}, u32[]{:S(2)}) collective-permute-start(bf16[3,1,4,32,256]{4,3,2,1,0:T(8,128)(2,1)S(1)} %pack.13), channel_id=1, source_target_pairs={{0,4},{2,6},{4,0},{6,2},{1,5},{3,7},{5,1},{7,3},{8,12},{10,14},{12... | collective-permute-start | bytes 589832 | tf_op jit(solution)/shard_map/ppermute | solution.py:216
  10.8 25.0 %collective-permute-start.2 = (bf16[3,1,4,32,256]{4,3,2,1,0:T(8,128)(2,1)S(1)}, bf16[3,1,4,32,256]{4,3,2,1,0:T(8,128)(2,1)S(1)}, u32[]{:S(2)}, u32[]{:S(2)}) collective-permute-start(bf16[3,1,4,32,256]{4,3,2,1,0:T(8,128)(2,1)S(1)} %pack.14), channel_id=1, source_target_pairs={{0,6},{2,0},{4,2},{6,4},{1,7},{3,1},{5,3},{7,5},{8,14},{10,8},{12,... | collective-permute-start | bytes 589832 | tf_op jit(solution)/shard_map/ppermute | solution.py:216
  14.1 26.7 %collective-permute-start.15 = (bf16[3,1,4,32,256]{4,3,2,1,0:T(8,128)(2,1)S(1)}, bf16[3,1,4,32,256]{4,3,2,1,0:T(8,128)(2,1)S(1)}, u32[]{:S(2)}, u32[]{:S(2)}) collective-permute-start(bf16[3,1,4,32,256]{4,3,2,1,0:T(8,128)(2,1)S(1)} %get-tuple-element.109), channel_id=1, source_target_pairs={{0,2},{2,4},{4,6},{6,0},{1,3},{3,5},{5,7},{7,1},{8,10},{10,12},{12... | collective-permute-start | bytes 589832 | tf_op jit(solution)/shard_map/ppermute | solution.py:216
  14.9 37.8 %collective-permute-start.16 = (bf16[3,1,4,32,256]{4,3,2,1,0:T(8,128)(2,1)S(1)}, bf16[3,1,4,32,256]{4,3,2,1,0:T(8,128)(2,1)S(1)}, u32[]{:S(2)}, u32[]{:S(2)}) collective-permute-start(bf16[3,1,4,32,256]{4,3,2,1,0:T(8,128)(2,1)S(1)} %get-tuple-element.110), channel_id=1, source_target_pairs={{0,4},{2,6},{4,0},{6,2},{1,5},{3,7},{5,1},{7,3},{8,12},{10,14},{12... | collective-permute-start | bytes 589832 | tf_op jit(solution)/shard_map/ppermute | solution.py:216
  38.6 57.2 %collective-permute-start.3 = (bf16[3,1,4,32,512]{4,3,2,1,0:T(8,128)(2,1)S(1)}, bf16[3,1,4,32,512]{4,3,2,1,0:T(8,128)(2,1)S(1)}, u32[]{:S(2)}, u32[]{:S(2)}) collective-permute-start(bf16[3,1,4,32,512]{4,3,2,1,0:T(8,128)(2,1)S(1)} %get-tuple-element.86), channel_id=1, source_target_pairs={{0,2},{2,4},{4,6},{6,0},{1,3},{3,5},{5,7},{7,1},{8,10},{10,12},{12... | collective-permute-start | bytes 1179656 | tf_op jit(solution)/shard_map/ppermute | solution.py:216
  39.3 59.5 %collective-permute-start.4 = (bf16[3,1,4,32,512]{4,3,2,1,0:T(8,128)(2,1)S(1)}, bf16[3,1,4,32,512]{4,3,2,1,0:T(8,128)(2,1)S(1)}, u32[]{:S(2)}, u32[]{:S(2)}) collective-permute-start(bf16[3,1,4,32,512]{4,3,2,1,0:T(8,128)(2,1)S(1)} %get-tuple-element.87), channel_id=1, source_target_pairs={{0,4},{2,6},{4,0},{6,2},{1,5},{3,7},{5,1},{7,3},{8,12},{10,14},{12... | collective-permute-start | bytes 1179656 | tf_op jit(solution)/shard_map/ppermute | solution.py:216
  40.8 58.6 %collective-permute-start.5 = (bf16[3,1,4,32,512]{4,3,2,1,0:T(8,128)(2,1)S(1)}, bf16[3,1,4,32,512]{4,3,2,1,0:T(8,128)(2,1)S(1)}, u32[]{:S(2)}, u32[]{:S(2)}) collective-permute-start(bf16[3,1,4,32,512]{4,3,2,1,0:T(8,128)(2,1)S(1)} %get-tuple-element.88), channel_id=1, source_target_pairs={{0,6},{2,0},{4,2},{6,4},{1,7},{3,1},{5,3},{7,5},{8,14},{10,8},{12,... | collective-permute-start | bytes 1179656 | tf_op jit(solution)/shard_map/ppermute | solution.py:216
  55.5 79.2 %collective-permute-start.18 = (bf16[3,1,4,32,512]{4,3,2,1,0:T(8,128)(2,1)S(1)}, bf16[3,1,4,32,512]{4,3,2,1,0:T(8,128)(2,1)S(1)}, u32[]{:S(2)}, u32[]{:S(2)}) collective-permute-start(bf16[3,1,4,32,512]{4,3,2,1,0:T(8,128)(2,1)S(1)} %get-tuple-element.113), channel_id=1, source_target_pairs={{0,2},{2,4},{4,6},{6,0},{1,3},{3,5},{5,7},{7,1},{8,10},{10,12},{12... | collective-permute-start | bytes 1179656 | tf_op jit(solution)/shard_map/ppermute | solution.py:216
  95.0 41.4 %collective-permute-start.19 = (bf16[3,1,4,32,512]{4,3,2,1,0:T(8,128)(2,1)S(1)}, bf16[3,1,4,32,512]{4,3,2,1,0:T(8,128)(2,1)S(1)}, u32[]{:S(2)}, u32[]{:S(2)}) collective-permute-start(bf16[3,1,4,32,512]{4,3,2,1,0:T(8,128)(2,1)S(1)} %get-tuple-element.114), channel_id=1, source_target_pairs={{0,4},{2,6},{4,0},{6,2},{1,5},{3,7},{5,1},{7,3},{8,12},{10,14},{12... | collective-permute-start | bytes 1179656 | tf_op jit(solution)/shard_map/ppermute | solution.py:216
  95.9 43.3 %collective-permute-start.20 = (bf16[3,1,4,32,512]{4,3,2,1,0:T(8,128)(2,1)S(1)}, bf16[3,1,4,32,512]{4,3,2,1,0:T(8,128)(2,1)S(1)}, u32[]{:S(2)}, u32[]{:S(2)}) collective-permute-start(bf16[3,1,4,32,512]{4,3,2,1,0:T(8,128)(2,1)S(1)} %get-tuple-element.115), channel_id=1, source_target_pairs={{0,6},{2,0},{4,2},{6,4},{1,7},{3,1},{5,3},{7,5},{8,14},{10,8},{12,... | collective-permute-start | bytes 1179656 | tf_op jit(solution)/shard_map/ppermute | solution.py:216
  99.4 35.4 %collective-permute-start.37 = (bf16[1,4,32,256]{3,2,1,0:T(8,128)(2,1)S(1)}, bf16[1,4,32,256]{3,2,1,0:T(8,128)(2,1)S(1)}, u32[]{:S(2)}, u32[]{:S(2)}) collective-permute-start(bf16[1,4,32,256]{3,2,1,0:T(8,128)(2,1)S(1)} %get-tuple-element.134), channel_id=1, source_target_pairs={{0,4},{2,6},{4,0},{6,2},{1,5},{3,7},{5,1},{7,3},{8,12},{10,14},{12... | collective-permute-start | bytes 196616 | tf_op jit(solution)/shard_map/ppermute | solution.py:216
  115.1 59.2 %collective-permute-start.6 = (bf16[3,1,4,32,512]{4,3,2,1,0:T(8,128)(2,1)S(1)}, bf16[3,1,4,32,512]{4,3,2,1,0:T(8,128)(2,1)S(1)}, u32[]{:S(2)}, u32[]{:S(2)}) collective-permute-start(bf16[3,1,4,32,512]{4,3,2,1,0:T(8,128)(2,1)S(1)} %get-tuple-element.90), channel_id=1, source_target_pairs={{0,2},{2,4},{4,6},{6,0},{1,3},{3,5},{5,7},{7,1},{8,10},{10,12},{12... | collective-permute-start | bytes 1179656 | tf_op jit(solution)/shard_map/ppermute | solution.py:216
  134.7 40.1 %collective-permute-start.7 = (bf16[3,1,4,32,512]{4,3,2,1,0:T(8,128)(2,1)S(1)}, bf16[3,1,4,32,512]{4,3,2,1,0:T(8,128)(2,1)S(1)}, u32[]{:S(2)}, u32[]{:S(2)}) collective-permute-start(bf16[3,1,4,32,512]{4,3,2,1,0:T(8,128)(2,1)S(1)} %get-tuple-element.91), channel_id=1, source_target_pairs={{0,4},{2,6},{4,0},{6,2},{1,5},{3,7},{5,1},{7,3},{8,12},{10,14},{12... | collective-permute-start | bytes 1179656 | tf_op jit(solution)/shard_map/ppermute | solution.py:216
  134.7 43.5 %collective-permute-start.8 = (bf16[3,1,4,32,512]{4,3,2,1,0:T(8,128)(2,1)S(1)}, bf16[3,1,4,32,512]{4,3,2,1,0:T(8,128)(2,1)S(1)}, u32[]{:S(2)}, u32[]{:S(2)}) collective-permute-start(bf16[3,1,4,32,512]{4,3,2,1,0:T(8,128)(2,1)S(1)} %get-tuple-element.92), channel_id=1, source_target_pairs={{0,6},{2,0},{4,2},{6,4},{1,7},{3,1},{5,3},{7,5},{8,14},{10,8},{12,... | collective-permute-start | bytes 1179656 | tf_op jit(solution)/shard_map/ppermute | solution.py:216
  136.4 37.9 %collective-permute-start.33 = (bf16[1,4,32,512]{3,2,1,0:T(8,128)(2,1)S(1)}, bf16[1,4,32,512]{3,2,1,0:T(8,128)(2,1)S(1)}, u32[]{:S(2)}, u32[]{:S(2)}) collective-permute-start(bf16[1,4,32,512]{3,2,1,0:T(8,128)(2,1)S(1)} %get-tuple-element.89), channel_id=1, source_target_pairs={{0,6},{2,0},{4,2},{6,4},{1,7},{3,1},{5,3},{7,5},{8,14},{10,8},{12,... | collective-permute-start | bytes 393224 | tf_op jit(solution)/shard_map/ppermute | solution.py:216
  163.6 25.2 %collective-permute-start.34 = (bf16[1,4,32,512]{3,2,1,0:T(8,128)(2,1)S(1)}, bf16[1,4,32,512]{3,2,1,0:T(8,128)(2,1)S(1)}, u32[]{:S(2)}, u32[]{:S(2)}) collective-permute-start(bf16[1,4,32,512]{3,2,1,0:T(8,128)(2,1)S(1)} %get-tuple-element.131), channel_id=1, source_target_pairs={{0,4},{2,6},{4,0},{6,2},{1,5},{3,7},{5,1},{7,3},{8,12},{10,14},{12... | collective-permute-start | bytes 393224 | tf_op jit(solution)/shard_map/ppermute | solution.py:216
  174.3 33.5 %collective-permute-start.21 = (bf16[3,1,4,32,256]{4,3,2,1,0:T(8,128)(2,1)S(1)}, bf16[3,1,4,32,256]{4,3,2,1,0:T(8,128)(2,1)S(1)}, u32[]{:S(2)}, u32[]{:S(2)}) collective-permute-start(bf16[3,1,4,32,256]{4,3,2,1,0:T(8,128)(2,1)S(1)} %get-tuple-element.117), channel_id=1, source_target_pairs={{0,2},{2,4},{4,6},{6,0},{1,3},{3,5},{5,7},{7,1},{8,10},{10,12},{12... | collective-permute-start | bytes 589832 | tf_op jit(solution)/shard_map/ppermute | solution.py:216
  178.2 25.9 %collective-permute-start.31 = (bf16[1,4,32,512]{3,2,1,0:T(8,128)(2,1)S(1)}, bf16[1,4,32,512]{3,2,1,0:T(8,128)(2,1)S(1)}, u32[]{:S(2)}, u32[]{:S(2)}) collective-permute-start(bf16[1,4,32,512]{3,2,1,0:T(8,128)(2,1)S(1)} %get-tuple-element.128), channel_id=1, source_target_pairs={{0,4},{2,6},{4,0},{6,2},{1,5},{3,7},{5,1},{7,3},{8,12},{10,14},{12... | collective-permute-start | bytes 393224 | tf_op jit(solution)/shard_map/ppermute | solution.py:216
  190.7 24.8 %collective-permute-start.23 = (bf16[3,1,4,32,256]{4,3,2,1,0:T(8,128)(2,1)S(1)}, bf16[3,1,4,32,256]{4,3,2,1,0:T(8,128)(2,1)S(1)}, u32[]{:S(2)}, u32[]{:S(2)}) collective-permute-start(bf16[3,1,4,32,256]{4,3,2,1,0:T(8,128)(2,1)S(1)} %get-tuple-element.119), channel_id=1, source_target_pairs={{0,6},{2,0},{4,2},{6,4},{1,7},{3,1},{5,3},{7,5},{8,14},{10,8},{12,... | collective-permute-start | bytes 589832 | tf_op jit(solution)/shard_map/ppermute | solution.py:216
  192.7 33.4 %collective-permute-start.10 = (bf16[3,1,4,32,256]{4,3,2,1,0:T(8,128)(2,1)S(1)}, bf16[3,1,4,32,256]{4,3,2,1,0:T(8,128)(2,1)S(1)}, u32[]{:S(2)}, u32[]{:S(2)}) collective-permute-start(bf16[3,1,4,32,256]{4,3,2,1,0:T(8,128)(2,1)S(1)} %get-tuple-element.95), channel_id=1, source_target_pairs={{0,4},{2,6},{4,0},{6,2},{1,5},{3,7},{5,1},{7,3},{8,12},{10,14},{12... | collective-permute-start | bytes 589832 | tf_op jit(solution)/shard_map/ppermute | solution.py:216
  207.8 33.6 %collective-permute-start.9 = (bf16[3,1,4,32,256]{4,3,2,1,0:T(8,128)(2,1)S(1)}, bf16[3,1,4,32,256]{4,3,2,1,0:T(8,128)(2,1)S(1)}, u32[]{:S(2)}, u32[]{:S(2)}) collective-permute-start(bf16[3,1,4,32,256]{4,3,2,1,0:T(8,128)(2,1)S(1)} %get-tuple-element.94), channel_id=1, source_target_pairs={{0,2},{2,4},{4,6},{6,0},{1,3},{3,5},{5,7},{7,1},{8,10},{10,12},{12... | collective-permute-start | bytes 589832 | tf_op jit(solution)/shard_map/ppermute | solution.py:216
  207.8 36.6 %collective-permute-start.32 = (bf16[1,4,32,512]{3,2,1,0:T(8,128)(2,1)S(1)}, bf16[1,4,32,512]{3,2,1,0:T(8,128)(2,1)S(1)}, u32[]{:S(2)}, u32[]{:S(2)}) collective-permute-start(bf16[1,4,32,512]{3,2,1,0:T(8,128)(2,1)S(1)} %get-tuple-element.129), channel_id=1, source_target_pairs={{0,2},{2,4},{4,6},{6,0},{1,3},{3,5},{5,7},{7,1},{8,10},{10,12},{12... | collective-permute-start | bytes 393224 | tf_op jit(solution)/shard_map/ppermute | solution.py:216
  215.5 31.5 %collective-permute-start.27 = (bf16[1,4,32,512]{3,2,1,0:T(8,128)(2,1)S(1)}, bf16[1,4,32,512]{3,2,1,0:T(8,128)(2,1)S(1)}, u32[]{:S(2)}, u32[]{:S(2)}) collective-permute-start(bf16[1,4,32,512]{3,2,1,0:T(8,128)(2,1)S(1)} %get-tuple-element.93), channel_id=1, source_target_pairs={{0,6},{2,0},{4,2},{6,4},{1,7},{3,1},{5,3},{7,5},{8,14},{10,8},{12,... | collective-permute-start | bytes 393224 | tf_op jit(solution)/shard_map/ppermute | solution.py:216
  (23 other events, 336.9 us)

commit v4 on v2

--- a/solution.py
+++ b/solution.py
@@ -53,51 +53,63 @@
     )(projected, projected, projected)
 
 
-def pack_kernel(n, me_ref, *refs):
-    for x, y in zip(refs[: n - 1], refs[n - 1 :]):
-        y[...] = x[...]
-
-
-def pack(projected, me, n, shifts, chunk, cols):
+def copy_units(x_ref, which, y_ref, at):
+    heads = x_ref.shape[-1] // E
+    for h in range(heads):
+        y_ref[at + h, 0] = x_ref[which, 0, :, :, h * E : (h + 1) * E]
+
+
+def pack_kernel(me_ref, *refs):
+    count = len(refs) // 2
+    for x, y in zip(refs[:count], refs[count:]):
+        copy_units(x, 0, y, 0)
+
+
+def pack(projected, me, n, shifts, chunk, heads):
     _, clips, frames, patches, _ = projected.shape
     rows = patches // n
-    block = (1, 1, frames, rows, cols)
 
     def spec(d):
         return pl.BlockSpec(
-            block, lambda a, c, me_ref: (a + 3, c, 0, lax.rem(me_ref[0] + d, n), chunk)
+            (1, 1, frames, rows, heads * E),
+            lambda a, c, me_ref: (a + 3, c, 0, lax.rem(me_ref[0] + d, n), chunk),
         )
 
-    shape = (3, clips, frames, rows, cols)
+    out_spec = pl.BlockSpec((heads, 1, frames, rows, E), lambda a, c, me_ref: (a, c, 0, 0, 0))
+    shape = jax.ShapeDtypeStruct((3 * heads, clips, frames, rows, E), jnp.bfloat16)
     return pl.pallas_call(
-        functools.partial(pack_kernel, n),
+        pack_kernel,
         grid_spec=pltpu.PrefetchScalarGridSpec(
             num_scalar_prefetch=1,
             grid=(3, clips),
             in_specs=[spec(d) for d in shifts],
-            out_specs=[pl.BlockSpec(block, lambda a, c, me_ref: (a, c, 0, 0, 0)) for _ in shifts],
-        ),
-        out_shape=[jax.ShapeDtypeStruct(shape, jnp.bfloat16) for _ in shifts],
+            out_specs=[out_spec] * len(shifts),
+        ),
+        out_shape=[shape] * len(shifts),
         compiler_params=params(),
         cost_estimate=pl.CostEstimate(
             flops=0,
-            bytes_accessed=12 * (n - 1) * clips * frames * rows * cols,
+            bytes_accessed=12 * len(shifts) * clips * frames * rows * heads * E,
             transcendentals=0,
         ),
         name="pack",
-    )(me, *([projected] * (n - 1)))
-
-
-def temporal_kernel(n, me_ref, bias_ref, action_ref, *refs):
-    ins, outs = refs[:n], refs[n:]
-    frames, _, cols = ins[0].shape[2:]
+    )(me, *([projected] * len(shifts)))
+
+
+def temporal_kernel(n, heads, skip, later, me_ref, bias_ref, action_ref, own_ref, *refs):
+    arrived, refs = refs[: n - 1], refs[n - 1 :]
+    ahead, refs = (refs[: n - 1], refs[n - 1 :]) if later else ((), refs)
+    own_out, outs = refs[0], refs[1:]
+    frames = own_ref.shape[2]
     slots = n * frames
     bias = bias_ref[0]
-    for h in range(cols // E):
+    for h in range(heads):
         cut = slice(h * E, (h + 1) * E)
 
         def slots_of(which):
-            return jnp.concatenate([x[which, 0, :, :, cut] for x in ins], axis=0)
+            unit = skip + which * heads + h
+            parts = [own_ref[which, 0, :, :, cut]] + [x[unit, 0] for x in arrived]
+            return jnp.concatenate(parts, axis=0)
 
         q = slots_of(0).reshape(slots * GROUP, E)
         k = slots_of(1).reshape(slots * GROUP, E)
@@ -110,58 +122,76 @@
         p = (w * (1.0 / jnp.sum(w, axis=-1, keepdims=True))).astype(jnp.bfloat16)
         o = jnp.dot(p, v, preferred_element_type=jnp.float32).astype(jnp.bfloat16)
         o = o.reshape(n, frames, GROUP, E)
-        for i in range(n):
-            outs[i][0, :, :, cut] = o[i]
-
-
-def temporal_attention(projected, arrived, bias, action, me, n, chunk, cols):
+        own_out[h, 0] = o[0]
+        for e in range(1, n):
+            outs[e - 1][h, 0] = o[n - e]
+    for e in range(1, n if later else 1):
+        for which in range(3):
+            copy_units(ahead[e - 1], which, outs[e - 1], heads + which * later)
+
+
+def temporal_attention(
+    projected, arrived, skip, bias, action, me, n, chunk, heads, later_chunk=0, later=0
+):
     _, clips, frames, patches, _ = projected.shape
     rows = patches // n
     groups = rows // GROUP
     slots = n * frames
-    block = (3, 1, frames, GROUP, cols)
-    own = pl.BlockSpec(block, lambda c, g, me_ref: (1, c, 0, me_ref[0] * groups + g, chunk))
-    other = pl.BlockSpec(block, lambda c, g, me_ref: (0, c, 0, g, 0))
+
+    def rows_of(device, at, count):
+        return pl.BlockSpec(
+            (3, 1, frames, GROUP, count * E),
+            lambda c, g, me_ref: (1, c, 0, lax.rem(me_ref[0] + device, n) * groups + g, at),
+        )
+
+    def units(count):
+        return pl.BlockSpec((count, 1, frames, GROUP, E), lambda c, g, me_ref: (0, c, 0, g, 0))
+
+    out = lambda count: jax.ShapeDtypeStruct((count, clips, frames, rows, E), jnp.bfloat16)
+    sent = heads + 3 * later
+    ahead = range(1, n) if later else ()
     return pl.pallas_call(
-        functools.partial(temporal_kernel, n),
+        functools.partial(temporal_kernel, n, heads, skip, later),
         grid_spec=pltpu.PrefetchScalarGridSpec(
             num_scalar_prefetch=1,
             grid=(clips, groups),
             in_specs=[
                 pl.BlockSpec((1, slots * GROUP, slots * GROUP), lambda c, g, me_ref: (c, 0, 0)),
-                pl.BlockSpec((1, slots, cols), lambda c, g, me_ref: (c, 0, chunk)),
-                own,
+                pl.BlockSpec((1, slots, heads * E), lambda c, g, me_ref: (c, 0, chunk)),
+                rows_of(0, chunk, heads),
             ]
-            + [other] * (n - 1),
-            out_specs=[
-                pl.BlockSpec((1, frames, GROUP, cols), lambda c, g, me_ref: (c, 0, g, 0))
-            ]
-            * n,
-        ),
-        out_shape=[jax.ShapeDtypeStruct((clips, frames, rows, cols), jnp.bfloat16)] * n,
+            + [units(skip + 3 * heads)] * (n - 1)
+            + [rows_of(e, later_chunk, later) for e in ahead],
+            out_specs=[units(heads)] + [units(sent)] * (n - 1),
+        ),
+        out_shape=[out(heads)] + [out(sent)] * (n - 1),
         compiler_params=params(),
         cost_estimate=pl.CostEstimate(
-            flops=4 * clips * groups * (slots * GROUP) ** 2 * cols,
-            bytes_accessed=8 * clips * slots * rows * cols,
-            transcendentals=clips * groups * (slots * GROUP) ** 2 * (cols // E),
+            flops=4 * clips * groups * (slots * GROUP) ** 2 * heads * E,
+            bytes_accessed=16 * clips * slots * rows * heads * E,
+            transcendentals=clips * groups * (slots * GROUP) ** 2 * heads,
         ),
         name="temporal",
-    )(me, bias, action, projected, *arrived)
+    )(me, bias, action, projected, *arrived, *([projected] * len(ahead)))
 
 
 def combine_kernel(n, me_ref, spatial_ref, *refs):
     parts, out_ref = refs[:n], refs[-1]
-    rows = parts[0].shape[2]
-    for d in range(n):
-        at = pl.ds(pl.multiple_of(lax.rem(me_ref[0] + d, n) * rows, rows), rows)
-        total = spatial_ref[0, :, at, :].astype(jnp.float32) + parts[d][0].astype(jnp.float32)
-        out_ref[0, :, at, :] = total.astype(jnp.bfloat16)
+    heads, _, _, rows, _ = parts[0].shape
+    for e in range(n):
+        at = pl.ds(pl.multiple_of(lax.rem(me_ref[0] + n - e, n) * rows, rows), rows)
+        for h in range(heads):
+            cut = slice(h * E, (h + 1) * E)
+            one, other = spatial_ref[0, :, at, cut], parts[e][h, 0]
+            total = one.astype(jnp.float32) + other.astype(jnp.float32)
+            out_ref[0, :, at, cut] = total.astype(jnp.bfloat16)
 
 
 def combine(mixed, spatial, parts, me, n, chunk, width):
     clips, frames, patches, cols = spatial.shape
     rows = patches // n
-    part = pl.BlockSpec((1, frames, rows, cols), lambda c, me_ref: (c, 0, 0, 0))
+    heads = cols // E
+    part = pl.BlockSpec((heads, 1, frames, rows, E), lambda c, me_ref: (0, c, 0, 0, 0))
     before = [] if mixed is None else [mixed]
     return pl.pallas_call(
         functools.partial(combine_kernel, n),
@@ -189,12 +219,18 @@
     return lax.optimization_barrier((x, *others))[0]
 
 
+def chunk_sizes(heads):
+    size = max(c for c in range(1, max(1, heads // CHUNKS) + 1) if heads % c == 0)
+    return [size] * (heads // size)
+
+
 def local(n, projected, codes, action_weight, clip_ids, frame_map, segments):
     _, clips, frames, patches, width = projected.shape
     slots = frame_map.shape[0]
     heads = width // E
-    chunks = max(c for c in range(1, CHUNKS + 1) if heads % c == 0)
-    cols = width // chunks
+    sizes = chunk_sizes(heads)
+    chunks = len(sizes)
+    starts = [sum(sizes[:j]) for j in range(chunks)]
     me_scalar = lax.axis_index("frame")
     me = me_scalar.astype(jnp.int32)[None]
     far_first = sorted(range(1, n), key=lambda d: abs(d - n // 2))
@@ -202,14 +238,17 @@
     def send(x, d):
         return lax.ppermute(x, "frame", [(i, (i + d) % n) for i in range(n)])
 
-    def forward(j, *others):
-        packed = pack(projected, me, n, far_first, j, cols)
-        if others:
-            packed = lax.optimization_barrier((*packed, *others))[: n - 1]
-        got = {d: send(x, d) for d, x in zip(far_first, packed)}
-        return [got[d] for d in range(1, n)]
-
-    arrived = [forward(j) for j in range(min(AHEAD, chunks))]
+    def exchange(outgoing):
+        got = {e: send(outgoing[e - 1], e) for e in far_first}
+        return [got[e] for e in range(1, n)]
+
+    first = {e: pack(projected, me, n, [e], 0, sizes[0])[0] for e in far_first}
+    arrived = [exchange([first[e] for e in range(1, n)])]
+    if chunks > 1:
+        at = starts[1] // sizes[1]
+        arrived.append(exchange(pack(projected, me, n, range(1, n), at, sizes[1])))
+    else:
+        arrived.append(None)
 
     source = lax.rem(me_scalar - jnp.arange(n) + n, n)
     order = (source[:, None] * frames + jnp.arange(frames)[None, :]).reshape(-1)
@@ -235,17 +274,33 @@
     )
     action = jnp.einsum("csa,ad->csd", codes_slot, action_weight, precision=HIGHEST)
 
+    places = [start // size for start, size in zip(starts, sizes)] + [0] * AHEAD
+    sizes = sizes + [0] * AHEAD
+    spatial, own = [], []
+    for j in range(chunks):
+        while len(spatial) < min(j + 2, chunks):
+            i = len(spatial)
+            spatial.append(spatial_attention(projected, places[i], sizes[i] * E))
+        ahead = j + AHEAD
+        done = temporal_attention(
+            projected,
+            arrived[j],
+            sizes[j - AHEAD] if j >= AHEAD else 0,
+            bias,
+            action,
+            after(me, *spatial),
+            n,
+            places[j],
+            sizes[j],
+            places[ahead],
+            sizes[ahead],
+        )
+        own.append(done[0])
+        arrived.append(exchange(done[1:]))
     mixed = None
     for j in range(chunks):
-        spatial = spatial_attention(projected, j, cols)
-        done = temporal_attention(
-            projected, arrived[j], bias, action, after(me, spatial), n, j, cols
-        )
-        back = {d: send(done[d], -d) for d in far_first}
-        if j + AHEAD < chunks:
-            arrived.append(forward(j + AHEAD, done[1]))
-        parts = [done[0]] + [back[d] for d in range(1, n)]
-        mixed = combine(mixed, spatial, parts, me, n, j, width)
+        parts = [own[j]] + arrived[j + AHEAD]
+        mixed = combine(mixed, spatial[j], parts, me, n, places[j], width)
     return mixed
 
 

time: 238 us -> 233 us (0.979)
  starting transfers between devices: 111 us -> 101 us
  waiting for transfers between devices: 50.5 us -> 54.7 us
    ppermute x30 -> x21, starting transfers between devices: 111 us -> 101 us  [send(): return lax.ppermute(x, 'frame', [(i, (i + d) % n) for i in range(n)])]
    ppermute x30 -> x21, waiting for transfers between devices: 50.5 us -> 54.7 us  [send(): return lax.ppermute(x, 'frame', [(i, (i + d) % n) for i in range(n)])]
    pallas_call x10 -> x9, Pallas kernels: 29.5 us -> 28.5 us  [the longest x5 18 us: temporal_attention(): pl.pallas_call(functools.partial(temporal_kernel, n, heads, skip, later),...]
  transfers between devices with their start and end apart: 30 -> 21, of which waited for: 7 -> 6; matrix products, arithmetic and copies ran while one was open for 1% -> 2% of each run, Pallas kernels for 27% -> 28%
where the time goes in v4:
time: 233 us; the launch traced here: 232 us
  starting transfers between devices  101 us (43%)
  Pallas kernels  66.8 us (29%)
  waiting for transfers between devices  54.7 us (23%)
  blocking collectives  5.18 us (2%)
  local copies, waits for them, and re-layouts  2.57 us (1%)
    ppermute x21, starting transfers between devices, send(): return lax.ppermute(x, 'frame', [(i, (i + d) % n) for i in range(n)])  101 us
    ppermute x21, waiting for transfers between devices, send(): return lax.ppermute(x, 'frame', [(i, (i + d) % n) for i in range(n)])  54.7 us
    pallas_call x5, Pallas kernels, spatial_attention(): pl.pallas_call(spatial_kernel, grid=(clips, frames), in_specs=[spec(0), s...  33.7 us
    pallas_call x5, Pallas kernels, temporal_attention(): pl.pallas_call(functools.partial(temporal_kernel, n, heads, skip, later),...  18 us
    pallas_call x4, Pallas kernels, pack(): pl.pallas_call(pack_kernel, grid_spec=pltpu.PrefetchScalarGridSpec(num_sc...  10.5 us
    all_gather x1, blocking collectives, local(): all_codes = lax.all_gather(codes, 'dp', axis=0, tiled=True)  5.18 us
  transfers between devices with their start and end apart: 21, of which 6 were waited for; matrix products, arithmetic and copies ran while one was open for 2% of the time, Pallas kernels for 28%

profile of v4, /device:TPU:0, one launch (start us, length us, event | category | flops | bytes accessed | tf_op | source)
XLA Modules:
  0.0 232.1 jit_solution(901347493677692663)
XLA Ops:
  2.0 3.1 %collective-permute-start = (bf16[12,1,4,32,128]{4,3,2,1,0:T(8,128)(2,1)S(1)}, bf16[12,1,4,32,128]{4,3,2,1,0:T(8,128)(2,1)S(1)}, u32[]{:S(2)}, u32[]{:S(2)}) collective-permute-start(bf16[12,1,4,32,128]{4,3,2,1,0:T(8,128)(2,1)S(1)} %pack.4), channel_id=1, source_target_pairs={{0,2},{2,4},{4,6},{6,0},{1,3},{3,5},{5,7},{7,1},{8,10},{10,12},{12... | collective-permute-start | bytes 1179656 | tf_op jit(solution)/shard_map/ppermute | solution.py:239
  14.3 3.3 %pack.7 = (bf16[12,1,4,32,128]{4,3,2,1,0:T(8,128)(2,1)}, bf16[12,1,4,32,128]{4,3,2,1,0:T(8,128)(2,1)}, bf16[12,1,4,32,128]{4,3,2,1,0:T(8,128)(2,1)}) custom-call(s32[1]{0:T(128)} %bitcast.me_ref, bf16[6,1,4,128,2560]{4,3,2,1,0:T(8,128)(2,1)} %own_ref.9, bf16[6,1,4,128,2560]{4,3,2,1,0:T(8,128)(2,1)} %own_ref.9, bf16[6,1,4,128,2560]{4,3,2,1,0:T(8,128)(2,1)} %own_ref.9), custom_call_target="tpu_custom_call" | custom-call | bytes 2359296 | tf_op jit(solution)/shard_map/pack/pallas_call | solution.py:80
  18.8 5.2 %all_gather.3 = f32[4,16,32]{2,1,0:T(8,128)S(1)} all-gather(f32[1,16,32]{2,1,0:T(8,128)S(1)} %copy-done.1), channel_id=1, replica_groups=mesh['dp'=4,'frame'=4,'mp'=2] {'dp'}, dimensions={0}, use_global_device_ids=true | all-gather | bytes 10240 | tf_op jit(solution)/shard_map/all_gather | solution.py:268
  27.9 6.7 %spatial.6.spatial_ref = bf16[1,4,128,512]{3,2,1,0:T(8,128)(2,1)S(1)} custom-call(bf16[6,1,4,128,2560]{4,3,2,1,0:T(8,128)(2,1)} %own_ref.9, bf16[6,1,4,128,2560]{4,3,2,1,0:T(8,128)(2,1)} %own_ref.9, bf16[6,1,4,128,2560]{4,3,2,1,0:T(8,128)(2,1)} %own_ref.9), custom_call_target="tpu_custom_call" | custom-call | flops 134217728 | bytes 2097152 | tf_op jit(solution)/shard_map/spatial/pallas_call | solution.py:40
  34.7 6.7 %spatial.7.spatial_ref = bf16[1,4,128,512]{3,2,1,0:T(8,128)(2,1)S(1)} custom-call(bf16[6,1,4,128,2560]{4,3,2,1,0:T(8,128)(2,1)} %own_ref.9, bf16[6,1,4,128,2560]{4,3,2,1,0:T(8,128)(2,1)} %own_ref.9, bf16[6,1,4,128,2560]{4,3,2,1,0:T(8,128)(2,1)} %own_ref.9), custom_call_target="tpu_custom_call" | custom-call | flops 134217728 | bytes 2097152 | tf_op jit(solution)/shard_map/spatial/pallas_call | solution.py:40
  44.9 3.8 %temporal.5 = (bf16[4,1,4,32,128]{4,3,2,1,0:T(8,128)(2,1)S(1)}, bf16[16,1,4,32,128]{4,3,2,1,0:T(8,128)(2,1)S(1)}, bf16[16,1,4,32,128]{4,3,2,1,0:T(8,128)(2,1)S(1)}, bf16[16,1,4,32,128]{4,3,2,1,0:T(8,128)(2,1)S(1)}) custom-call(s32[1]{0:T(128)} %bitcast.me_ref, f32[1,256,256]{2,1,0:T(8,128)S(1)} %and_select_fusion.bias_ref, ...), custom_call_target="tpu_custom_call" | custom-call | flops 268435456 | bytes 4194304 | tf_op jit(solution)/shard_map/temporal/pallas_call | solution.py:153
  48.7 15.0 %collective-permute-start.3 = (bf16[16,1,4,32,128]{4,3,2,1,0:T(8,128)(2,1)S(1)}, bf16[16,1,4,32,128]{4,3,2,1,0:T(8,128)(2,1)S(1)}, u32[]{:S(2)}, u32[]{:S(2)}) collective-permute-start(bf16[16,1,4,32,128]{4,3,2,1,0:T(8,128)(2,1)S(1)} %get-tuple-element.35), channel_id=1, source_target_pairs={{0,2},{2,4},{4,6},{6,0},{1,3},{3,5},{5,7},{7,1},{8,10},{10,12},{12... | collective-permute-start | bytes 1572872 | tf_op jit(solution)/shard_map/ppermute | solution.py:239
  63.7 6.7 %spatial.8.spatial_ref = bf16[1,4,128,512]{3,2,1,0:T(8,128)(2,1)S(1)} custom-call(bf16[6,1,4,128,2560]{4,3,2,1,0:T(8,128)(2,1)} %own_ref.9, bf16[6,1,4,128,2560]{4,3,2,1,0:T(8,128)(2,1)} %own_ref.9, bf16[6,1,4,128,2560]{4,3,2,1,0:T(8,128)(2,1)} %own_ref.9), custom_call_target="tpu_custom_call" | custom-call | flops 134217728 | bytes 2097152 | tf_op jit(solution)/shard_map/spatial/pallas_call | solution.py:40
  72.9 16.5 %collective-permute-done.13.refs_1_ = bf16[12,1,4,32,128]{4,3,2,1,0:T(8,128)(2,1)S(1)} collective-permute-done((bf16[12,1,4,32,128]{4,3,2,1,0:T(8,128)(2,1)}, bf16[12,1,4,32,128]{4,3,2,1,0:T(8,128)(2,1)S(1)}, u32[]{:S(2)}, u32[]{:S(2)}) %collective-permute-start.13) | collective-permute-done | bytes 393248 | tf_op jit(solution)/shard_map/ppermute | solution.py:239
  89.3 3.8 %temporal.8 = (bf16[4,1,4,32,128]{4,3,2,1,0:T(8,128)(2,1)S(1)}, bf16[16,1,4,32,128]{4,3,2,1,0:T(8,128)(2,1)S(1)}, bf16[16,1,4,32,128]{4,3,2,1,0:T(8,128)(2,1)S(1)}, bf16[16,1,4,32,128]{4,3,2,1,0:T(8,128)(2,1)S(1)}) custom-call(s32[1]{0:T(128)} %bitcast.me_ref, f32[1,256,256]{2,1,0:T(8,128)S(1)} %and_select_fusion.bias_ref, ...), custom_call_target="tpu_custom_call" | custom-call | flops 268435456 | bytes 4194304 | tf_op jit(solution)/shard_map/temporal/pallas_call | solution.py:153
  93.2 26.0 %collective-permute-start.15 = (bf16[16,1,4,32,128]{4,3,2,1,0:T(8,128)(2,1)S(1)}, bf16[16,1,4,32,128]{4,3,2,1,0:T(8,128)(2,1)S(1)}, u32[]{:S(2)}, u32[]{:S(2)}) collective-permute-start(bf16[16,1,4,32,128]{4,3,2,1,0:T(8,128)(2,1)S(1)} %get-tuple-element.49), channel_id=1, source_target_pairs={{0,2},{2,4},{4,6},{6,0},{1,3},{3,5},{5,7},{7,1},{8,10},{10,12},{12... | collective-permute-start | bytes 1572872 | tf_op jit(solution)/shard_map/ppermute | solution.py:239
  121.6 6.7 %spatial.9.spatial_ref = bf16[1,4,128,512]{3,2,1,0:T(8,128)(2,1)S(1)} custom-call(bf16[6,1,4,128,2560]{4,3,2,1,0:T(8,128)(2,1)} %own_ref.9, bf16[6,1,4,128,2560]{4,3,2,1,0:T(8,128)(2,1)} %own_ref.9, bf16[6,1,4,128,2560]{4,3,2,1,0:T(8,128)(2,1)} %own_ref.9), custom_call_target="tpu_custom_call" | custom-call | flops 134217728 | bytes 2097152 | tf_op jit(solution)/shard_map/spatial/pallas_call | solution.py:40
  128.4 3.1 %collective-permute-done.4.refs_1_.refs_2_ = bf16[16,1,4,32,128]{4,3,2,1,0:T(8,128)(2,1)S(1)} collective-permute-done((bf16[16,1,4,32,128]{4,3,2,1,0:T(8,128)(2,1)S(1)}, bf16[16,1,4,32,128]{4,3,2,1,0:T(8,128)(2,1)S(1)}, u32[]{:S(2)}, u32[]{:S(2)}) %collective-permute-start.4) | collective-permute-done | bytes 524320 | tf_op jit(solution)/shard_map/ppermute | solution.py:239
  131.5 3.8 %temporal.6 = (bf16[4,1,4,32,128]{4,3,2,1,0:T(8,128)(2,1)S(1)}, bf16[16,1,4,32,128]{4,3,2,1,0:T(8,128)(2,1)S(1)}, bf16[16,1,4,32,128]{4,3,2,1,0:T(8,128)(2,1)S(1)}, bf16[16,1,4,32,128]{4,3,2,1,0:T(8,128)(2,1)S(1)}) custom-call(s32[1]{0:T(128)} %bitcast.me_ref, f32[1,256,256]{2,1,0:T(8,128)S(1)} %and_select_fusion.bias_ref, ...), custom_call_target="tpu_custom_call" | custom-call | flops 268435456 | bytes 4194304 | tf_op jit(solution)/shard_map/temporal/pallas_call | solution.py:153
  135.3 11.8 %collective-permute-start.6 = (bf16[16,1,4,32,128]{4,3,2,1,0:T(8,128)(2,1)S(1)}, bf16[16,1,4,32,128]{4,3,2,1,0:T(8,128)(2,1)S(1)}, u32[]{:S(2)}, u32[]{:S(2)}) collective-permute-start(bf16[16,1,4,32,128]{4,3,2,1,0:T(8,128)(2,1)S(1)} %get-tuple-element.38), channel_id=1, source_target_pairs={{0,2},{2,4},{4,6},{6,0},{1,3},{3,5},{5,7},{7,1},{8,10},{10,12},{12... | collective-permute-start | bytes 1572872 | tf_op jit(solution)/shard_map/ppermute | solution.py:239
  149.8 6.7 %spatial.5.spatial_ref = bf16[1,4,128,512]{3,2,1,0:T(8,128)(2,1)S(1)} custom-call(bf16[6,1,4,128,2560]{4,3,2,1,0:T(8,128)(2,1)} %own_ref.9, bf16[6,1,4,128,2560]{4,3,2,1,0:T(8,128)(2,1)} %own_ref.9, bf16[6,1,4,128,2560]{4,3,2,1,0:T(8,128)(2,1)} %own_ref.9), custom_call_target="tpu_custom_call" | custom-call | flops 134217728 | bytes 2097152 | tf_op jit(solution)/shard_map/spatial/pallas_call | solution.py:40
  156.6 19.9 %collective-permute-done.16.refs_1_.refs_2_ = bf16[16,1,4,32,128]{4,3,2,1,0:T(8,128)(2,1)S(1)} collective-permute-done((bf16[16,1,4,32,128]{4,3,2,1,0:T(8,128)(2,1)S(1)}, bf16[16,1,4,32,128]{4,3,2,1,0:T(8,128)(2,1)S(1)}, u32[]{:S(2)}, u32[]{:S(2)}) %collective-permute-start.16) | collective-permute-done | bytes 524320 | tf_op jit(solution)/shard_map/ppermute | solution.py:239
  176.5 3.3 %temporal.9 = (bf16[4,1,4,32,128]{4,3,2,1,0:T(8,128)(2,1)S(1)}, bf16[4,1,4,32,128]{4,3,2,1,0:T(8,128)(2,1)S(1)}, bf16[4,1,4,32,128]{4,3,2,1,0:T(8,128)(2,1)S(1)}, bf16[4,1,4,32,128]{4,3,2,1,0:T(8,128)(2,1)S(1)}) custom-call(s32[1]{0:T(128)} %bitcast.me_ref, f32[1,256,256]{2,1,0:T(8,128)S(1)} %and_select_fusion.bias_ref, ...), custom_call_target="tpu_custom_call" | custom-call | flops 268435456 | bytes 4194304 | tf_op jit(solution)/shard_map/temporal/pallas_call | solution.py:153
  179.8 11.8 %collective-permute-start.18 = (bf16[4,1,4,32,128]{4,3,2,1,0:T(8,128)(2,1)S(1)}, bf16[4,1,4,32,128]{4,3,2,1,0:T(8,128)(2,1)S(1)}, u32[]{:S(2)}, u32[]{:S(2)}) collective-permute-start(bf16[4,1,4,32,128]{4,3,2,1,0:T(8,128)(2,1)S(1)} %get-tuple-element.53), channel_id=1, source_target_pairs={{0,2},{2,4},{4,6},{6,0},{1,3},{3,5},{5,7},{7,1},{8,10},{10,12},{12... | collective-permute-start | bytes 393224 | tf_op jit(solution)/shard_map/ppermute | solution.py:239
  194.4 10.2 %collective-permute-done.7.refs_1_.refs_2_ = bf16[16,1,4,32,128]{4,3,2,1,0:T(8,128)(2,1)S(1)} collective-permute-done((bf16[16,1,4,32,128]{4,3,2,1,0:T(8,128)(2,1)S(1)}, bf16[16,1,4,32,128]{4,3,2,1,0:T(8,128)(2,1)S(1)}, u32[]{:S(2)}, u32[]{:S(2)}) %collective-permute-start.7) | collective-permute-done | bytes 524320 | tf_op jit(solution)/shard_map/ppermute | solution.py:239
  204.6 3.3 %temporal.7 = (bf16[4,1,4,32,128]{4,3,2,1,0:T(8,128)(2,1)S(1)}, bf16[4,1,4,32,128]{4,3,2,1,0:T(8,128)(2,1)S(1)}, bf16[4,1,4,32,128]{4,3,2,1,0:T(8,128)(2,1)S(1)}, bf16[4,1,4,32,128]{4,3,2,1,0:T(8,128)(2,1)S(1)}) custom-call(s32[1]{0:T(128)} %bitcast.me_ref, f32[1,256,256]{2,1,0:T(8,128)S(1)} %and_select_fusion.bias_ref, ...), custom_call_target="tpu_custom_call" | custom-call | flops 268435456 | bytes 4194304 | tf_op jit(solution)/shard_map/temporal/pallas_call | solution.py:153
  207.9 10.8 %collective-permute-start.10 = (bf16[4,1,4,32,128]{4,3,2,1,0:T(8,128)(2,1)S(1)}, bf16[4,1,4,32,128]{4,3,2,1,0:T(8,128)(2,1)S(1)}, u32[]{:S(2)}, u32[]{:S(2)}) collective-permute-start(bf16[4,1,4,32,128]{4,3,2,1,0:T(8,128)(2,1)S(1)} %get-tuple-element.43), channel_id=1, source_target_pairs={{0,4},{2,6},{4,0},{6,2},{1,5},{3,7},{5,1},{7,3},{8,12},{10,14},{12... | collective-permute-start | bytes 393224 | tf_op jit(solution)/shard_map/ppermute | solution.py:239
  218.7 3.4 %collective-permute-start.11 = (bf16[4,1,4,32,128]{4,3,2,1,0:T(8,128)(2,1)S(1)}, bf16[4,1,4,32,128]{4,3,2,1,0:T(8,128)(2,1)S(1)}, u32[]{:S(2)}, u32[]{:S(2)}) collective-permute-start(bf16[4,1,4,32,128]{4,3,2,1,0:T(8,128)(2,1)S(1)} %get-tuple-element.44), channel_id=1, source_target_pairs={{0,6},{2,0},{4,2},{6,4},{1,7},{3,1},{5,3},{7,5},{8,14},{10,8},{12,... | collective-permute-start | bytes 393224 | tf_op jit(solution)/shard_map/ppermute | solution.py:239
  227.1 4.1 %collective-permute-done.9.refs_1_ = bf16[4,1,4,32,128]{4,3,2,1,0:T(8,128)(2,1)S(1)} collective-permute-done((bf16[4,1,4,32,128]{4,3,2,1,0:T(8,128)(2,1)S(1)}, bf16[4,1,4,32,128]{4,3,2,1,0:T(8,128)(2,1)S(1)}, u32[]{:S(2)}, u32[]{:S(2)}) %collective-permute-start.9) | collective-permute-done | bytes 131104 | tf_op jit(solution)/shard_map/ppermute | solution.py:239
  (63 shorter events, 36.0 us)
Async XLA Ops:
  0.0 24.8 %copy-start = (f32[32,2560]{1,0:T(8,128)S(1)}, f32[32,2560]{1,0:T(8,128)}, u32[]{:S(2)}) copy-start(f32[32,2560]{1,0:T(8,128)} %param.8) | copy-start | bytes 983044
  2.0 23.1 %collective-permute-start = (bf16[12,1,4,32,128]{4,3,2,1,0:T(8,128)(2,1)S(1)}, bf16[12,1,4,32,128]{4,3,2,1,0:T(8,128)(2,1)S(1)}, u32[]{:S(2)}, u32[]{:S(2)}) collective-permute-start(bf16[12,1,4,32,128]{4,3,2,1,0:T(8,128)(2,1)S(1)} %pack.4), channel_id=1, source_target_pairs={{0,2},{2,4},{4,6},{6,0},{1,3},{3,5},{5,7},{7,1},{8,10},{10,12},{12... | collective-permute-start | bytes 1179656 | tf_op jit(solution)/shard_map/ppermute | solution.py:239
  7.7 37.2 %collective-permute-start.1 = (bf16[12,1,4,32,128]{4,3,2,1,0:T(8,128)(2,1)}, bf16[12,1,4,32,128]{4,3,2,1,0:T(8,128)(2,1)S(1)}, u32[]{:S(2)}, u32[]{:S(2)}) collective-permute-start(bf16[12,1,4,32,128]{4,3,2,1,0:T(8,128)(2,1)} %pack.5), channel_id=1, source_target_pairs={{0,4},{2,6},{4,0},{6,2},{1,5},{3,7},{5,1},{7,3},{8,12},{10,14},{12... | collective-permute-start | bytes 1179656 | tf_op jit(solution)/shard_map/ppermute | solution.py:239
  12.9 11.2 %copy-start.4 = (s32[1,16]{1,0:T(1,128)S(1)}, s32[1,16]{1,0:T(1,128)}, u32[]{:S(2)}) copy-start(s32[1,16]{1,0:T(1,128)} %param.11) | copy-start | bytes 196
  12.9 11.4 %copy-start.2 = (s32[4]{0:T(128)S(1)}, s32[4]{0:T(128)}, u32[]{:S(2)}) copy-start(s32[4]{0:T(128)} %param.9) | copy-start | bytes 52
  12.9 32.0 %collective-permute-start.2 = (bf16[12,1,4,32,128]{4,3,2,1,0:T(8,128)(2,1)}, bf16[12,1,4,32,128]{4,3,2,1,0:T(8,128)(2,1)S(1)}, u32[]{:S(2)}, u32[]{:S(2)}) collective-permute-start(bf16[12,1,4,32,128]{4,3,2,1,0:T(8,128)(2,1)} %pack.6), channel_id=1, source_target_pairs={{0,6},{2,0},{4,2},{6,4},{1,7},{3,1},{5,3},{7,5},{8,14},{10,8},{12,... | collective-permute-start | bytes 1179656 | tf_op jit(solution)/shard_map/ppermute | solution.py:239
  17.6 54.7 %collective-permute-start.12 = (bf16[12,1,4,32,128]{4,3,2,1,0:T(8,128)(2,1)}, bf16[12,1,4,32,128]{4,3,2,1,0:T(8,128)(2,1)S(1)}, u32[]{:S(2)}, u32[]{:S(2)}) collective-permute-start(bf16[12,1,4,32,128]{4,3,2,1,0:T(8,128)(2,1)} %get-tuple-element.46), channel_id=1, source_target_pairs={{0,2},{2,4},{4,6},{6,0},{1,3},{3,5},{5,7},{7,1},{8,10},{10,12},{12... | collective-permute-start | bytes 1179656 | tf_op jit(solution)/shard_map/ppermute | solution.py:239
  18.3 71.1 %collective-permute-start.13 = (bf16[12,1,4,32,128]{4,3,2,1,0:T(8,128)(2,1)}, bf16[12,1,4,32,128]{4,3,2,1,0:T(8,128)(2,1)S(1)}, u32[]{:S(2)}, u32[]{:S(2)}) collective-permute-start(bf16[12,1,4,32,128]{4,3,2,1,0:T(8,128)(2,1)} %get-tuple-element.47), channel_id=1, source_target_pairs={{0,4},{2,6},{4,0},{6,2},{1,5},{3,7},{5,1},{7,3},{8,12},{10,14},{12... | collective-permute-start | bytes 1179656 | tf_op jit(solution)/shard_map/ppermute | solution.py:239
  25.1 64.3 %collective-permute-start.14 = (bf16[12,1,4,32,128]{4,3,2,1,0:T(8,128)(2,1)}, bf16[12,1,4,32,128]{4,3,2,1,0:T(8,128)(2,1)}, u32[]{:S(2)}, u32[]{:S(2)}) collective-permute-start(bf16[12,1,4,32,128]{4,3,2,1,0:T(8,128)(2,1)} %get-tuple-element.48), channel_id=1, source_target_pairs={{0,6},{2,0},{4,2},{6,4},{1,7},{3,1},{5,3},{7,5},{8,14},{10,8},{12,... | collective-permute-start | bytes 1179656 | tf_op jit(solution)/shard_map/ppermute | solution.py:239
  48.7 70.5 %collective-permute-start.3 = (bf16[16,1,4,32,128]{4,3,2,1,0:T(8,128)(2,1)S(1)}, bf16[16,1,4,32,128]{4,3,2,1,0:T(8,128)(2,1)S(1)}, u32[]{:S(2)}, u32[]{:S(2)}) collective-permute-start(bf16[16,1,4,32,128]{4,3,2,1,0:T(8,128)(2,1)S(1)} %get-tuple-element.35), channel_id=1, source_target_pairs={{0,2},{2,4},{4,6},{6,0},{1,3},{3,5},{5,7},{7,1},{8,10},{10,12},{12... | collective-permute-start | bytes 1572872 | tf_op jit(solution)/shard_map/ppermute | solution.py:239
  70.4 61.1 %collective-permute-start.4 = (bf16[16,1,4,32,128]{4,3,2,1,0:T(8,128)(2,1)S(1)}, bf16[16,1,4,32,128]{4,3,2,1,0:T(8,128)(2,1)S(1)}, u32[]{:S(2)}, u32[]{:S(2)}) collective-permute-start(bf16[16,1,4,32,128]{4,3,2,1,0:T(8,128)(2,1)S(1)} %get-tuple-element.36), channel_id=1, source_target_pairs={{0,4},{2,6},{4,0},{6,2},{1,5},{3,7},{5,1},{7,3},{8,12},{10,14},{12... | collective-permute-start | bytes 1572872 | tf_op jit(solution)/shard_map/ppermute | solution.py:239
  72.3 59.2 %collective-permute-start.5 = (bf16[16,1,4,32,128]{4,3,2,1,0:T(8,128)(2,1)S(1)}, bf16[16,1,4,32,128]{4,3,2,1,0:T(8,128)(2,1)S(1)}, u32[]{:S(2)}, u32[]{:S(2)}) collective-permute-start(bf16[16,1,4,32,128]{4,3,2,1,0:T(8,128)(2,1)S(1)} %get-tuple-element.37), channel_id=1, source_target_pairs={{0,6},{2,0},{4,2},{6,4},{1,7},{3,1},{5,3},{7,5},{8,14},{10,8},{12,... | collective-permute-start | bytes 1572872 | tf_op jit(solution)/shard_map/ppermute | solution.py:239
  93.2 56.6 %collective-permute-start.15 = (bf16[16,1,4,32,128]{4,3,2,1,0:T(8,128)(2,1)S(1)}, bf16[16,1,4,32,128]{4,3,2,1,0:T(8,128)(2,1)S(1)}, u32[]{:S(2)}, u32[]{:S(2)}) collective-permute-start(bf16[16,1,4,32,128]{4,3,2,1,0:T(8,128)(2,1)S(1)} %get-tuple-element.49), channel_id=1, source_target_pairs={{0,2},{2,4},{4,6},{6,0},{1,3},{3,5},{5,7},{7,1},{8,10},{10,12},{12... | collective-permute-start | bytes 1572872 | tf_op jit(solution)/shard_map/ppermute | solution.py:239
  119.2 57.3 %collective-permute-start.16 = (bf16[16,1,4,32,128]{4,3,2,1,0:T(8,128)(2,1)S(1)}, bf16[16,1,4,32,128]{4,3,2,1,0:T(8,128)(2,1)S(1)}, u32[]{:S(2)}, u32[]{:S(2)}) collective-permute-start(bf16[16,1,4,32,128]{4,3,2,1,0:T(8,128)(2,1)S(1)} %get-tuple-element.50), channel_id=1, source_target_pairs={{0,4},{2,6},{4,0},{6,2},{1,5},{3,7},{5,1},{7,3},{8,12},{10,14},{12... | collective-permute-start | bytes 1572872 | tf_op jit(solution)/shard_map/ppermute | solution.py:239
  119.2 57.3 %collective-permute-start.17 = (bf16[16,1,4,32,128]{4,3,2,1,0:T(8,128)(2,1)S(1)}, bf16[16,1,4,32,128]{4,3,2,1,0:T(8,128)(2,1)S(1)}, u32[]{:S(2)}, u32[]{:S(2)}) collective-permute-start(bf16[16,1,4,32,128]{4,3,2,1,0:T(8,128)(2,1)S(1)} %get-tuple-element.51), channel_id=1, source_target_pairs={{0,6},{2,0},{4,2},{6,4},{1,7},{3,1},{5,3},{7,5},{8,14},{10,8},{12,... | collective-permute-start | bytes 1572872 | tf_op jit(solution)/shard_map/ppermute | solution.py:239
  135.3 59.1 %collective-permute-start.6 = (bf16[16,1,4,32,128]{4,3,2,1,0:T(8,128)(2,1)S(1)}, bf16[16,1,4,32,128]{4,3,2,1,0:T(8,128)(2,1)S(1)}, u32[]{:S(2)}, u32[]{:S(2)}) collective-permute-start(bf16[16,1,4,32,128]{4,3,2,1,0:T(8,128)(2,1)S(1)} %get-tuple-element.38), channel_id=1, source_target_pairs={{0,2},{2,4},{4,6},{6,0},{1,3},{3,5},{5,7},{7,1},{8,10},{10,12},{12... | collective-permute-start | bytes 1572872 | tf_op jit(solution)/shard_map/ppermute | solution.py:239
  147.1 57.5 %collective-permute-start.7 = (bf16[16,1,4,32,128]{4,3,2,1,0:T(8,128)(2,1)S(1)}, bf16[16,1,4,32,128]{4,3,2,1,0:T(8,128)(2,1)S(1)}, u32[]{:S(2)}, u32[]{:S(2)}) collective-permute-start(bf16[16,1,4,32,128]{4,3,2,1,0:T(8,128)(2,1)S(1)} %get-tuple-element.39), channel_id=1, source_target_pairs={{0,4},{2,6},{4,0},{6,2},{1,5},{3,7},{5,1},{7,3},{8,12},{10,14},{12... | collective-permute-start | bytes 1572872 | tf_op jit(solution)/shard_map/ppermute | solution.py:239
  149.8 54.7 %collective-permute-start.8 = (bf16[16,1,4,32,128]{4,3,2,1,0:T(8,128)(2,1)S(1)}, bf16[16,1,4,32,128]{4,3,2,1,0:T(8,128)(2,1)S(1)}, u32[]{:S(2)}, u32[]{:S(2)}) collective-permute-start(bf16[16,1,4,32,128]{4,3,2,1,0:T(8,128)(2,1)S(1)} %get-tuple-element.40), channel_id=1, source_target_pairs={{0,6},{2,0},{4,2},{6,4},{1,7},{3,1},{5,3},{7,5},{8,14},{10,8},{12,... | collective-permute-start | bytes 1572872 | tf_op jit(solution)/shard_map/ppermute | solution.py:239
  179.8 42.3 %collective-permute-start.18 = (bf16[4,1,4,32,128]{4,3,2,1,0:T(8,128)(2,1)S(1)}, bf16[4,1,4,32,128]{4,3,2,1,0:T(8,128)(2,1)S(1)}, u32[]{:S(2)}, u32[]{:S(2)}) collective-permute-start(bf16[4,1,4,32,128]{4,3,2,1,0:T(8,128)(2,1)S(1)} %get-tuple-element.53), channel_id=1, source_target_pairs={{0,2},{2,4},{4,6},{6,0},{1,3},{3,5},{5,7},{7,1},{8,10},{10,12},{12... | collective-permute-start | bytes 393224 | tf_op jit(solution)/shard_map/ppermute | solution.py:239
  191.6 33.6 %collective-permute-start.19 = (bf16[4,1,4,32,128]{4,3,2,1,0:T(8,128)(2,1)S(1)}, bf16[4,1,4,32,128]{4,3,2,1,0:T(8,128)(2,1)S(1)}, u32[]{:S(2)}, u32[]{:S(2)}) collective-permute-start(bf16[4,1,4,32,128]{4,3,2,1,0:T(8,128)(2,1)S(1)} %get-tuple-element.54), channel_id=1, source_target_pairs={{0,4},{2,6},{4,0},{6,2},{1,5},{3,7},{5,1},{7,3},{8,12},{10,14},{12... | collective-permute-start | bytes 393224 | tf_op jit(solution)/shard_map/ppermute | solution.py:239
  194.4 30.9 %collective-permute-start.20 = (bf16[4,1,4,32,128]{4,3,2,1,0:T(8,128)(2,1)S(1)}, bf16[4,1,4,32,128]{4,3,2,1,0:T(8,128)(2,1)S(1)}, u32[]{:S(2)}, u32[]{:S(2)}) collective-permute-start(bf16[4,1,4,32,128]{4,3,2,1,0:T(8,128)(2,1)S(1)} %get-tuple-element.55), channel_id=1, source_target_pairs={{0,6},{2,0},{4,2},{6,4},{1,7},{3,1},{5,3},{7,5},{8,14},{10,8},{12,... | collective-permute-start | bytes 393224 | tf_op jit(solution)/shard_map/ppermute | solution.py:239
  207.9 19.2 %collective-permute-start.10 = (bf16[4,1,4,32,128]{4,3,2,1,0:T(8,128)(2,1)S(1)}, bf16[4,1,4,32,128]{4,3,2,1,0:T(8,128)(2,1)S(1)}, u32[]{:S(2)}, u32[]{:S(2)}) collective-permute-start(bf16[4,1,4,32,128]{4,3,2,1,0:T(8,128)(2,1)S(1)} %get-tuple-element.43), channel_id=1, source_target_pairs={{0,4},{2,6},{4,0},{6,2},{1,5},{3,7},{5,1},{7,3},{8,12},{10,14},{12... | collective-permute-start | bytes 393224 | tf_op jit(solution)/shard_map/ppermute | solution.py:239
  218.7 8.4 %collective-permute-start.11 = (bf16[4,1,4,32,128]{4,3,2,1,0:T(8,128)(2,1)S(1)}, bf16[4,1,4,32,128]{4,3,2,1,0:T(8,128)(2,1)S(1)}, u32[]{:S(2)}, u32[]{:S(2)}) collective-permute-start(bf16[4,1,4,32,128]{4,3,2,1,0:T(8,128)(2,1)S(1)} %get-tuple-element.44), channel_id=1, source_target_pairs={{0,6},{2,0},{4,2},{6,4},{1,7},{3,1},{5,3},{7,5},{8,14},{10,8},{12,... | collective-permute-start | bytes 393224 | tf_op jit(solution)/shard_map/ppermute | solution.py:239
  222.1 9.1 %collective-permute-start.9 = (bf16[4,1,4,32,128]{4,3,2,1,0:T(8,128)(2,1)S(1)}, bf16[4,1,4,32,128]{4,3,2,1,0:T(8,128)(2,1)S(1)}, u32[]{:S(2)}, u32[]{:S(2)}) collective-permute-start(bf16[4,1,4,32,128]{4,3,2,1,0:T(8,128)(2,1)S(1)} %get-tuple-element.42), channel_id=1, source_target_pairs={{0,2},{2,4},{4,6},{6,0},{1,3},{3,5},{5,7},{7,1},{8,10},{10,12},{12... | collective-permute-start | bytes 393224 | tf_op jit(solution)/shard_map/ppermute | solution.py:239
  (2 other events, 17.0 us)

commit v5 on v2

v5 whole, which is shorter than its diff:
```python
import functools
import math

import jax
import jax.numpy as jnp
from jax import lax
from jax.experimental import pallas as pl
from jax.experimental.pallas import tpu as pltpu
from jax.sharding import PartitionSpec as P

E = 128
GROUP = 16
SHARES = (4, 4, 4, 4, 4)
AHEAD = 2
EPISODES = 3
HIGHEST = lax.Precision.HIGHEST
VMEM = 48 * 1024 * 1024


def params():
    return pltpu.CompilerParams(vmem_limit_bytes=VMEM)


def pieces(start, heads):
    size = math.gcd(start, heads)
    return heads // size, size, start // size


def spatial_kernel(q_ref, k_ref, v_ref, o_ref):
    heads = q_ref.shape[-1] // E
    for h in range(heads):
        cols = slice(h * E, (h + 1) * E)
        q, k, v = q_ref[0, 0, 0, :, cols], k_ref[0, 0, 0, :, cols], v_ref[0, 0, 0, :, cols]
        s = lax.dot_general(q, k, (((1,), (1,)), ((), ())), preferred_element_type=jnp.float32)
        s = s * (1.0 / E**0.5)
        w = jnp.exp(s - jnp.max(s, axis=-1, keepdims=True))
        p = (w * (1.0 / jnp.sum(w, axis=-1, keepdims=True))).astype(jnp.bfloat16)
        o = jnp.dot(p, v, preferred_element_type=jnp.float32)
        o_ref[0, 0, :, cols] = o.astype(jnp.bfloat16)


def spatial_attention(projected, start, heads):
    _, clips, frames, patches, _ = projected.shape
    count, size, first = pieces(start, heads)
    cols = heads * E
    spec = lambda which: pl.BlockSpec(
        (1, 1, 1, patches, size * E), lambda c, f, i: (which, c, f, 0, first + i)
    )
    return pl.pallas_call(
        spatial_kernel,
        grid=(clips, frames, count),
        in_specs=[spec(0), spec(1), spec(2)],
        out_specs=pl.BlockSpec((1, 1, patches, size * E), lambda c, f, i: (c, f, 0, i)),
        out_shape=jax.ShapeDtypeStruct((clips, frames, patches, cols), jnp.bfloat16),
        compiler_params=params(),
        cost_estimate=pl.CostEstimate(
            flops=4 * clips * frames * patches * patches * cols,
            bytes_accessed=8 * clips * frames * patches * cols,
            transcendentals=clips * frames * patches * patches * (cols // E),
        ),
        name="spatial",
    )(projected, projected, projected)


class Plan:
    def __init__(self, n, frames, patches, heads):
        ends = [round(sum(SHARES[: j + 1]) * heads / sum(SHARES)) for j in range(len(SHARES))]
        self.chunks = [(a, b - a) for a, b in zip([0] + ends, ends) if b > a]
        self.n, self.frames = n, frames
        self.groups = patches // n // GROUP
        self.halved = n == 4 and self.groups == 2 and len({c[1] for c in self.chunks}) == 1
        self.slots = n * frames - EPISODES

    def heads(self, j):
        return self.chunks[j][1] if 0 <= j < len(self.chunks) else 0

    def slotted(self, k):
        return self.halved and self.heads(k) > 0 and self.heads(k - AHEAD) > 0

    def parts(self, k, m):
        full = self.groups * self.frames
        sizes = {}
        if self.slotted(k) and m > 1:
            sizes["kv"] = 2 * self.heads(k) * full
            sizes["slots"] = self.heads(k) * self.slots
        else:
            if self.heads(k):
                sizes["qkv"] = 3 * self.heads(k) * full
            if self.heads(k - AHEAD):
                sizes["o"] = self.heads(k - AHEAD) * full
            if m == 1 and self.slotted(k + AHEAD):
                sizes["ql"] = 2 * self.heads(k + AHEAD) * self.frames
            if m == 1 and self.slotted(k - AHEAD):
                sizes["ol"] = 2 * self.heads(k - AHEAD) * self.frames
        at, total = {}, 0
        for name, size in sizes.items():
            at[name] = total
            total += size
        return at, total

    def tile(self, i, g):
        return (i * self.groups + g) * self.frames


def rows_of(g):
    return pl.ds(pl.multiple_of(g * GROUP, GROUP), GROUP)


def head_cols(refs, h):
    size = refs[0].shape[-1] // E
    return refs[h // size], slice(h % size * E, (h % size + 1) * E)


def write_qkv(plan, heads, which, source, out, at):
    for i, a in enumerate(which):
        for h in range(heads):
            x, cut = head_cols(source, h)
            for g in range(plan.groups):
                to = at + plan.tile(i * heads + h, g)
                rows = slice(g * GROUP, (g + 1) * GROUP)
                out[to : to + plan.frames, 0] = x[a, 0, :, rows, cut]


def write_local_queries(plan, heads, parity, sources, out, at):
    for c, source in enumerate(sources):
        for h in range(heads):
            x, cut = head_cols(source, h)
            to = at + (c * heads + h) * plan.frames
            out[to : to + plan.frames, 0] = x[0, 0, :, rows_of(1 - parity), cut]


def pack_kernel(plan, k, m, me_ref, *refs):
    at, _ = plan.parts(k, m)
    count = len(refs) - 1
    blocks = pieces(*plan.chunks[k])[0]
    write_qkv(plan, plan.heads(k), range(3), refs[:blocks], refs[-1], at["qkv"])
    if "ql" in at:
        later = refs[blocks:count]
        half = len(later) // 2
        sources = [later[:half], later[half:]]
        parity = lax.rem(me_ref[0], 2)
        write_local_queries(plan, plan.heads(k + AHEAD), parity, sources, refs[-1], at["ql"])


def peer_rows(plan, chunk, m, arrays, first_array, patches):
    count, size, first = pieces(*chunk)
    return [
        pl.BlockSpec(
            (arrays, 1, plan.frames, patches // plan.n, size * E),
            lambda c, me_ref, *_, i=i: (first_array, c, 0, me_ref[0] ^ m, first + i),
        )
        for i in range(count)
    ]


def tiles(total):
    return pl.BlockSpec((total, 1, GROUP, E), lambda c, *_: (0, c, 0, 0))


def pack(plan, projected, me, k, m):
    _, clips, _, patches, _ = projected.shape
    at, total = plan.parts(k, m)
    specs = peer_rows(plan, plan.chunks[k], m, 3, 1, patches)
    if "ql" in at:
        for peer in (2, 3):
            specs += peer_rows(plan, plan.chunks[k + AHEAD], peer, 1, 3, patches)
    return pl.pallas_call(
        functools.partial(pack_kernel, plan, k, m),
        grid_spec=pltpu.PrefetchScalarGridSpec(
            num_scalar_prefetch=1, grid=(clips,), in_specs=specs, out_specs=tiles(total)
        ),
        out_shape=jax.ShapeDtypeStruct((total, clips, GROUP, E), jnp.bfloat16),
        compiler_params=params(),
        cost_estimate=pl.CostEstimate(
            flops=0, bytes_accessed=4 * total * clips * GROUP * E, transcendentals=0
        ),
        name="pack",
    )(me, *([projected] * len(specs)))


def slot(plan, base, h, i):
    return base + h * plan.slots + jnp.minimum(i, plan.slots - 1)


def temporal_kernel(plan, j, me_ref, rank_ref, alone_ref, kept_ref, *refs):
    n, frames, groups = plan.n, plan.frames, plan.groups
    slots, heads = n * frames, plan.heads(j)
    half = 2 * frames
    c = pl.program_id(0)
    parity = lax.rem(me_ref[0], 2)
    rank = lambda x: rank_ref[c * slots + x]
    alone = lambda x: alone_ref[c * slots + x]
    kept_here, kept_there = kept_ref[c * 2], kept_ref[c * 2 + 1]
    bias_ref, action_ref, refs = refs[0], refs[1], refs[2:]
    bias = bias_ref[0]
    start = plan.chunks[j][0]
    own, refs = refs[: pieces(*plan.chunks[j])[0]], refs[pieces(*plan.chunks[j])[0] :]
    arrived, refs = refs[: n - 1], refs[n - 1 :]
    k = j + AHEAD
    ahead = []
    if plan.heads(k):
        blocks = pieces(*plan.chunks[k])[0]
        for _ in range(1, n):
            ahead.append(refs[:blocks])
            refs = refs[blocks:]
    beyond = []
    if "ql" in plan.parts(k, 1)[0]:
        blocks = pieces(*plan.chunks[k + AHEAD])[0]
        for _ in range(2):
            beyond.append(refs[:blocks])
            refs = refs[blocks:]
    own_out, outs = refs[0], refs[1:]
    came = [plan.parts(j, m)[0] for m in range(1, n)]
    goes = [plan.parts(k, m)[0] for m in range(1, n)]
    slots_in, slots_out = plan.slotted(j), plan.slotted(k)

    for h in range(heads):
        x, cut = head_cols(own, h)
        for r in range(groups):
            g = lax.rem(parity + r, 2) if plan.halved else r
            rows = rows_of(g) if plan.halved else slice(g * GROUP, (g + 1) * GROUP)

            def array(a):
                parts = [x[a, 0, :, rows, cut]]
                for m in range(1, n):
                    at = came[m - 1]
                    if slots_in and m > 1 and a == 0:
                        if m == 2:
                            for y in range(half, slots):
                                to = slot(plan, at["slots"], h, rank(y))
                                parts.append(arrived[1 + r][pl.ds(to, 1), 0])
                        continue
                    i = (a * heads + h) if "qkv" in at else ((a - 1) * heads + h)
                    to = at["qkv" if "qkv" in at else "kv"] + plan.tile(i, g)
                    parts.append(arrived[m - 1][pl.ds(to, frames), 0])
                return jnp.concatenate(parts, axis=0)

            q = array(0).reshape(slots * GROUP, E)
            key = array(1).reshape(slots * GROUP, E)
            action = action_ref[0, :, (start + h) * E : (start + h + 1) * E].reshape(slots, 1, E)
            v = (array(2).astype(jnp.float32) + action).astype(jnp.bfloat16)
            v = v.reshape(slots * GROUP, E)
            s = lax.dot_general(
                q, key, (((1,), (1,)), ((), ())), preferred_element_type=jnp.float32
            )
            s = s * (1.0 / E**0.5) + bias
            w = jnp.exp(s - jnp.max(s, axis=-1, keepdims=True))
            p = (w * (1.0 / jnp.sum(w, axis=-1, keepdims=True))).astype(jnp.bfloat16)
            o = jnp.dot(p, v, preferred_element_type=jnp.float32).astype(jnp.bfloat16)
            o = o.reshape(slots, GROUP, E)
            own_out[pl.ds(plan.tile(h, g), frames), 0] = o[:frames]
            for m in range(1, n):
                if slots_out and m > 1:
                    continue
                to = goes[m - 1]["o"] + plan.tile(h, g)
                outs[m - 1][pl.ds(to, frames), 0] = o[m * frames : (m + 1) * frames]
            if slots_out:
                for y in range(half, slots):

                    @pl.when(alone(y) == 0)
                    def _():
                        to = slot(plan, goes[1]["slots"], h, kept_here + rank(y))
                        outs[1 + r][pl.ds(to, 1), 0] = o[y : y + 1]

    if ahead:
        later = plan.heads(k)
        for m in range(1, n):
            at = goes[m - 1]
            if "qkv" in at:
                write_qkv(plan, later, range(3), ahead[m - 1], outs[m - 1], at["qkv"])
                continue
            write_qkv(plan, later, (1, 2), ahead[m - 1], outs[m - 1], at["kv"])
            for h in range(later):
                x, cut = head_cols(ahead[m - 1], h)
                for y in range(half):
                    local = came[0]["ql"] + ((m ^ 1) - 2) * later * frames + h * frames + y - frames

                    @pl.when(alone(y) == 0)
                    def _():
                        to = slot(plan, at["slots"], h, rank(y))
                        if y < frames:
                            outs[m - 1][pl.ds(to, 1), 0] = x[0, 0, y : y + 1, rows_of(parity), cut]
                        else:
                            outs[m - 1][pl.ds(to, 1), 0] = arrived[0][local : local + 1, 0]

    if beyond:
        write_local_queries(plan, plan.heads(k + AHEAD), parity, beyond, outs[0], goes[0]["ql"])
    if "ol" in goes[0]:
        for i in range(2):
            for h in range(plan.heads(j - AHEAD)):
                for y in range(frames):
                    at = slot(plan, came[1 + i]["slots"], h, kept_there + rank(frames + y))
                    to = goes[0]["ol"] + (i * plan.heads(j - AHEAD) + h) * frames + y
                    outs[0][to : to + 1, 0] = arrived[1 + i][pl.ds(at, 1), 0]


def temporal_attention(plan, projected, arrived, bias, action, me, tables, j):
    _, clips, frames, patches, _ = projected.shape
    n, k, heads = plan.n, j + AHEAD, plan.heads(j)
    slots = n * frames
    own = peer_rows(plan, plan.chunks[j], 0, 3, 1, patches)
    ahead = []
    if plan.heads(k):
        for m in range(1, n):
            ahead += peer_rows(plan, plan.chunks[k], m, 3, 1, patches)
    if "ql" in plan.parts(k, 1)[0]:
        for peer in (2, 3):
            ahead += peer_rows(plan, plan.chunks[k + AHEAD], peer, 1, 3, patches)
    totals = [heads * plan.groups * frames] + [plan.parts(k, m)[1] for m in range(1, n)]
    return pl.pallas_call(
        functools.partial(temporal_kernel, plan, j),
        grid_spec=pltpu.PrefetchScalarGridSpec(
            num_scalar_prefetch=4,
            grid=(clips,),
            in_specs=[
                pl.BlockSpec((1, slots * GROUP, slots * GROUP), lambda c, *_: (c, 0, 0)),
                pl.BlockSpec((1, slots, action.shape[2]), lambda c, *_: (c, 0, 0)),
            ]
            + own
            + [tiles(x.shape[0]) for x in arrived]
            + ahead,
            out_specs=[tiles(total) for total in totals],
        ),
        out_shape=[
            jax.ShapeDtypeStruct((total, clips, GROUP, E), jnp.bfloat16) for total in totals
        ],
        compiler_params=params(),
        cost_estimate=pl.CostEstimate(
            flops=4 * clips * plan.groups * (slots * GROUP) ** 2 * heads * E,
            bytes_accessed=4 * clips * sum(totals) * GROUP * E,
            transcendentals=clips * plan.groups * (slots * GROUP) ** 2 * heads,
        ),
        name="temporal",
    )(
        me,
        *tables,
        bias,
        action,
        *([projected] * len(own)),
        *arrived,
        *([projected] * len(ahead)),
    )


def combine_kernel(plan, j, me_ref, rank_ref, alone_ref, kept_ref, spatial_ref, *refs):
    n, frames, heads = plan.n, plan.frames, plan.heads(j)
    own, back, refs = refs[0], refs[1:n], refs[n:]
    out_ref = refs[-1]
    c = pl.program_id(0)
    me = me_ref[0]
    parity = lax.rem(me, 2)
    slotted = plan.slotted(j + AHEAD)
    came = [plan.parts(j + AHEAD, m)[0] for m in range(1, n)]
    share = plan.groups * GROUP
    kept_there = kept_ref[c * 2 + 1]

    def put(f, h, at, temporal):
        rows = pl.ds(pl.multiple_of(at, GROUP), temporal.shape[0])
        cut = slice(h * E, (h + 1) * E)
        total = spatial_ref[0, f, rows, cut].astype(jnp.float32) + temporal.astype(jnp.float32)
        out_ref[0, f, rows, cut] = total.astype(jnp.bfloat16)

    for h in range(heads):
        for f in range(frames):
            for m in range(n):
                row = (me ^ m) * share
                if slotted and m > 1:
                    to = slot(
                        plan,
                        came[m - 1]["slots"],
                        h,
                        kept_there + rank_ref[c * n * frames + f],
                    )
                    put(f, h, row + parity * GROUP, back[m - 1][pl.ds(to, 1), 0][0])
                    local = plan.parts(j + 2 * AHEAD, 1)[0]["ol"]
                    local += (((m ^ 1) - 2) * heads + h) * frames + f
                    put(f, h, row + (1 - parity) * GROUP, refs[0][local, 0])
                    continue
                x = own if m == 0 else back[m - 1]
                base = 0 if m == 0 else came[m - 1]["o"]
                for g in range(plan.groups):
                    put(f, h, row + g * GROUP, x[base + plan.tile(h, g) + f, 0])
    if slotted:
        blocks = pieces(*plan.chunks[j])[0]
        values, action_ref = refs[1 : 1 + blocks], refs[1 + blocks]
        start = plan.chunks[j][0]
        for f in range(frames):

            @pl.when(alone_ref[c * n * frames + f] == 1)
            def _():
                for h in range(heads):
                    x, cut = head_cols(values, h)
                    action = action_ref[0, f : f + 1, (start + h) * E : (start + h + 1) * E]
                    v = x[0, 0, f, :, cut].astype(jnp.float32) + action
                    put(f, h, 0, v.astype(jnp.bfloat16))


def combine(plan, mixed, spatial, own, back, handed, projected, action, me, tables, j, width):
    clips, frames, patches, cols = spatial.shape
    n = plan.n
    start, heads = plan.chunks[j]
    count, size, first = pieces(start, heads)
    whole = pl.BlockSpec((1, frames, patches, cols), lambda c, *_: (c, 0, 0, 0))
    arrays, specs = [spatial, own, *back], [whole] + [tiles(x.shape[0]) for x in (own, *back)]
    if plan.slotted(j + AHEAD):
        arrays += [handed] + [projected] * count + [action]
        specs += [tiles(handed.shape[0])]
        specs += [
            pl.BlockSpec(
                (1, 1, frames, patches, size * E), lambda c, *_, i=i: (5, c, 0, 0, first + i)
            )
            for i in range(count)
        ]
        specs += [pl.BlockSpec((1, action.shape[1], action.shape[2]), lambda c, *_: (c, 0, 0))]
    if mixed is not None:
        arrays += [mixed]
        specs += [pl.BlockSpec(memory_space=pl.ANY)]
    assert start % heads == 0
    return pl.pallas_call(
        functools.partial(combine_kernel, plan, j),
        grid_spec=pltpu.PrefetchScalarGridSpec(
            num_scalar_prefetch=4,
            grid=(clips,),
            in_specs=specs,
            out_specs=pl.BlockSpec(
                (1, frames, patches, cols), lambda c, *_: (c, 0, 0, start // heads)
            ),
        ),
        out_shape=jax.ShapeDtypeStruct((clips, frames, patches, width), jnp.bfloat16),
        input_output_aliases={} if mixed is None else {3 + len(arrays): 0},
        compiler_params=params(),
        cost_estimate=pl.CostEstimate(
            flops=clips * frames * patches * cols,
            bytes_accessed=6 * clips * frames * patches * cols,
            transcendentals=0,
        ),
        name="combine",
    )(me, *tables, *arrays)


def after(x, *others):
    return lax.optimization_barrier((x, *others))[0]


def local(n, projected, codes, action_weight, clip_ids, frame_map, segments):
    _, clips, frames, patches, width = projected.shape
    slots = frame_map.shape[0]
    plan = Plan(n, frames, patches, width // E)
    count = len(plan.chunks)
    me_scalar = lax.axis_index("frame").astype(jnp.int32)
    me = me_scalar[None]
    order_of_peers = [*range(2, n), 1]

    def send(x, m):
        return lax.ppermute(x, "frame", [(i, i ^ m) for i in range(n)])

    def exchange(outgoing):
        got = {m: send(outgoing[m - 1], m) for m in order_of_peers}
        return [got[m] for m in range(1, n)]

    arrived = []
    for k in range(min(AHEAD, count)):
        packed = {m: pack(plan, projected, me, k, m) for m in order_of_peers}
        arrived.append(exchange([packed[m] for m in range(1, n)]))

    source = me_scalar ^ jnp.arange(n, dtype=jnp.int32)
    order = (source[:, None] * frames + jnp.arange(frames, dtype=jnp.int32)[None, :]).reshape(-1)
    time_of = jnp.sum(
        jnp.where(order[:, None] == jnp.arange(slots)[None, :], frame_map[None, :], 0), axis=-1
    )
    at_time = time_of[:, None] == jnp.arange(slots, dtype=jnp.int32)[None, :]
    seg_slot = jnp.sum(jnp.where(at_time[None], segments[:, None, :], 0), axis=-1)
    allowed = (time_of[None, :] <= time_of[:, None])[None] & (
        seg_slot[:, None, :] == seg_slot[:, :, None]
    )
    row = jnp.arange(slots * GROUP)
    same_patch = (row[:, None] % GROUP) == (row[None, :] % GROUP)
    wide = jnp.repeat(jnp.repeat(allowed, GROUP, axis=1), GROUP, axis=2)
    bias = jnp.where(wide & same_patch[None], 0.0, -1e30).astype(jnp.float32)

    alone = jnp.sum(allowed.astype(jnp.int32), axis=-1) == 1
    half_of = order // (slots // 2)
    before = (half_of[:, None] == half_of[None, :]) & (order[None, :] < order[:, None])
    rank = jnp.sum((before[None] & ~alone[:, None, :]).astype(jnp.int32), axis=-1)
    here = (half_of == half_of[0])[None]
    kept = jnp.stack(
        [jnp.sum((~alone & here).astype(jnp.int32), -1), jnp.sum((~alone & ~here).astype(jnp.int32), -1)],
        axis=-1,
    )
    tables = [rank.reshape(-1), alone.astype(jnp.int32).reshape(-1), kept.reshape(-1)]

    all_codes = lax.all_gather(codes, "dp", axis=0, tiled=True)
    owned = lax.axis_index("dp") * clips + jnp.arange(clips, dtype=jnp.int32)
    select = (clip_ids[:, None] == owned[None, :]).astype(jnp.float32)
    by_clip = jnp.einsum("ic,ifa->cfa", select, all_codes, precision=HIGHEST)
    codes_slot = jnp.einsum(
        "st,cta->csa", at_time.astype(jnp.float32), by_clip, precision=HIGHEST
    )
    action = jnp.einsum("csa,ad->csd", codes_slot, action_weight, precision=HIGHEST)

    spatial, own = [], []
    for j in range(count):
        for early in plan.chunks[len(spatial) : j + 2]:
            spatial.append(spatial_attention(projected, *early))
        done = temporal_attention(
            plan, projected, arrived[j], bias, action, after(me, *spatial), tables, j
        )
        own.append(done[0])
        arrived.append(exchange(done[1:]))
    mixed = None
    for j in range(count):
        handed = arrived[j + 2 * AHEAD][0] if plan.slotted(j + AHEAD) else None
        mixed = combine(
            plan, mixed, spatial[j], own[j], arrived[j + AHEAD], handed, projected, action, me, tables,
            j, width,
        )
    return mixed


def solution(mesh):
    return jax.shard_map(
        functools.partial(local, mesh.shape["frame"]),
        mesh=mesh,
        in_specs=(
            P(None, "dp", "frame", None, "mp"),
            P("dp", None, None),
            P(None, "mp"),
            P(),
            P(),
            P("dp", None),
        ),
        out_specs=P("dp", "frame", None, "mp"),
        check_vma=False,
    )
```

time: 238 us -> 228 us (0.958)
  starting transfers between devices: 111 us -> 46.4 us
  waiting for transfers between devices: 50.5 us -> 88.8 us
  Pallas kernels: 68.1 us -> 82.6 us
  other arithmetic: 0.64 us -> 3.08 us
    ppermute x30 -> x21, starting transfers between devices: 111 us -> 46.4 us  [send(): return lax.ppermute(x, 'frame', [(i, i ^ m) for i in range(n)])]
    ppermute x30 -> x21, waiting for transfers between devices: 50.5 us -> 88.8 us  [send(): return lax.ppermute(x, 'frame', [(i, i ^ m) for i in range(n)])]
    pallas_call x20 -> x21, Pallas kernels: 68.1 us -> 82.6 us  [the longest x5 33.6 us: spatial_attention(): pl.pallas_call(spatial_kernel, grid=(clips, frames, count), in_specs=[spe...]
  transfers between devices with their start and end apart: 30 -> 21, of which waited for: 7 -> 8; matrix products, arithmetic and copies ran while one was open for 1% -> 2% of each run, Pallas kernels for 27% -> 35%
where the time goes in v5:
time: 228 us; the launch traced here: 227 us
  waiting for transfers between devices  88.8 us (39%)
  Pallas kernels  82.6 us (36%)
  starting transfers between devices  46.4 us (20%)
  blocking collectives  5.19 us (2%)
  other arithmetic  3.08 us (1%)
    ppermute x21, waiting for transfers between devices, send(): return lax.ppermute(x, 'frame', [(i, i ^ m) for i in range(n)])  88.8 us
    ppermute x21, starting transfers between devices, send(): return lax.ppermute(x, 'frame', [(i, i ^ m) for i in range(n)])  46.4 us
    pallas_call x5, Pallas kernels, spatial_attention(): pl.pallas_call(spatial_kernel, grid=(clips, frames, count), in_specs=[spe...  33.6 us
    pallas_call x5, Pallas kernels, temporal_attention(): pl.pallas_call(functools.partial(temporal_kernel, plan, j), grid_spec=plt...  29.3 us
    pallas_call x5, Pallas kernels, combine(): pl.pallas_call(functools.partial(combine_kernel, plan, j), grid_spec=pltp...  10.8 us
    pallas_call x6, Pallas kernels, pack(): pl.pallas_call(functools.partial(pack_kernel, plan, k, m), grid_spec=pltp...  8.93 us
    all_gather x1, blocking collectives, local(): all_codes = lax.all_gather(codes, 'dp', axis=0, tiled=True)  5.19 us
  transfers between devices with their start and end apart: 21, of which 8 were waited for; matrix products, arithmetic and copies ran while one was open for 2% of the time, Pallas kernels for 35%

profile of v5, /device:TPU:0, one launch (start us, length us, event | category | flops | bytes accessed | tf_op | source)
XLA Modules:
  0.0 227.4 jit_solution(11952624707531528857)
XLA Ops:
  1.9 4.0 %collective-permute-start.1 = (bf16[96,1,16,128]{3,2,1,0:T(8,128)(2,1)}, bf16[96,1,16,128]{3,2,1,0:T(8,128)(2,1)S(1)}, u32[]{:S(2)}, u32[]{:S(2)}) collective-permute-start(bf16[96,1,16,128]{3,2,1,0:T(8,128)(2,1)} %pack.7), channel_id=1, source_target_pairs={{0,4},{2,6},{4,0},{6,2},{1,5},{3,7},{5,1},{7,3},{8,12},{10,14},{12... | collective-permute-start | bytes 1179656 | tf_op jit(solution)/shard_map/ppermute | solution.py:455
  18.2 5.2 %all_gather.3 = f32[4,16,32]{2,1,0:T(8,128)S(1)} all-gather(f32[1,16,32]{2,1,0:T(8,128)S(1)} %copy-done.1), channel_id=1, replica_groups=mesh['dp'=4,'frame'=4,'mp'=2] {'dp'}, dimensions={0}, use_global_device_ids=true | all-gather | bytes 10240 | tf_op jit(solution)/shard_map/all_gather | solution.py:492
  26.3 6.7 %spatial.7.spatial_ref = bf16[1,4,128,512]{3,2,1,0:T(8,128)(2,1)S(1)} custom-call(bf16[6,1,4,128,2560]{4,3,2,1,0:T(8,128)(2,1)} %refs_5_.5, bf16[6,1,4,128,2560]{4,3,2,1,0:T(8,128)(2,1)} %refs_5_.5, bf16[6,1,4,128,2560]{4,3,2,1,0:T(8,128)(2,1)} %refs_5_.5), custom_call_target="tpu_custom_call" | custom-call | flops 134217728 | bytes 2097152 | tf_op jit(solution)/shard_map/spatial/pallas_call | solution.py:49
  34.5 6.9 %collective-permute-done.1.refs_4_ = bf16[96,1,16,128]{3,2,1,0:T(8,128)(2,1)S(1)} collective-permute-done((bf16[96,1,16,128]{3,2,1,0:T(8,128)(2,1)}, bf16[96,1,16,128]{3,2,1,0:T(8,128)(2,1)S(1)}, u32[]{:S(2)}, u32[]{:S(2)}) %collective-permute-start.1) | collective-permute-done | bytes 393248 | tf_op jit(solution)/shard_map/ppermute | solution.py:455
  41.4 2.8 %collective-permute-start.14 = (bf16[96,1,16,128]{3,2,1,0:T(8,128)(2,1)S(1)}, bf16[96,1,16,128]{3,2,1,0:T(8,128)(2,1)S(1)}, u32[]{:S(2)}, u32[]{:S(2)}) collective-permute-start(bf16[96,1,16,128]{3,2,1,0:T(8,128)(2,1)S(1)} %pack.11), channel_id=1, source_target_pairs={{0,6},{2,4},{4,2},{6,0},{1,7},{3,5},{5,3},{7,1},{8,14},{10,12},{12... | collective-permute-start | bytes 1179656 | tf_op jit(solution)/shard_map/ppermute | solution.py:455
  44.2 6.7 %spatial.6.spatial_ref = bf16[1,4,128,512]{3,2,1,0:T(8,128)(2,1)S(1)} custom-call(bf16[6,1,4,128,2560]{4,3,2,1,0:T(8,128)(2,1)} %refs_5_.5, bf16[6,1,4,128,2560]{4,3,2,1,0:T(8,128)(2,1)} %refs_5_.5, bf16[6,1,4,128,2560]{4,3,2,1,0:T(8,128)(2,1)} %refs_5_.5), custom_call_target="tpu_custom_call" | custom-call | flops 134217728 | bytes 2097152 | tf_op jit(solution)/shard_map/spatial/pallas_call | solution.py:49
  51.0 7.7 %temporal.5 = (bf16[32,1,16,128]{3,2,1,0:T(8,128)(2,1)S(1)}, bf16[160,1,16,128]{3,2,1,0:T(8,128)(2,1)S(1)}, bf16[116,1,16,128]{3,2,1,0:T(8,128)(2,1)S(1)}, bf16[116,1,16,128]{3,2,1,0:T(8,128)(2,1)S(1)}) custom-call(s32[1]{0:T(128)} %bitcast.me_ref, s32[16]{0:T(128)S(1)} %convert_reduce_fusion.rank_ref, s32[16]{0:T(128)S(1)} %get-tuple-element.55.alone_ref, ...), custom_call_target="tpu_custom_call" | custom-call | flops 268435456 | bytes 3473408 | tf_op jit(solution)/shard_map/temporal/pallas_call | solution.py:310
  60.4 6.4 %collective-permute-done.13.refs_4_ = bf16[96,1,16,128]{3,2,1,0:T(8,128)(2,1)S(1)} collective-permute-done((bf16[96,1,16,128]{3,2,1,0:T(8,128)(2,1)}, bf16[96,1,16,128]{3,2,1,0:T(8,128)(2,1)S(1)}, u32[]{:S(2)}, u32[]{:S(2)}) %collective-permute-start.13) | collective-permute-done | bytes 393248 | tf_op jit(solution)/shard_map/ppermute | solution.py:455
  66.7 2.8 %collective-permute-start.5 = (bf16[116,1,16,128]{3,2,1,0:T(8,128)(2,1)S(1)}, bf16[116,1,16,128]{3,2,1,0:T(8,128)(2,1)S(1)}, u32[]{:S(2)}, u32[]{:S(2)}) collective-permute-start(bf16[116,1,16,128]{3,2,1,0:T(8,128)(2,1)S(1)} %get-tuple-element.34), channel_id=1, source_target_pairs={{0,6},{2,4},{4,2},{6,0},{1,7},{3,5},{5,3},{7,1},{8,14},{10,12},{12... | collective-permute-start | bytes 1425416 | tf_op jit(solution)/shard_map/ppermute | solution.py:455
  69.6 6.7 %spatial.8.spatial_ref = bf16[1,4,128,512]{3,2,1,0:T(8,128)(2,1)S(1)} custom-call(bf16[6,1,4,128,2560]{4,3,2,1,0:T(8,128)(2,1)} %refs_5_.5, bf16[6,1,4,128,2560]{4,3,2,1,0:T(8,128)(2,1)} %refs_5_.5, bf16[6,1,4,128,2560]{4,3,2,1,0:T(8,128)(2,1)} %refs_5_.5), custom_call_target="tpu_custom_call" | custom-call | flops 134217728 | bytes 2097152 | tf_op jit(solution)/shard_map/spatial/pallas_call | solution.py:49
  76.3 7.5 %temporal.8 = (bf16[32,1,16,128]{3,2,1,0:T(8,128)(2,1)S(1)}, bf16[128,1,16,128]{3,2,1,0:T(8,128)(2,1)S(1)}, bf16[116,1,16,128]{3,2,1,0:T(8,128)(2,1)S(1)}, bf16[116,1,16,128]{3,2,1,0:T(8,128)(2,1)S(1)}) custom-call(s32[1]{0:T(128)} %bitcast.me_ref, s32[16]{0:T(128)S(1)} %convert_reduce_fusion.rank_ref, s32[16]{0:T(128)S(1)} %get-tuple-element.55.alone_ref, ...), custom_call_target="tpu_custom_call" | custom-call | flops 268435456 | bytes 3211264 | tf_op jit(solution)/shard_map/temporal/pallas_call | solution.py:310
  84.7 6.7 %spatial.9.spatial_ref = bf16[1,4,128,512]{3,2,1,0:T(8,128)(2,1)S(1)} custom-call(bf16[6,1,4,128,2560]{4,3,2,1,0:T(8,128)(2,1)} %refs_5_.5, bf16[6,1,4,128,2560]{4,3,2,1,0:T(8,128)(2,1)} %refs_5_.5, bf16[6,1,4,128,2560]{4,3,2,1,0:T(8,128)(2,1)} %refs_5_.5), custom_call_target="tpu_custom_call" | custom-call | flops 134217728 | bytes 2097152 | tf_op jit(solution)/shard_map/spatial/pallas_call | solution.py:49
  91.4 24.5 %collective-permute-done.4.refs_4_.refs_2_ = bf16[116,1,16,128]{3,2,1,0:T(8,128)(2,1)S(1)} collective-permute-done((bf16[116,1,16,128]{3,2,1,0:T(8,128)(2,1)S(1)}, bf16[116,1,16,128]{3,2,1,0:T(8,128)(2,1)S(1)}, u32[]{:S(2)}, u32[]{:S(2)}) %collective-permute-start.4) | collective-permute-done | bytes 475168 | tf_op jit(solution)/shard_map/ppermute | solution.py:455
  115.9 7.7 %temporal.6 = (bf16[32,1,16,128]{3,2,1,0:T(8,128)(2,1)S(1)}, bf16[160,1,16,128]{3,2,1,0:T(8,128)(2,1)S(1)}, bf16[116,1,16,128]{3,2,1,0:T(8,128)(2,1)S(1)}, bf16[116,1,16,128]{3,2,1,0:T(8,128)(2,1)S(1)}) custom-call(s32[1]{0:T(128)} %bitcast.me_ref, s32[16]{0:T(128)S(1)} %convert_reduce_fusion.rank_ref, s32[16]{0:T(128)S(1)} %get-tuple-element.55.alone_ref, ...), custom_call_target="tpu_custom_call" | custom-call | flops 268435456 | bytes 3473408 | tf_op jit(solution)/shard_map/temporal/pallas_call | solution.py:310
  123.7 10.8 %collective-permute-start.6 = (bf16[160,1,16,128]{3,2,1,0:T(8,128)(2,1)S(1)}, bf16[160,1,16,128]{3,2,1,0:T(8,128)(2,1)S(1)}, u32[]{:S(2)}, u32[]{:S(2)}) collective-permute-start(bf16[160,1,16,128]{3,2,1,0:T(8,128)(2,1)S(1)} %get-tuple-element.35), channel_id=1, source_target_pairs={{0,2},{2,0},{4,6},{6,4},{1,3},{3,1},{5,7},{7,5},{8,10},{10,8},{12,... | collective-permute-start | bytes 1966088 | tf_op jit(solution)/shard_map/ppermute | solution.py:455
  140.8 6.7 %spatial.5.spatial_ref = bf16[1,4,128,512]{3,2,1,0:T(8,128)(2,1)S(1)} custom-call(bf16[6,1,4,128,2560]{4,3,2,1,0:T(8,128)(2,1)} %refs_5_.5, bf16[6,1,4,128,2560]{4,3,2,1,0:T(8,128)(2,1)} %refs_5_.5, bf16[6,1,4,128,2560]{4,3,2,1,0:T(8,128)(2,1)} %refs_5_.5), custom_call_target="tpu_custom_call" | custom-call | flops 134217728 | bytes 2097152 | tf_op jit(solution)/shard_map/spatial/pallas_call | solution.py:49
  147.5 26.9 %collective-permute-done.17.refs_5_.refs_3_ = bf16[116,1,16,128]{3,2,1,0:T(8,128)(2,1)S(1)} collective-permute-done((bf16[116,1,16,128]{3,2,1,0:T(8,128)(2,1)S(1)}, bf16[116,1,16,128]{3,2,1,0:T(8,128)(2,1)S(1)}, u32[]{:S(2)}, u32[]{:S(2)}) %collective-permute-start.17) | collective-permute-done | bytes 475168 | tf_op jit(solution)/shard_map/ppermute | solution.py:455
  174.4 6.7 %collective-permute-done.15.refs_3_.refs_1_ = bf16[128,1,16,128]{3,2,1,0:T(8,128)(2,1)S(1)} collective-permute-done((bf16[128,1,16,128]{3,2,1,0:T(8,128)(2,1)S(1)}, bf16[128,1,16,128]{3,2,1,0:T(8,128)(2,1)S(1)}, u32[]{:S(2)}, u32[]{:S(2)}) %collective-permute-start.15) | collective-permute-done | bytes 524320 | tf_op jit(solution)/shard_map/ppermute | solution.py:455
  181.1 3.1 %temporal.9 = (bf16[32,1,16,128]{3,2,1,0:T(8,128)(2,1)S(1)}, bf16[64,1,16,128]{3,2,1,0:T(8,128)(2,1)S(1)}, bf16[32,1,16,128]{3,2,1,0:T(8,128)(2,1)S(1)}, bf16[32,1,16,128]{3,2,1,0:T(8,128)(2,1)S(1)}) custom-call(s32[1]{0:T(128)} %bitcast.me_ref, s32[16]{0:T(128)S(1)} %convert_reduce_fusion.rank_ref, s32[16]{0:T(128)S(1)} %get-tuple-element.55.alone_ref, ...), custom_call_target="tpu_custom_call" | custom-call | flops 268435456 | bytes 1310720 | tf_op jit(solution)/shard_map/temporal/pallas_call | solution.py:310
  184.3 9.5 %collective-permute-done.8.refs_5_.refs_3_ = bf16[116,1,16,128]{3,2,1,0:T(8,128)(2,1)S(1)} collective-permute-done((bf16[116,1,16,128]{3,2,1,0:T(8,128)(2,1)S(1)}, bf16[116,1,16,128]{3,2,1,0:T(8,128)(2,1)S(1)}, u32[]{:S(2)}, u32[]{:S(2)}) %collective-permute-start.8) | collective-permute-done | bytes 475168 | tf_op jit(solution)/shard_map/ppermute | solution.py:455
  193.8 3.1 %temporal.7 = (bf16[32,1,16,128]{3,2,1,0:T(8,128)(2,1)S(1)}, bf16[64,1,16,128]{3,2,1,0:T(8,128)(2,1)S(1)}, bf16[32,1,16,128]{3,2,1,0:T(8,128)(2,1)S(1)}, bf16[32,1,16,128]{3,2,1,0:T(8,128)(2,1)S(1)}) custom-call(s32[1]{0:T(128)} %bitcast.me_ref, s32[16]{0:T(128)S(1)} %convert_reduce_fusion.rank_ref, s32[16]{0:T(128)S(1)} %get-tuple-element.55.alone_ref, ...), custom_call_target="tpu_custom_call" | custom-call | flops 268435456 | bytes 1310720 | tf_op jit(solution)/shard_map/temporal/pallas_call | solution.py:310
  197.0 6.0 %collective-permute-start.9 = (bf16[64,1,16,128]{3,2,1,0:T(8,128)(2,1)S(1)}, bf16[64,1,16,128]{3,2,1,0:T(8,128)(2,1)S(1)}, u32[]{:S(2)}, u32[]{:S(2)}) collective-permute-start(bf16[64,1,16,128]{3,2,1,0:T(8,128)(2,1)S(1)} %get-tuple-element.39), channel_id=1, source_target_pairs={{0,2},{2,0},{4,6},{6,4},{1,3},{3,1},{5,7},{7,5},{8,10},{10,8},{12,... | collective-permute-start | bytes 786440 | tf_op jit(solution)/shard_map/ppermute | solution.py:455
  216.7 4.9 %collective-permute-done.19.refs_2_ = bf16[32,1,16,128]{3,2,1,0:T(8,128)(2,1)S(1)} collective-permute-done((bf16[32,1,16,128]{3,2,1,0:T(8,128)(2,1)S(1)}, bf16[32,1,16,128]{3,2,1,0:T(8,128)(2,1)S(1)}, u32[]{:S(2)}, u32[]{:S(2)}) %collective-permute-start.19) | collective-permute-done | bytes 131104 | tf_op jit(solution)/shard_map/ppermute | solution.py:455
  223.1 2.9 %collective-permute-done.10.refs_2_ = bf16[32,1,16,128]{3,2,1,0:T(8,128)(2,1)S(1)} collective-permute-done((bf16[32,1,16,128]{3,2,1,0:T(8,128)(2,1)S(1)}, bf16[32,1,16,128]{3,2,1,0:T(8,128)(2,1)S(1)}, u32[]{:S(2)}, u32[]{:S(2)}) %collective-permute-start.10) | collective-permute-done | bytes 131104 | tf_op jit(solution)/shard_map/ppermute | solution.py:455
  (71 shorter events, 43.9 us)
Async XLA Ops:
  0.0 34.2 %copy-start = (f32[32,2560]{1,0:T(8,128)S(1)}, f32[32,2560]{1,0:T(8,128)}, u32[]{:S(2)}) copy-start(f32[32,2560]{1,0:T(8,128)} %param.8) | copy-start | bytes 983044
  1.9 39.6 %collective-permute-start.1 = (bf16[96,1,16,128]{3,2,1,0:T(8,128)(2,1)}, bf16[96,1,16,128]{3,2,1,0:T(8,128)(2,1)S(1)}, u32[]{:S(2)}, u32[]{:S(2)}) collective-permute-start(bf16[96,1,16,128]{3,2,1,0:T(8,128)(2,1)} %pack.7), channel_id=1, source_target_pairs={{0,4},{2,6},{4,0},{6,2},{1,5},{3,7},{5,1},{7,3},{8,12},{10,14},{12... | collective-permute-start | bytes 1179656 | tf_op jit(solution)/shard_map/ppermute | solution.py:455
  7.7 43.2 %collective-permute-start.2 = (bf16[96,1,16,128]{3,2,1,0:T(8,128)(2,1)}, bf16[96,1,16,128]{3,2,1,0:T(8,128)(2,1)}, u32[]{:S(2)}, u32[]{:S(2)}) collective-permute-start(bf16[96,1,16,128]{3,2,1,0:T(8,128)(2,1)} %pack.8), channel_id=1, source_target_pairs={{0,6},{2,4},{4,2},{6,0},{1,7},{3,5},{5,3},{7,1},{8,14},{10,12},{12... | collective-permute-start | bytes 1179656 | tf_op jit(solution)/shard_map/ppermute | solution.py:455
  10.9 55.9 %collective-permute-start.13 = (bf16[96,1,16,128]{3,2,1,0:T(8,128)(2,1)}, bf16[96,1,16,128]{3,2,1,0:T(8,128)(2,1)S(1)}, u32[]{:S(2)}, u32[]{:S(2)}) collective-permute-start(bf16[96,1,16,128]{3,2,1,0:T(8,128)(2,1)} %pack.10), channel_id=1, source_target_pairs={{0,4},{2,6},{4,0},{6,2},{1,5},{3,7},{5,1},{7,3},{8,12},{10,14},{12... | collective-permute-start | bytes 1179656 | tf_op jit(solution)/shard_map/ppermute | solution.py:455
  13.8 4.4 %copy-start.1 = (f32[1,16,32]{2,1,0:T(8,128)S(1)}, f32[1,16,32]{2,1,0:T(8,128)}, u32[]{:S(2)}) copy-start(f32[1,16,32]{2,1,0:T(8,128)} %param.7) | copy-start | bytes 6148
  13.8 9.6 %copy-start.2 = (s32[4]{0:T(128)S(1)}, s32[4]{0:T(128)}, u32[]{:S(2)}) copy-start(s32[4]{0:T(128)} %param.9) | copy-start | bytes 52
  13.8 37.2 %collective-permute-start = (bf16[128,1,16,128]{3,2,1,0:T(8,128)(2,1)S(1)}, bf16[128,1,16,128]{3,2,1,0:T(8,128)(2,1)S(1)}, u32[]{:S(2)}, u32[]{:S(2)}) collective-permute-start(bf16[128,1,16,128]{3,2,1,0:T(8,128)(2,1)S(1)} %pack.6), channel_id=1, source_target_pairs={{0,2},{2,0},{4,6},{6,4},{1,3},{3,1},{5,7},{7,5},{8,10},{10,8},{12,... | collective-permute-start | bytes 1572872 | tf_op jit(solution)/shard_map/ppermute | solution.py:455
  16.4 59.9 %collective-permute-start.12 = (bf16[128,1,16,128]{3,2,1,0:T(8,128)(2,1)S(1)}, bf16[128,1,16,128]{3,2,1,0:T(8,128)(2,1)S(1)}, u32[]{:S(2)}, u32[]{:S(2)}) collective-permute-start(bf16[128,1,16,128]{3,2,1,0:T(8,128)(2,1)S(1)} %pack.9), channel_id=1, source_target_pairs={{0,2},{2,0},{4,6},{6,4},{1,3},{3,1},{5,7},{7,5},{8,10},{10,8},{12,... | collective-permute-start | bytes 1572872 | tf_op jit(solution)/shard_map/ppermute | solution.py:455
  41.4 34.9 %collective-permute-start.14 = (bf16[96,1,16,128]{3,2,1,0:T(8,128)(2,1)S(1)}, bf16[96,1,16,128]{3,2,1,0:T(8,128)(2,1)S(1)}, u32[]{:S(2)}, u32[]{:S(2)}) collective-permute-start(bf16[96,1,16,128]{3,2,1,0:T(8,128)(2,1)S(1)} %pack.11), channel_id=1, source_target_pairs={{0,6},{2,4},{4,2},{6,0},{1,7},{3,5},{5,3},{7,1},{8,14},{10,12},{12... | collective-permute-start | bytes 1179656 | tf_op jit(solution)/shard_map/ppermute | solution.py:455
  58.7 57.2 %collective-permute-start.3 = (bf16[160,1,16,128]{3,2,1,0:T(8,128)(2,1)S(1)}, bf16[160,1,16,128]{3,2,1,0:T(8,128)(2,1)S(1)}, u32[]{:S(2)}, u32[]{:S(2)}) collective-permute-start(bf16[160,1,16,128]{3,2,1,0:T(8,128)(2,1)S(1)} %get-tuple-element.32), channel_id=1, source_target_pairs={{0,2},{2,0},{4,6},{6,4},{1,3},{3,1},{5,7},{7,5},{8,10},{10,8},{12,... | collective-permute-start | bytes 1966088 | tf_op jit(solution)/shard_map/ppermute | solution.py:455
  58.8 57.1 %collective-permute-start.4 = (bf16[116,1,16,128]{3,2,1,0:T(8,128)(2,1)S(1)}, bf16[116,1,16,128]{3,2,1,0:T(8,128)(2,1)S(1)}, u32[]{:S(2)}, u32[]{:S(2)}) collective-permute-start(bf16[116,1,16,128]{3,2,1,0:T(8,128)(2,1)S(1)} %get-tuple-element.33), channel_id=1, source_target_pairs={{0,4},{2,6},{4,0},{6,2},{1,5},{3,7},{5,1},{7,3},{8,12},{10,14},{12... | collective-permute-start | bytes 1425416 | tf_op jit(solution)/shard_map/ppermute | solution.py:455
  66.7 49.2 %collective-permute-start.5 = (bf16[116,1,16,128]{3,2,1,0:T(8,128)(2,1)S(1)}, bf16[116,1,16,128]{3,2,1,0:T(8,128)(2,1)S(1)}, u32[]{:S(2)}, u32[]{:S(2)}) collective-permute-start(bf16[116,1,16,128]{3,2,1,0:T(8,128)(2,1)S(1)} %get-tuple-element.34), channel_id=1, source_target_pairs={{0,6},{2,4},{4,2},{6,0},{1,7},{3,5},{5,3},{7,1},{8,14},{10,12},{12... | collective-permute-start | bytes 1425416 | tf_op jit(solution)/shard_map/ppermute | solution.py:455
  83.8 54.1 %collective-permute-start.16 = (bf16[116,1,16,128]{3,2,1,0:T(8,128)(2,1)S(1)}, bf16[116,1,16,128]{3,2,1,0:T(8,128)(2,1)S(1)}, u32[]{:S(2)}, u32[]{:S(2)}) collective-permute-start(bf16[116,1,16,128]{3,2,1,0:T(8,128)(2,1)S(1)} %get-tuple-element.44), channel_id=1, source_target_pairs={{0,4},{2,6},{4,0},{6,2},{1,5},{3,7},{5,1},{7,3},{8,12},{10,14},{12... | collective-permute-start | bytes 1425416 | tf_op jit(solution)/shard_map/ppermute | solution.py:455
  123.7 70.1 %collective-permute-start.6 = (bf16[160,1,16,128]{3,2,1,0:T(8,128)(2,1)S(1)}, bf16[160,1,16,128]{3,2,1,0:T(8,128)(2,1)S(1)}, u32[]{:S(2)}, u32[]{:S(2)}) collective-permute-start(bf16[160,1,16,128]{3,2,1,0:T(8,128)(2,1)S(1)} %get-tuple-element.35), channel_id=1, source_target_pairs={{0,2},{2,0},{4,6},{6,4},{1,3},{3,1},{5,7},{7,5},{8,10},{10,8},{12,... | collective-permute-start | bytes 1966088 | tf_op jit(solution)/shard_map/ppermute | solution.py:455
  134.5 46.6 %collective-permute-start.15 = (bf16[128,1,16,128]{3,2,1,0:T(8,128)(2,1)S(1)}, bf16[128,1,16,128]{3,2,1,0:T(8,128)(2,1)S(1)}, u32[]{:S(2)}, u32[]{:S(2)}) collective-permute-start(bf16[128,1,16,128]{3,2,1,0:T(8,128)(2,1)S(1)} %get-tuple-element.43), channel_id=1, source_target_pairs={{0,2},{2,0},{4,6},{6,4},{1,3},{3,1},{5,7},{7,5},{8,10},{10,8},{12,... | collective-permute-start | bytes 1572872 | tf_op jit(solution)/shard_map/ppermute | solution.py:455
  134.6 39.8 %collective-permute-start.17 = (bf16[116,1,16,128]{3,2,1,0:T(8,128)(2,1)S(1)}, bf16[116,1,16,128]{3,2,1,0:T(8,128)(2,1)S(1)}, u32[]{:S(2)}, u32[]{:S(2)}) collective-permute-start(bf16[116,1,16,128]{3,2,1,0:T(8,128)(2,1)S(1)} %get-tuple-element.45), channel_id=1, source_target_pairs={{0,6},{2,4},{4,2},{6,0},{1,7},{3,5},{5,3},{7,1},{8,14},{10,12},{12... | collective-permute-start | bytes 1425416 | tf_op jit(solution)/shard_map/ppermute | solution.py:455
  137.4 47.0 %collective-permute-start.7 = (bf16[116,1,16,128]{3,2,1,0:T(8,128)(2,1)S(1)}, bf16[116,1,16,128]{3,2,1,0:T(8,128)(2,1)S(1)}, u32[]{:S(2)}, u32[]{:S(2)}) collective-permute-start(bf16[116,1,16,128]{3,2,1,0:T(8,128)(2,1)S(1)} %get-tuple-element.36), channel_id=1, source_target_pairs={{0,4},{2,6},{4,0},{6,2},{1,5},{3,7},{5,1},{7,3},{8,12},{10,14},{12... | collective-permute-start | bytes 1425416 | tf_op jit(solution)/shard_map/ppermute | solution.py:455
  138.0 55.8 %collective-permute-start.8 = (bf16[116,1,16,128]{3,2,1,0:T(8,128)(2,1)S(1)}, bf16[116,1,16,128]{3,2,1,0:T(8,128)(2,1)S(1)}, u32[]{:S(2)}, u32[]{:S(2)}) collective-permute-start(bf16[116,1,16,128]{3,2,1,0:T(8,128)(2,1)S(1)} %get-tuple-element.37), channel_id=1, source_target_pairs={{0,6},{2,4},{4,2},{6,0},{1,7},{3,5},{5,3},{7,1},{8,14},{10,12},{12... | collective-permute-start | bytes 1425416 | tf_op jit(solution)/shard_map/ppermute | solution.py:455
  184.3 23.4 %collective-permute-start.18 = (bf16[64,1,16,128]{3,2,1,0:T(8,128)(2,1)S(1)}, bf16[64,1,16,128]{3,2,1,0:T(8,128)(2,1)S(1)}, u32[]{:S(2)}, u32[]{:S(2)}) collective-permute-start(bf16[64,1,16,128]{3,2,1,0:T(8,128)(2,1)S(1)} %get-tuple-element.47), channel_id=1, source_target_pairs={{0,2},{2,0},{4,6},{6,4},{1,3},{3,1},{5,7},{7,5},{8,10},{10,8},{12,... | collective-permute-start | bytes 786440 | tf_op jit(solution)/shard_map/ppermute | solution.py:455
  197.0 17.1 %collective-permute-start.9 = (bf16[64,1,16,128]{3,2,1,0:T(8,128)(2,1)S(1)}, bf16[64,1,16,128]{3,2,1,0:T(8,128)(2,1)S(1)}, u32[]{:S(2)}, u32[]{:S(2)}) collective-permute-start(bf16[64,1,16,128]{3,2,1,0:T(8,128)(2,1)S(1)} %get-tuple-element.39), channel_id=1, source_target_pairs={{0,2},{2,0},{4,6},{6,4},{1,3},{3,1},{5,7},{7,5},{8,10},{10,8},{12,... | collective-permute-start | bytes 786440 | tf_op jit(solution)/shard_map/ppermute | solution.py:455
  203.0 18.6 %collective-permute-start.19 = (bf16[32,1,16,128]{3,2,1,0:T(8,128)(2,1)S(1)}, bf16[32,1,16,128]{3,2,1,0:T(8,128)(2,1)S(1)}, u32[]{:S(2)}, u32[]{:S(2)}) collective-permute-start(bf16[32,1,16,128]{3,2,1,0:T(8,128)(2,1)S(1)} %get-tuple-element.48), channel_id=1, source_target_pairs={{0,4},{2,6},{4,0},{6,2},{1,5},{3,7},{5,1},{7,3},{8,12},{10,14},{12... | collective-permute-start | bytes 393224 | tf_op jit(solution)/shard_map/ppermute | solution.py:455
  204.2 17.4 %collective-permute-start.20 = (bf16[32,1,16,128]{3,2,1,0:T(8,128)(2,1)S(1)}, bf16[32,1,16,128]{3,2,1,0:T(8,128)(2,1)S(1)}, u32[]{:S(2)}, u32[]{:S(2)}) collective-permute-start(bf16[32,1,16,128]{3,2,1,0:T(8,128)(2,1)S(1)} %get-tuple-element.49), channel_id=1, source_target_pairs={{0,6},{2,4},{4,2},{6,0},{1,7},{3,5},{5,3},{7,1},{8,14},{10,12},{12... | collective-permute-start | bytes 393224 | tf_op jit(solution)/shard_map/ppermute | solution.py:455
  205.6 20.3 %collective-permute-start.10 = (bf16[32,1,16,128]{3,2,1,0:T(8,128)(2,1)S(1)}, bf16[32,1,16,128]{3,2,1,0:T(8,128)(2,1)S(1)}, u32[]{:S(2)}, u32[]{:S(2)}) collective-permute-start(bf16[32,1,16,128]{3,2,1,0:T(8,128)(2,1)S(1)} %get-tuple-element.40), channel_id=1, source_target_pairs={{0,4},{2,6},{4,0},{6,2},{1,5},{3,7},{5,1},{7,3},{8,12},{10,14},{12... | collective-permute-start | bytes 393224 | tf_op jit(solution)/shard_map/ppermute | solution.py:455
  207.6 18.3 %collective-permute-start.11 = (bf16[32,1,16,128]{3,2,1,0:T(8,128)(2,1)S(1)}, bf16[32,1,16,128]{3,2,1,0:T(8,128)(2,1)S(1)}, u32[]{:S(2)}, u32[]{:S(2)}) collective-permute-start(bf16[32,1,16,128]{3,2,1,0:T(8,128)(2,1)S(1)} %get-tuple-element.41), channel_id=1, source_target_pairs={{0,6},{2,4},{4,2},{6,0},{1,7},{3,5},{5,3},{7,1},{8,14},{10,12},{12... | collective-permute-start | bytes 393224 | tf_op jit(solution)/shard_map/ppermute | solution.py:455
  (2 other events, 7.3 us)

commit v6 on v5

--- a/solution.py
+++ b/solution.py
@@ -506,7 +506,10 @@
             plan, projected, arrived[j], bias, action, after(me, *spatial), tables, j
         )
         own.append(done[0])
-        arrived.append(exchange(done[1:]))
+        outgoing = done[1:]
+        if j + 1 == count and n > 2:
+            outgoing = lax.optimization_barrier((*outgoing, *arrived[-1][1:]))[: n - 1]
+        arrived.append(exchange(outgoing))
     mixed = None
     for j in range(count):
         handed = arrived[j + 2 * AHEAD][0] if plan.slotted(j + AHEAD) else None

time: 228 us -> 226 us (level)
  starting transfers between devices: 46.4 us -> 39.9 us
  waiting for transfers between devices: 88.8 us -> 92.7 us
    ppermute x21, starting transfers between devices: 46.4 us -> 39.9 us  [send(): return lax.ppermute(x, 'frame', [(i, i ^ m) for i in range(n)])]
    ppermute x21, waiting for transfers between devices: 88.8 us -> 92.7 us  [send(): return lax.ppermute(x, 'frame', [(i, i ^ m) for i in range(n)])]
where the time goes in v6:
time: 226 us; the launch traced here: 225 us
  waiting for transfers between devices  92.7 us (41%)
  Pallas kernels  82.4 us (36%)
  starting transfers between devices  39.9 us (18%)
  blocking collectives  5.19 us (2%)
  other arithmetic  3.08 us (1%)
    ppermute x21, waiting for transfers between devices, send(): return lax.ppermute(x, 'frame', [(i, i ^ m) for i in range(n)])  92.7 us
    ppermute x21, starting transfers between devices, send(): return lax.ppermute(x, 'frame', [(i, i ^ m) for i in range(n)])  39.9 us
    pallas_call x5, Pallas kernels, spatial_attention(): pl.pallas_call(spatial_kernel, grid=(clips, frames, count), in_specs=[spe...  33.6 us
    pallas_call x5, Pallas kernels, temporal_attention(): pl.pallas_call(functools.partial(temporal_kernel, plan, j), grid_spec=plt...  29.3 us
    pallas_call x5, Pallas kernels, combine(): pl.pallas_call(functools.partial(combine_kernel, plan, j), grid_spec=pltp...  10.6 us
    pallas_call x6, Pallas kernels, pack(): pl.pallas_call(functools.partial(pack_kernel, plan, k, m), grid_spec=pltp...  8.93 us
    all_gather x1, blocking collectives, local(): all_codes = lax.all_gather(codes, 'dp', axis=0, tiled=True)  5.19 us
  transfers between devices with their start and end apart: 21, of which 8 were waited for; matrix products, arithmetic and copies ran while one was open for 2% of the time, Pallas kernels for 35%

profile of v6, /device:TPU:0, one launch (start us, length us, event | category | flops | bytes accessed | tf_op | source)
XLA Modules:
  0.0 224.8 jit_solution(17198456487515261073)
XLA Ops:
  1.9 4.0 %collective-permute-start.1 = (bf16[96,1,16,128]{3,2,1,0:T(8,128)(2,1)}, bf16[96,1,16,128]{3,2,1,0:T(8,128)(2,1)S(1)}, u32[]{:S(2)}, u32[]{:S(2)}) collective-permute-start(bf16[96,1,16,128]{3,2,1,0:T(8,128)(2,1)} %pack.7), channel_id=1, source_target_pairs={{0,4},{2,6},{4,0},{6,2},{1,5},{3,7},{5,1},{7,3},{8,12},{10,14},{12... | collective-permute-start | bytes 1179656 | tf_op jit(solution)/shard_map/ppermute | solution.py:455
  18.2 5.2 %all_gather.3 = f32[4,16,32]{2,1,0:T(8,128)S(1)} all-gather(f32[1,16,32]{2,1,0:T(8,128)S(1)} %copy-done.1), channel_id=1, replica_groups=mesh['dp'=4,'frame'=4,'mp'=2] {'dp'}, dimensions={0}, use_global_device_ids=true | all-gather | bytes 10240 | tf_op jit(solution)/shard_map/all_gather | solution.py:492
  26.3 6.7 %spatial.7.spatial_ref = bf16[1,4,128,512]{3,2,1,0:T(8,128)(2,1)S(1)} custom-call(bf16[6,1,4,128,2560]{4,3,2,1,0:T(8,128)(2,1)} %refs_5_.5, bf16[6,1,4,128,2560]{4,3,2,1,0:T(8,128)(2,1)} %refs_5_.5, bf16[6,1,4,128,2560]{4,3,2,1,0:T(8,128)(2,1)} %refs_5_.5), custom_call_target="tpu_custom_call" | custom-call | flops 134217728 | bytes 2097152 | tf_op jit(solution)/shard_map/spatial/pallas_call | solution.py:49
  34.5 6.9 %collective-permute-done.1.refs_4_ = bf16[96,1,16,128]{3,2,1,0:T(8,128)(2,1)S(1)} collective-permute-done((bf16[96,1,16,128]{3,2,1,0:T(8,128)(2,1)}, bf16[96,1,16,128]{3,2,1,0:T(8,128)(2,1)S(1)}, u32[]{:S(2)}, u32[]{:S(2)}) %collective-permute-start.1) | collective-permute-done | bytes 393248 | tf_op jit(solution)/shard_map/ppermute | solution.py:455
  41.4 2.8 %collective-permute-start.11 = (bf16[96,1,16,128]{3,2,1,0:T(8,128)(2,1)S(1)}, bf16[96,1,16,128]{3,2,1,0:T(8,128)(2,1)S(1)}, u32[]{:S(2)}, u32[]{:S(2)}) collective-permute-start(bf16[96,1,16,128]{3,2,1,0:T(8,128)(2,1)S(1)} %pack.11), channel_id=1, source_target_pairs={{0,6},{2,4},{4,2},{6,0},{1,7},{3,5},{5,3},{7,1},{8,14},{10,12},{12... | collective-permute-start | bytes 1179656 | tf_op jit(solution)/shard_map/ppermute | solution.py:455
  44.2 6.7 %spatial.6.spatial_ref = bf16[1,4,128,512]{3,2,1,0:T(8,128)(2,1)S(1)} custom-call(bf16[6,1,4,128,2560]{4,3,2,1,0:T(8,128)(2,1)} %refs_5_.5, bf16[6,1,4,128,2560]{4,3,2,1,0:T(8,128)(2,1)} %refs_5_.5, bf16[6,1,4,128,2560]{4,3,2,1,0:T(8,128)(2,1)} %refs_5_.5), custom_call_target="tpu_custom_call" | custom-call | flops 134217728 | bytes 2097152 | tf_op jit(solution)/shard_map/spatial/pallas_call | solution.py:49
  51.0 7.7 %temporal.5 = (bf16[32,1,16,128]{3,2,1,0:T(8,128)(2,1)S(1)}, bf16[160,1,16,128]{3,2,1,0:T(8,128)(2,1)S(1)}, bf16[116,1,16,128]{3,2,1,0:T(8,128)(2,1)S(1)}, bf16[116,1,16,128]{3,2,1,0:T(8,128)(2,1)S(1)}) custom-call(s32[1]{0:T(128)} %bitcast.me_ref, s32[16]{0:T(128)S(1)} %convert_reduce_fusion.rank_ref, s32[16]{0:T(128)S(1)} %get-tuple-element.61.alone_ref, ...), custom_call_target="tpu_custom_call" | custom-call | flops 268435456 | bytes 3473408 | tf_op jit(solution)/shard_map/temporal/pallas_call | solution.py:310
  60.4 6.4 %collective-permute-done.10.refs_4_ = bf16[96,1,16,128]{3,2,1,0:T(8,128)(2,1)S(1)} collective-permute-done((bf16[96,1,16,128]{3,2,1,0:T(8,128)(2,1)}, bf16[96,1,16,128]{3,2,1,0:T(8,128)(2,1)S(1)}, u32[]{:S(2)}, u32[]{:S(2)}) %collective-permute-start.10) | collective-permute-done | bytes 393248 | tf_op jit(solution)/shard_map/ppermute | solution.py:455
  66.7 2.8 %collective-permute-start.5 = (bf16[116,1,16,128]{3,2,1,0:T(8,128)(2,1)S(1)}, bf16[116,1,16,128]{3,2,1,0:T(8,128)(2,1)S(1)}, u32[]{:S(2)}, u32[]{:S(2)}) collective-permute-start(bf16[116,1,16,128]{3,2,1,0:T(8,128)(2,1)S(1)} %get-tuple-element.37), channel_id=1, source_target_pairs={{0,6},{2,4},{4,2},{6,0},{1,7},{3,5},{5,3},{7,1},{8,14},{10,12},{12... | collective-permute-start | bytes 1425416 | tf_op jit(solution)/shard_map/ppermute | solution.py:455
  69.6 6.7 %spatial.8.spatial_ref = bf16[1,4,128,512]{3,2,1,0:T(8,128)(2,1)S(1)} custom-call(bf16[6,1,4,128,2560]{4,3,2,1,0:T(8,128)(2,1)} %refs_5_.5, bf16[6,1,4,128,2560]{4,3,2,1,0:T(8,128)(2,1)} %refs_5_.5, bf16[6,1,4,128,2560]{4,3,2,1,0:T(8,128)(2,1)} %refs_5_.5), custom_call_target="tpu_custom_call" | custom-call | flops 134217728 | bytes 2097152 | tf_op jit(solution)/shard_map/spatial/pallas_call | solution.py:49
  76.3 7.5 %temporal.8 = (bf16[32,1,16,128]{3,2,1,0:T(8,128)(2,1)S(1)}, bf16[128,1,16,128]{3,2,1,0:T(8,128)(2,1)S(1)}, bf16[116,1,16,128]{3,2,1,0:T(8,128)(2,1)S(1)}, bf16[116,1,16,128]{3,2,1,0:T(8,128)(2,1)S(1)}) custom-call(s32[1]{0:T(128)} %bitcast.me_ref, s32[16]{0:T(128)S(1)} %convert_reduce_fusion.rank_ref, s32[16]{0:T(128)S(1)} %get-tuple-element.61.alone_ref, ...), custom_call_target="tpu_custom_call" | custom-call | flops 268435456 | bytes 3211264 | tf_op jit(solution)/shard_map/temporal/pallas_call | solution.py:310
  84.7 6.7 %spatial.9.spatial_ref = bf16[1,4,128,512]{3,2,1,0:T(8,128)(2,1)S(1)} custom-call(bf16[6,1,4,128,2560]{4,3,2,1,0:T(8,128)(2,1)} %refs_5_.5, bf16[6,1,4,128,2560]{4,3,2,1,0:T(8,128)(2,1)} %refs_5_.5, bf16[6,1,4,128,2560]{4,3,2,1,0:T(8,128)(2,1)} %refs_5_.5), custom_call_target="tpu_custom_call" | custom-call | flops 134217728 | bytes 2097152 | tf_op jit(solution)/shard_map/spatial/pallas_call | solution.py:49
  92.3 23.7 %collective-permute-done.4.refs_4_.refs_2_ = bf16[116,1,16,128]{3,2,1,0:T(8,128)(2,1)S(1)} collective-permute-done((bf16[116,1,16,128]{3,2,1,0:T(8,128)(2,1)S(1)}, bf16[116,1,16,128]{3,2,1,0:T(8,128)(2,1)S(1)}, u32[]{:S(2)}, u32[]{:S(2)}) %collective-permute-start.4) | collective-permute-done | bytes 475168 | tf_op jit(solution)/shard_map/ppermute | solution.py:455
  116.0 7.7 %temporal.6 = (bf16[32,1,16,128]{3,2,1,0:T(8,128)(2,1)S(1)}, bf16[160,1,16,128]{3,2,1,0:T(8,128)(2,1)S(1)}, bf16[116,1,16,128]{3,2,1,0:T(8,128)(2,1)S(1)}, bf16[116,1,16,128]{3,2,1,0:T(8,128)(2,1)S(1)}) custom-call(s32[1]{0:T(128)} %bitcast.me_ref, s32[16]{0:T(128)S(1)} %convert_reduce_fusion.rank_ref, s32[16]{0:T(128)S(1)} %get-tuple-element.61.alone_ref, ...), custom_call_target="tpu_custom_call" | custom-call | flops 268435456 | bytes 3473408 | tf_op jit(solution)/shard_map/temporal/pallas_call | solution.py:310
  123.8 10.8 %collective-permute-start.6 = (bf16[160,1,16,128]{3,2,1,0:T(8,128)(2,1)S(1)}, bf16[160,1,16,128]{3,2,1,0:T(8,128)(2,1)S(1)}, u32[]{:S(2)}, u32[]{:S(2)}) collective-permute-start(bf16[160,1,16,128]{3,2,1,0:T(8,128)(2,1)S(1)} %get-tuple-element.38), channel_id=1, source_target_pairs={{0,2},{2,0},{4,6},{6,4},{1,3},{3,1},{5,7},{7,5},{8,10},{10,8},{12,... | collective-permute-start | bytes 1966088 | tf_op jit(solution)/shard_map/ppermute | solution.py:455
  134.6 2.8 %collective-permute-start.14 = (bf16[116,1,16,128]{3,2,1,0:T(8,128)(2,1)S(1)}, bf16[116,1,16,128]{3,2,1,0:T(8,128)(2,1)S(1)}, u32[]{:S(2)}, u32[]{:S(2)}) collective-permute-start(bf16[116,1,16,128]{3,2,1,0:T(8,128)(2,1)S(1)} %get-tuple-element.48), channel_id=1, source_target_pairs={{0,6},{2,4},{4,2},{6,0},{1,7},{3,5},{5,3},{7,1},{8,14},{10,12},{12... | collective-permute-start | bytes 1425416 | tf_op jit(solution)/shard_map/ppermute | solution.py:455
  139.2 6.7 %spatial.5.spatial_ref = bf16[1,4,128,512]{3,2,1,0:T(8,128)(2,1)S(1)} custom-call(bf16[6,1,4,128,2560]{4,3,2,1,0:T(8,128)(2,1)} %refs_5_.5, bf16[6,1,4,128,2560]{4,3,2,1,0:T(8,128)(2,1)} %refs_5_.5, bf16[6,1,4,128,2560]{4,3,2,1,0:T(8,128)(2,1)} %refs_5_.5), custom_call_target="tpu_custom_call" | custom-call | flops 134217728 | bytes 2097152 | tf_op jit(solution)/shard_map/spatial/pallas_call | solution.py:49
  145.9 17.3 %collective-permute-done.14.refs_5_.refs_3_ = bf16[116,1,16,128]{3,2,1,0:T(8,128)(2,1)S(1)} collective-permute-done((bf16[116,1,16,128]{3,2,1,0:T(8,128)(2,1)S(1)}, bf16[116,1,16,128]{3,2,1,0:T(8,128)(2,1)S(1)}, u32[]{:S(2)}, u32[]{:S(2)}) %collective-permute-start.14) | collective-permute-done | bytes 475168 | tf_op jit(solution)/shard_map/ppermute | solution.py:455
  163.3 3.1 %temporal.9 = (bf16[32,1,16,128]{3,2,1,0:T(8,128)(2,1)S(1)}, bf16[64,1,16,128]{3,2,1,0:T(8,128)(2,1)S(1)}, bf16[32,1,16,128]{3,2,1,0:T(8,128)(2,1)S(1)}, bf16[32,1,16,128]{3,2,1,0:T(8,128)(2,1)S(1)}) custom-call(s32[1]{0:T(128)} %bitcast.me_ref, s32[16]{0:T(128)S(1)} %convert_reduce_fusion.rank_ref, s32[16]{0:T(128)S(1)} %get-tuple-element.61.alone_ref, ...), custom_call_target="tpu_custom_call" | custom-call | flops 268435456 | bytes 1310720 | tf_op jit(solution)/shard_map/temporal/pallas_call | solution.py:310
  167.5 26.7 %collective-permute-done.7.refs_4_.refs_2_ = bf16[116,1,16,128]{3,2,1,0:T(8,128)(2,1)S(1)} collective-permute-done((bf16[116,1,16,128]{3,2,1,0:T(8,128)(2,1)S(1)}, bf16[116,1,16,128]{3,2,1,0:T(8,128)(2,1)S(1)}, u32[]{:S(2)}, u32[]{:S(2)}) %collective-permute-start.7) | collective-permute-done | bytes 475168 | tf_op jit(solution)/shard_map/ppermute | solution.py:455
  194.2 3.1 %temporal.7 = (bf16[32,1,16,128]{3,2,1,0:T(8,128)(2,1)S(1)}, bf16[64,1,16,128]{3,2,1,0:T(8,128)(2,1)S(1)}, bf16[32,1,16,128]{3,2,1,0:T(8,128)(2,1)S(1)}, bf16[32,1,16,128]{3,2,1,0:T(8,128)(2,1)S(1)}) custom-call(s32[1]{0:T(128)} %bitcast.me_ref, s32[16]{0:T(128)S(1)} %convert_reduce_fusion.rank_ref, s32[16]{0:T(128)S(1)} %get-tuple-element.61.alone_ref, ...), custom_call_target="tpu_custom_call" | custom-call | flops 268435456 | bytes 1310720 | tf_op jit(solution)/shard_map/temporal/pallas_call | solution.py:310
  197.4 9.8 %collective-permute-done.15.refs_2_ = bf16[32,1,16,128]{3,2,1,0:T(8,128)(2,1)S(1)} collective-permute-done((bf16[32,1,16,128]{3,2,1,0:T(8,128)(2,1)S(1)}, bf16[32,1,16,128]{3,2,1,0:T(8,128)(2,1)S(1)}, u32[]{:S(2)}, u32[]{:S(2)}) %collective-permute-start.15) | collective-permute-done | bytes 131104 | tf_op jit(solution)/shard_map/ppermute | solution.py:455
  214.9 2.6 %combine.6.refs_7_ = bf16[1,4,128,2560]{3,2,1,0:T(8,128)(2,1)} custom-call(s32[1]{0:T(128)} %bitcast.me_ref, s32[16]{0:T(128)S(1)} %convert_reduce_fusion.rank_ref, s32[16]{0:T(128)S(1)} %get-tuple-element.61.alone_ref, s32[2]{0:T(128)S(1)} %add_bitcast_fusion.kept_ref, ...), custom_call_target="tpu_custom_call", output_to_operand_aliasing={{}: (12, {})} | custom-call | flops 262144 | bytes 1572864 | tf_op jit(solution)/shard_map/combine/pallas_call | solution.py:419
  218.2 2.6 %combine.7.refs_4_ = bf16[1,4,128,2560]{3,2,1,0:T(8,128)(2,1)} custom-call(s32[1]{0:T(128)} %bitcast.me_ref, s32[16]{0:T(128)S(1)} %convert_reduce_fusion.rank_ref, s32[16]{0:T(128)S(1)} %get-tuple-element.61.alone_ref, s32[2]{0:T(128)S(1)} %add_bitcast_fusion.kept_ref, ...), custom_call_target="tpu_custom_call", output_to_operand_aliasing={{}: (12, {})} | custom-call | flops 262144 | bytes 1572864 | tf_op jit(solution)/shard_map/combine/pallas_call | solution.py:419
  (71 shorter events, 37.2 us)
Async XLA Ops:
  0.0 34.2 %copy-start = (f32[32,2560]{1,0:T(8,128)S(1)}, f32[32,2560]{1,0:T(8,128)}, u32[]{:S(2)}) copy-start(f32[32,2560]{1,0:T(8,128)} %param.8) | copy-start | bytes 983044
  1.9 39.6 %collective-permute-start.1 = (bf16[96,1,16,128]{3,2,1,0:T(8,128)(2,1)}, bf16[96,1,16,128]{3,2,1,0:T(8,128)(2,1)S(1)}, u32[]{:S(2)}, u32[]{:S(2)}) collective-permute-start(bf16[96,1,16,128]{3,2,1,0:T(8,128)(2,1)} %pack.7), channel_id=1, source_target_pairs={{0,4},{2,6},{4,0},{6,2},{1,5},{3,7},{5,1},{7,3},{8,12},{10,14},{12... | collective-permute-start | bytes 1179656 | tf_op jit(solution)/shard_map/ppermute | solution.py:455
  7.7 43.2 %collective-permute-start.2 = (bf16[96,1,16,128]{3,2,1,0:T(8,128)(2,1)}, bf16[96,1,16,128]{3,2,1,0:T(8,128)(2,1)}, u32[]{:S(2)}, u32[]{:S(2)}) collective-permute-start(bf16[96,1,16,128]{3,2,1,0:T(8,128)(2,1)} %pack.8), channel_id=1, source_target_pairs={{0,6},{2,4},{4,2},{6,0},{1,7},{3,5},{5,3},{7,1},{8,14},{10,12},{12... | collective-permute-start | bytes 1179656 | tf_op jit(solution)/shard_map/ppermute | solution.py:455
  10.9 55.9 %collective-permute-start.10 = (bf16[96,1,16,128]{3,2,1,0:T(8,128)(2,1)}, bf16[96,1,16,128]{3,2,1,0:T(8,128)(2,1)S(1)}, u32[]{:S(2)}, u32[]{:S(2)}) collective-permute-start(bf16[96,1,16,128]{3,2,1,0:T(8,128)(2,1)} %pack.10), channel_id=1, source_target_pairs={{0,4},{2,6},{4,0},{6,2},{1,5},{3,7},{5,1},{7,3},{8,12},{10,14},{12... | collective-permute-start | bytes 1179656 | tf_op jit(solution)/shard_map/ppermute | solution.py:455
  13.8 4.4 %copy-start.1 = (f32[1,16,32]{2,1,0:T(8,128)S(1)}, f32[1,16,32]{2,1,0:T(8,128)}, u32[]{:S(2)}) copy-start(f32[1,16,32]{2,1,0:T(8,128)} %param.7) | copy-start | bytes 6148
  13.8 9.6 %copy-start.2 = (s32[4]{0:T(128)S(1)}, s32[4]{0:T(128)}, u32[]{:S(2)}) copy-start(s32[4]{0:T(128)} %param.9) | copy-start | bytes 52
  13.8 37.2 %collective-permute-start = (bf16[128,1,16,128]{3,2,1,0:T(8,128)(2,1)S(1)}, bf16[128,1,16,128]{3,2,1,0:T(8,128)(2,1)S(1)}, u32[]{:S(2)}, u32[]{:S(2)}) collective-permute-start(bf16[128,1,16,128]{3,2,1,0:T(8,128)(2,1)S(1)} %pack.6), channel_id=1, source_target_pairs={{0,2},{2,0},{4,6},{6,4},{1,3},{3,1},{5,7},{7,5},{8,10},{10,8},{12,... | collective-permute-start | bytes 1572872 | tf_op jit(solution)/shard_map/ppermute | solution.py:455
  16.4 59.9 %collective-permute-start.9 = (bf16[128,1,16,128]{3,2,1,0:T(8,128)(2,1)S(1)}, bf16[128,1,16,128]{3,2,1,0:T(8,128)(2,1)S(1)}, u32[]{:S(2)}, u32[]{:S(2)}) collective-permute-start(bf16[128,1,16,128]{3,2,1,0:T(8,128)(2,1)S(1)} %pack.9), channel_id=1, source_target_pairs={{0,2},{2,0},{4,6},{6,4},{1,3},{3,1},{5,7},{7,5},{8,10},{10,8},{12,... | collective-permute-start | bytes 1572872 | tf_op jit(solution)/shard_map/ppermute | solution.py:455
  41.4 34.9 %collective-permute-start.11 = (bf16[96,1,16,128]{3,2,1,0:T(8,128)(2,1)S(1)}, bf16[96,1,16,128]{3,2,1,0:T(8,128)(2,1)S(1)}, u32[]{:S(2)}, u32[]{:S(2)}) collective-permute-start(bf16[96,1,16,128]{3,2,1,0:T(8,128)(2,1)S(1)} %pack.11), channel_id=1, source_target_pairs={{0,6},{2,4},{4,2},{6,0},{1,7},{3,5},{5,3},{7,1},{8,14},{10,12},{12... | collective-permute-start | bytes 1179656 | tf_op jit(solution)/shard_map/ppermute | solution.py:455
  58.7 57.3 %collective-permute-start.3 = (bf16[160,1,16,128]{3,2,1,0:T(8,128)(2,1)S(1)}, bf16[160,1,16,128]{3,2,1,0:T(8,128)(2,1)S(1)}, u32[]{:S(2)}, u32[]{:S(2)}) collective-permute-start(bf16[160,1,16,128]{3,2,1,0:T(8,128)(2,1)S(1)} %get-tuple-element.35), channel_id=1, source_target_pairs={{0,2},{2,0},{4,6},{6,4},{1,3},{3,1},{5,7},{7,5},{8,10},{10,8},{12,... | collective-permute-start | bytes 1966088 | tf_op jit(solution)/shard_map/ppermute | solution.py:455
  58.8 57.2 %collective-permute-start.4 = (bf16[116,1,16,128]{3,2,1,0:T(8,128)(2,1)S(1)}, bf16[116,1,16,128]{3,2,1,0:T(8,128)(2,1)S(1)}, u32[]{:S(2)}, u32[]{:S(2)}) collective-permute-start(bf16[116,1,16,128]{3,2,1,0:T(8,128)(2,1)S(1)} %get-tuple-element.36), channel_id=1, source_target_pairs={{0,4},{2,6},{4,0},{6,2},{1,5},{3,7},{5,1},{7,3},{8,12},{10,14},{12... | collective-permute-start | bytes 1425416 | tf_op jit(solution)/shard_map/ppermute | solution.py:455
  66.7 49.3 %collective-permute-start.5 = (bf16[116,1,16,128]{3,2,1,0:T(8,128)(2,1)S(1)}, bf16[116,1,16,128]{3,2,1,0:T(8,128)(2,1)S(1)}, u32[]{:S(2)}, u32[]{:S(2)}) collective-permute-start(bf16[116,1,16,128]{3,2,1,0:T(8,128)(2,1)S(1)} %get-tuple-element.37), channel_id=1, source_target_pairs={{0,6},{2,4},{4,2},{6,0},{1,7},{3,5},{5,3},{7,1},{8,14},{10,12},{12... | collective-permute-start | bytes 1425416 | tf_op jit(solution)/shard_map/ppermute | solution.py:455
  83.8 53.6 %collective-permute-start.13 = (bf16[116,1,16,128]{3,2,1,0:T(8,128)(2,1)S(1)}, bf16[116,1,16,128]{3,2,1,0:T(8,128)(2,1)S(1)}, u32[]{:S(2)}, u32[]{:S(2)}) collective-permute-start(bf16[116,1,16,128]{3,2,1,0:T(8,128)(2,1)S(1)} %get-tuple-element.47), channel_id=1, source_target_pairs={{0,4},{2,6},{4,0},{6,2},{1,5},{3,7},{5,1},{7,3},{8,12},{10,14},{12... | collective-permute-start | bytes 1425416 | tf_op jit(solution)/shard_map/ppermute | solution.py:455
  91.4 71.8 %collective-permute-start.12 = (bf16[128,1,16,128]{3,2,1,0:T(8,128)(2,1)S(1)}, bf16[128,1,16,128]{3,2,1,0:T(8,128)(2,1)S(1)}, u32[]{:S(2)}, u32[]{:S(2)}) collective-permute-start(bf16[128,1,16,128]{3,2,1,0:T(8,128)(2,1)S(1)} %get-tuple-element.46), channel_id=1, source_target_pairs={{0,2},{2,0},{4,6},{6,4},{1,3},{3,1},{5,7},{7,5},{8,10},{10,8},{12,... | collective-permute-start | bytes 1572872 | tf_op jit(solution)/shard_map/ppermute | solution.py:455
  123.8 70.5 %collective-permute-start.6 = (bf16[160,1,16,128]{3,2,1,0:T(8,128)(2,1)S(1)}, bf16[160,1,16,128]{3,2,1,0:T(8,128)(2,1)S(1)}, u32[]{:S(2)}, u32[]{:S(2)}) collective-permute-start(bf16[160,1,16,128]{3,2,1,0:T(8,128)(2,1)S(1)} %get-tuple-element.38), channel_id=1, source_target_pairs={{0,2},{2,0},{4,6},{6,4},{1,3},{3,1},{5,7},{7,5},{8,10},{10,8},{12,... | collective-permute-start | bytes 1966088 | tf_op jit(solution)/shard_map/ppermute | solution.py:455
  134.6 28.7 %collective-permute-start.14 = (bf16[116,1,16,128]{3,2,1,0:T(8,128)(2,1)S(1)}, bf16[116,1,16,128]{3,2,1,0:T(8,128)(2,1)S(1)}, u32[]{:S(2)}, u32[]{:S(2)}) collective-permute-start(bf16[116,1,16,128]{3,2,1,0:T(8,128)(2,1)S(1)} %get-tuple-element.48), channel_id=1, source_target_pairs={{0,6},{2,4},{4,2},{6,0},{1,7},{3,5},{5,3},{7,1},{8,14},{10,12},{12... | collective-permute-start | bytes 1425416 | tf_op jit(solution)/shard_map/ppermute | solution.py:455
  137.4 56.8 %collective-permute-start.7 = (bf16[116,1,16,128]{3,2,1,0:T(8,128)(2,1)S(1)}, bf16[116,1,16,128]{3,2,1,0:T(8,128)(2,1)S(1)}, u32[]{:S(2)}, u32[]{:S(2)}) collective-permute-start(bf16[116,1,16,128]{3,2,1,0:T(8,128)(2,1)S(1)} %get-tuple-element.39), channel_id=1, source_target_pairs={{0,4},{2,6},{4,0},{6,2},{1,5},{3,7},{5,1},{7,3},{8,12},{10,14},{12... | collective-permute-start | bytes 1425416 | tf_op jit(solution)/shard_map/ppermute | solution.py:455
  137.4 56.8 %collective-permute-start.8 = (bf16[116,1,16,128]{3,2,1,0:T(8,128)(2,1)S(1)}, bf16[116,1,16,128]{3,2,1,0:T(8,128)(2,1)S(1)}, u32[]{:S(2)}, u32[]{:S(2)}) collective-permute-start(bf16[116,1,16,128]{3,2,1,0:T(8,128)(2,1)S(1)} %get-tuple-element.40), channel_id=1, source_target_pairs={{0,6},{2,4},{4,2},{6,0},{1,7},{3,5},{5,3},{7,1},{8,14},{10,12},{12... | collective-permute-start | bytes 1425416 | tf_op jit(solution)/shard_map/ppermute | solution.py:455
  166.4 40.8 %collective-permute-start.15 = (bf16[32,1,16,128]{3,2,1,0:T(8,128)(2,1)S(1)}, bf16[32,1,16,128]{3,2,1,0:T(8,128)(2,1)S(1)}, u32[]{:S(2)}, u32[]{:S(2)}) collective-permute-start(bf16[32,1,16,128]{3,2,1,0:T(8,128)(2,1)S(1)} %get-tuple-element.49), channel_id=1, source_target_pairs={{0,4},{2,6},{4,0},{6,2},{1,5},{3,7},{5,1},{7,3},{8,12},{10,14},{12... | collective-permute-start | bytes 393224 | tf_op jit(solution)/shard_map/ppermute | solution.py:455
  166.5 40.7 %collective-permute-start.16 = (bf16[32,1,16,128]{3,2,1,0:T(8,128)(2,1)S(1)}, bf16[32,1,16,128]{3,2,1,0:T(8,128)(2,1)S(1)}, u32[]{:S(2)}, u32[]{:S(2)}) collective-permute-start(bf16[32,1,16,128]{3,2,1,0:T(8,128)(2,1)S(1)} %get-tuple-element.50), channel_id=1, source_target_pairs={{0,6},{2,4},{4,2},{6,0},{1,7},{3,5},{5,3},{7,1},{8,14},{10,12},{12... | collective-permute-start | bytes 393224 | tf_op jit(solution)/shard_map/ppermute | solution.py:455
  194.2 20.7 %collective-permute-start.20 = (bf16[64,1,16,128]{3,2,1,0:T(8,128)(2,1)S(1)}, bf16[64,1,16,128]{3,2,1,0:T(8,128)(2,1)S(1)}, u32[]{:S(2)}, u32[]{:S(2)}) collective-permute-start(bf16[64,1,16,128]{3,2,1,0:T(8,128)(2,1)S(1)} %get-tuple-element.55), channel_id=1, source_target_pairs={{0,2},{2,0},{4,6},{6,4},{1,3},{3,1},{5,7},{7,5},{8,10},{10,8},{12,... | collective-permute-start | bytes 786440 | tf_op jit(solution)/shard_map/ppermute | solution.py:455
  207.2 11.0 %collective-permute-start.17 = (bf16[64,1,16,128]{3,2,1,0:T(8,128)(2,1)S(1)}, bf16[64,1,16,128]{3,2,1,0:T(8,128)(2,1)S(1)}, u32[]{:S(2)}, u32[]{:S(2)}) collective-permute-start(bf16[64,1,16,128]{3,2,1,0:T(8,128)(2,1)S(1)} %get-tuple-element.51), channel_id=1, source_target_pairs={{0,2},{2,0},{4,6},{6,4},{1,3},{3,1},{5,7},{7,5},{8,10},{10,8},{12,... | collective-permute-start | bytes 786440 | tf_op jit(solution)/shard_map/ppermute | solution.py:455
  209.7 12.6 %collective-permute-start.18 = (bf16[32,1,16,128]{3,2,1,0:T(8,128)(2,1)S(1)}, bf16[32,1,16,128]{3,2,1,0:T(8,128)(2,1)S(1)}, u32[]{:S(2)}, u32[]{:S(2)}) collective-permute-start(bf16[32,1,16,128]{3,2,1,0:T(8,128)(2,1)S(1)} %get-tuple-element.52), channel_id=1, source_target_pairs={{0,4},{2,6},{4,0},{6,2},{1,5},{3,7},{5,1},{7,3},{8,12},{10,14},{12... | collective-permute-start | bytes 393224 | tf_op jit(solution)/shard_map/ppermute | solution.py:455
  210.9 12.4 %collective-permute-start.19 = (bf16[32,1,16,128]{3,2,1,0:T(8,128)(2,1)S(1)}, bf16[32,1,16,128]{3,2,1,0:T(8,128)(2,1)S(1)}, u32[]{:S(2)}, u32[]{:S(2)}) collective-permute-start(bf16[32,1,16,128]{3,2,1,0:T(8,128)(2,1)S(1)} %get-tuple-element.53), channel_id=1, source_target_pairs={{0,6},{2,4},{4,2},{6,0},{1,7},{3,5},{5,3},{7,1},{8,14},{10,12},{12... | collective-permute-start | bytes 393224 | tf_op jit(solution)/shard_map/ppermute | solution.py:455
  (2 other events, 7.3 us)

commit v7 on v6

--- a/solution.py
+++ b/solution.py
@@ -12,6 +12,7 @@
 GROUP = 16
 SHARES = (4, 4, 4, 4, 4)
 AHEAD = 2
+LAST = {1: (2,), 2: (2,), 3: (2, 3)}
 EPISODES = 3
 HIGHEST = lax.Precision.HIGHEST
 VMEM = 48 * 1024 * 1024
@@ -68,7 +69,8 @@
         self.chunks = [(a, b - a) for a, b in zip([0] + ends, ends) if b > a]
         self.n, self.frames = n, frames
         self.groups = patches // n // GROUP
-        self.halved = n == 4 and self.groups == 2 and len({c[1] for c in self.chunks}) == 1
+        alternate = all(a[1] == b[1] for a, b in zip(self.chunks, self.chunks[AHEAD:]))
+        self.halved = n == 4 and self.groups == 2 and alternate
         self.slots = n * frames - EPISODES
 
     def heads(self, j):
@@ -354,45 +356,41 @@
     share = plan.groups * GROUP
     kept_there = kept_ref[c * 2 + 1]
 
-    def put(f, h, at, temporal):
-        rows = pl.ds(pl.multiple_of(at, GROUP), temporal.shape[0])
-        cut = slice(h * E, (h + 1) * E)
+    def put(f, i, at, temporal):
+        rows = pl.ds(pl.multiple_of(at, GROUP), temporal.shape[-2])
+        cut = slice(i * E, (i + 1) * E)
         total = spatial_ref[0, f, rows, cut].astype(jnp.float32) + temporal.astype(jnp.float32)
         out_ref[0, f, rows, cut] = total.astype(jnp.bfloat16)
 
-    for h in range(heads):
-        for f in range(frames):
-            for m in range(n):
-                row = (me ^ m) * share
-                if slotted and m > 1:
-                    to = slot(
-                        plan,
-                        came[m - 1]["slots"],
-                        h,
-                        kept_there + rank_ref[c * n * frames + f],
-                    )
-                    put(f, h, row + parity * GROUP, back[m - 1][pl.ds(to, 1), 0][0])
-                    local = plan.parts(j + 2 * AHEAD, 1)[0]["ol"]
-                    local += (((m ^ 1) - 2) * heads + h) * frames + f
-                    put(f, h, row + (1 - parity) * GROUP, refs[0][local, 0])
-                    continue
+    blocks, size, _ = pieces(*plan.chunks[j])
+    piece = pl.program_id(1)
+    for i in range(size):
+        h = i if blocks == 1 else piece * size + i
+        for m in range(n):
+            row = (me ^ m) * share
+            if not slotted or m < 2:
                 x = own if m == 0 else back[m - 1]
                 base = 0 if m == 0 else came[m - 1]["o"]
                 for g in range(plan.groups):
-                    put(f, h, row + g * GROUP, x[base + plan.tile(h, g) + f, 0])
+                    part = x[pl.ds(base + plan.tile(h, g), frames), 0]
+                    put(slice(None), i, row + g * GROUP, part)
+                continue
+            local = plan.parts(j + 2 * AHEAD, 1)[0]["ol"] + (((m ^ 1) - 2) * heads + h) * frames
+            put(slice(None), i, row + (1 - parity) * GROUP, refs[0][pl.ds(local, frames), 0])
+            for f in range(frames):
+                kept = kept_there + rank_ref[c * n * frames + f]
+                to = slot(plan, came[m - 1]["slots"], h, kept)
+                put(f, i, row + parity * GROUP, back[m - 1][to, 0])
     if slotted:
-        blocks = pieces(*plan.chunks[j])[0]
-        values, action_ref = refs[1 : 1 + blocks], refs[1 + blocks]
-        start = plan.chunks[j][0]
+        values, action_ref = refs[1], refs[2]
         for f in range(frames):
 
             @pl.when(alone_ref[c * n * frames + f] == 1)
             def _():
-                for h in range(heads):
-                    x, cut = head_cols(values, h)
-                    action = action_ref[0, f : f + 1, (start + h) * E : (start + h + 1) * E]
-                    v = x[0, 0, f, :, cut].astype(jnp.float32) + action
-                    put(f, h, 0, v.astype(jnp.bfloat16))
+                for i in range(size):
+                    cut = slice(i * E, (i + 1) * E)
+                    v = values[0, 0, f, :, cut].astype(jnp.float32) + action_ref[0, f : f + 1, cut]
+                    put(f, i, 0, v.astype(jnp.bfloat16))
 
 
 def combine(plan, mixed, spatial, own, back, handed, projected, action, me, tables, j, width):
@@ -400,30 +398,28 @@
     n = plan.n
     start, heads = plan.chunks[j]
     count, size, first = pieces(start, heads)
-    whole = pl.BlockSpec((1, frames, patches, cols), lambda c, *_: (c, 0, 0, 0))
+    whole = pl.BlockSpec((1, frames, patches, size * E), lambda c, i, *_: (c, 0, 0, i))
     arrays, specs = [spatial, own, *back], [whole] + [tiles(x.shape[0]) for x in (own, *back)]
     if plan.slotted(j + AHEAD):
-        arrays += [handed] + [projected] * count + [action]
-        specs += [tiles(handed.shape[0])]
+        arrays += [handed, projected, action]
         specs += [
+            tiles(handed.shape[0]),
             pl.BlockSpec(
-                (1, 1, frames, patches, size * E), lambda c, *_, i=i: (5, c, 0, 0, first + i)
-            )
-            for i in range(count)
+                (1, 1, frames, patches, size * E), lambda c, i, *_: (5, c, 0, 0, first + i)
+            ),
+            pl.BlockSpec((1, action.shape[1], size * E), lambda c, i, *_: (c, 0, first + i)),
         ]
-        specs += [pl.BlockSpec((1, action.shape[1], action.shape[2]), lambda c, *_: (c, 0, 0))]
     if mixed is not None:
         arrays += [mixed]
         specs += [pl.BlockSpec(memory_space=pl.ANY)]
-    assert start % heads == 0
     return pl.pallas_call(
         functools.partial(combine_kernel, plan, j),
         grid_spec=pltpu.PrefetchScalarGridSpec(
             num_scalar_prefetch=4,
-            grid=(clips,),
+            grid=(clips, count),
             in_specs=specs,
             out_specs=pl.BlockSpec(
-                (1, frames, patches, cols), lambda c, *_: (c, 0, 0, start // heads)
+                (1, frames, patches, size * E), lambda c, i, *_: (c, 0, 0, first + i)
             ),
         ),
         out_shape=jax.ShapeDtypeStruct((clips, frames, patches, width), jnp.bfloat16),
@@ -503,12 +499,14 @@
         for early in plan.chunks[len(spatial) : j + 2]:
             spatial.append(spatial_attention(projected, *early))
         done = temporal_attention(
-            plan, projected, arrived[j], bias, action, after(me, *spatial), tables, j
+            plan, projected, arrived[j], bias, action, after(me, *spatial, *own), tables, j
         )
         own.append(done[0])
         outgoing = done[1:]
-        if j + 1 == count and n > 2:
-            outgoing = lax.optimization_barrier((*outgoing, *arrived[-1][1:]))[: n - 1]
+        if j + 1 == count and n > max(LAST):
+            outgoing = list(outgoing)
+            for m, gates in LAST.items():
+                outgoing[m - 1] = after(outgoing[m - 1], *[arrived[-1][g - 1] for g in gates])
         arrived.append(exchange(outgoing))
     mixed = None
     for j in range(count):

time: 226 us -> 224 us (level)
  transfers between devices with their start and end apart: 21 -> 21, of which waited for: 8 -> 7; matrix products, arithmetic and copies ran while one was open for 2% -> 2% of each run, Pallas kernels for 35% -> 35%
where the time goes in v7:
time: 224 us
  waiting for transfers between devices  92.8 us (41%)
  Pallas kernels  82.4 us (37%)
  starting transfers between devices  38.7 us (17%)
  blocking collectives  5.19 us (2%)
  other arithmetic  3.08 us (1%)
    ppermute x21, waiting for transfers between devices, send(): return lax.ppermute(x, 'frame', [(i, i ^ m) for i in range(n)])  92.8 us
    ppermute x21, starting transfers between devices, send(): return lax.ppermute(x, 'frame', [(i, i ^ m) for i in range(n)])  38.7 us
    pallas_call x5, Pallas kernels, spatial_attention(): pl.pallas_call(spatial_kernel, grid=(clips, frames, count), in_specs=[spe...  33.6 us
    pallas_call x5, Pallas kernels, temporal_attention(): pl.pallas_call(functools.partial(temporal_kernel, plan, j), grid_spec=plt...  29.3 us
    pallas_call x5, Pallas kernels, combine(): pl.pallas_call(functools.partial(combine_kernel, plan, j), grid_spec=pltp...  10.6 us
    pallas_call x6, Pallas kernels, pack(): pl.pallas_call(functools.partial(pack_kernel, plan, k, m), grid_spec=pltp...  8.93 us
    all_gather x1, blocking collectives, local(): all_codes = lax.all_gather(codes, 'dp', axis=0, tiled=True)  5.19 us
  transfers between devices with their start and end apart: 21, of which 7 were waited for; matrix products, arithmetic and copies ran while one was open for 2% of the time, Pallas kernels for 35%

profile of v7, /device:TPU:0, one launch (start us, length us, event | category | flops | bytes accessed | tf_op | source)
XLA Modules:
  0.0 223.7 jit_solution(9397324383499929507)
XLA Ops:
  1.9 4.0 %collective-permute-start.1 = (bf16[96,1,16,128]{3,2,1,0:T(8,128)(2,1)}, bf16[96,1,16,128]{3,2,1,0:T(8,128)(2,1)S(1)}, u32[]{:S(2)}, u32[]{:S(2)}) collective-permute-start(bf16[96,1,16,128]{3,2,1,0:T(8,128)(2,1)} %pack.7), channel_id=1, source_target_pairs={{0,4},{2,6},{4,0},{6,2},{1,5},{3,7},{5,1},{7,3},{8,12},{10,14},{12... | collective-permute-start | bytes 1179656 | tf_op jit(solution)/shard_map/ppermute | solution.py:451
  18.2 5.2 %all_gather.3 = f32[4,16,32]{2,1,0:T(8,128)S(1)} all-gather(f32[1,16,32]{2,1,0:T(8,128)S(1)} %copy-done.1), channel_id=1, replica_groups=mesh['dp'=4,'frame'=4,'mp'=2] {'dp'}, dimensions={0}, use_global_device_ids=true | all-gather | bytes 10240 | tf_op jit(solution)/shard_map/all_gather | solution.py:488
  26.3 6.7 %spatial.7.spatial_ref = bf16[1,4,128,512]{3,2,1,0:T(8,128)(2,1)S(1)} custom-call(bf16[6,1,4,128,2560]{4,3,2,1,0:T(8,128)(2,1)} %refs_5_.5, bf16[6,1,4,128,2560]{4,3,2,1,0:T(8,128)(2,1)} %refs_5_.5, bf16[6,1,4,128,2560]{4,3,2,1,0:T(8,128)(2,1)} %refs_5_.5), custom_call_target="tpu_custom_call" | custom-call | flops 134217728 | bytes 2097152 | tf_op jit(solution)/shard_map/spatial/pallas_call | solution.py:50
  34.5 6.9 %collective-permute-done.1.refs_4_ = bf16[96,1,16,128]{3,2,1,0:T(8,128)(2,1)S(1)} collective-permute-done((bf16[96,1,16,128]{3,2,1,0:T(8,128)(2,1)}, bf16[96,1,16,128]{3,2,1,0:T(8,128)(2,1)S(1)}, u32[]{:S(2)}, u32[]{:S(2)}) %collective-permute-start.1) | collective-permute-done | bytes 393248 | tf_op jit(solution)/shard_map/ppermute | solution.py:451
  41.4 2.8 %collective-permute-start.5 = (bf16[96,1,16,128]{3,2,1,0:T(8,128)(2,1)S(1)}, bf16[96,1,16,128]{3,2,1,0:T(8,128)(2,1)S(1)}, u32[]{:S(2)}, u32[]{:S(2)}) collective-permute-start(bf16[96,1,16,128]{3,2,1,0:T(8,128)(2,1)S(1)} %pack.11), channel_id=1, source_target_pairs={{0,6},{2,4},{4,2},{6,0},{1,7},{3,5},{5,3},{7,1},{8,14},{10,12},{12... | collective-permute-start | bytes 1179656 | tf_op jit(solution)/shard_map/ppermute | solution.py:451
  44.2 6.7 %spatial.6.spatial_ref = bf16[1,4,128,512]{3,2,1,0:T(8,128)(2,1)S(1)} custom-call(bf16[6,1,4,128,2560]{4,3,2,1,0:T(8,128)(2,1)} %refs_5_.5, bf16[6,1,4,128,2560]{4,3,2,1,0:T(8,128)(2,1)} %refs_5_.5, bf16[6,1,4,128,2560]{4,3,2,1,0:T(8,128)(2,1)} %refs_5_.5), custom_call_target="tpu_custom_call" | custom-call | flops 134217728 | bytes 2097152 | tf_op jit(solution)/shard_map/spatial/pallas_call | solution.py:50
  51.0 7.7 %temporal.5 = (bf16[32,1,16,128]{3,2,1,0:T(8,128)(2,1)S(1)}, bf16[160,1,16,128]{3,2,1,0:T(8,128)(2,1)S(1)}, bf16[116,1,16,128]{3,2,1,0:T(8,128)(2,1)S(1)}, bf16[116,1,16,128]{3,2,1,0:T(8,128)(2,1)S(1)}) custom-call(s32[1]{0:T(128)} %bitcast.me_ref, s32[16]{0:T(128)S(1)} %convert_reduce_fusion.rank_ref, s32[16]{0:T(128)S(1)} %get-tuple-element.63.alone_ref, ...), custom_call_target="tpu_custom_call" | custom-call | flops 268435456 | bytes 3473408 | tf_op jit(solution)/shard_map/temporal/pallas_call | solution.py:312
  60.4 6.4 %collective-permute-done.4.refs_4_ = bf16[96,1,16,128]{3,2,1,0:T(8,128)(2,1)S(1)} collective-permute-done((bf16[96,1,16,128]{3,2,1,0:T(8,128)(2,1)}, bf16[96,1,16,128]{3,2,1,0:T(8,128)(2,1)S(1)}, u32[]{:S(2)}, u32[]{:S(2)}) %collective-permute-start.4) | collective-permute-done | bytes 393248 | tf_op jit(solution)/shard_map/ppermute | solution.py:451
  66.7 2.8 %collective-permute-start.8 = (bf16[116,1,16,128]{3,2,1,0:T(8,128)(2,1)S(1)}, bf16[116,1,16,128]{3,2,1,0:T(8,128)(2,1)S(1)}, u32[]{:S(2)}, u32[]{:S(2)}) collective-permute-start(bf16[116,1,16,128]{3,2,1,0:T(8,128)(2,1)S(1)} %get-tuple-element.40), channel_id=1, source_target_pairs={{0,6},{2,4},{4,2},{6,0},{1,7},{3,5},{5,3},{7,1},{8,14},{10,12},{12... | collective-permute-start | bytes 1425416 | tf_op jit(solution)/shard_map/ppermute | solution.py:451
  69.6 6.7 %spatial.8.spatial_ref = bf16[1,4,128,512]{3,2,1,0:T(8,128)(2,1)S(1)} custom-call(bf16[6,1,4,128,2560]{4,3,2,1,0:T(8,128)(2,1)} %refs_5_.5, bf16[6,1,4,128,2560]{4,3,2,1,0:T(8,128)(2,1)} %refs_5_.5, bf16[6,1,4,128,2560]{4,3,2,1,0:T(8,128)(2,1)} %refs_5_.5), custom_call_target="tpu_custom_call" | custom-call | flops 134217728 | bytes 2097152 | tf_op jit(solution)/shard_map/spatial/pallas_call | solution.py:50
  76.3 7.5 %temporal.6 = (bf16[32,1,16,128]{3,2,1,0:T(8,128)(2,1)S(1)}, bf16[128,1,16,128]{3,2,1,0:T(8,128)(2,1)S(1)}, bf16[116,1,16,128]{3,2,1,0:T(8,128)(2,1)S(1)}, bf16[116,1,16,128]{3,2,1,0:T(8,128)(2,1)S(1)}) custom-call(s32[1]{0:T(128)} %bitcast.me_ref, s32[16]{0:T(128)S(1)} %convert_reduce_fusion.rank_ref, s32[16]{0:T(128)S(1)} %get-tuple-element.63.alone_ref, ...), custom_call_target="tpu_custom_call" | custom-call | flops 268435456 | bytes 3211264 | tf_op jit(solution)/shard_map/temporal/pallas_call | solution.py:312
  84.7 6.7 %spatial.9.spatial_ref = bf16[1,4,128,512]{3,2,1,0:T(8,128)(2,1)S(1)} custom-call(bf16[6,1,4,128,2560]{4,3,2,1,0:T(8,128)(2,1)} %refs_5_.5, bf16[6,1,4,128,2560]{4,3,2,1,0:T(8,128)(2,1)} %refs_5_.5, bf16[6,1,4,128,2560]{4,3,2,1,0:T(8,128)(2,1)} %refs_5_.5), custom_call_target="tpu_custom_call" | custom-call | flops 134217728 | bytes 2097152 | tf_op jit(solution)/shard_map/spatial/pallas_call | solution.py:50
  92.3 23.7 %collective-permute-done.7.refs_4_.refs_2_ = bf16[116,1,16,128]{3,2,1,0:T(8,128)(2,1)S(1)} collective-permute-done((bf16[116,1,16,128]{3,2,1,0:T(8,128)(2,1)S(1)}, bf16[116,1,16,128]{3,2,1,0:T(8,128)(2,1)S(1)}, u32[]{:S(2)}, u32[]{:S(2)}) %collective-permute-start.7) | collective-permute-done | bytes 475168 | tf_op jit(solution)/shard_map/ppermute | solution.py:451
  116.0 7.7 %temporal.7 = (bf16[32,1,16,128]{3,2,1,0:T(8,128)(2,1)S(1)}, bf16[160,1,16,128]{3,2,1,0:T(8,128)(2,1)S(1)}, bf16[116,1,16,128]{3,2,1,0:T(8,128)(2,1)S(1)}, bf16[116,1,16,128]{3,2,1,0:T(8,128)(2,1)S(1)}) custom-call(s32[1]{0:T(128)} %bitcast.me_ref, s32[16]{0:T(128)S(1)} %convert_reduce_fusion.rank_ref, s32[16]{0:T(128)S(1)} %get-tuple-element.63.alone_ref, ...), custom_call_target="tpu_custom_call" | custom-call | flops 268435456 | bytes 3473408 | tf_op jit(solution)/shard_map/temporal/pallas_call | solution.py:312
  123.8 10.8 %collective-permute-start.12 = (bf16[160,1,16,128]{3,2,1,0:T(8,128)(2,1)S(1)}, bf16[160,1,16,128]{3,2,1,0:T(8,128)(2,1)S(1)}, u32[]{:S(2)}, u32[]{:S(2)}) collective-permute-start(bf16[160,1,16,128]{3,2,1,0:T(8,128)(2,1)S(1)} %get-tuple-element.48), channel_id=1, source_target_pairs={{0,2},{2,0},{4,6},{6,4},{1,3},{3,1},{5,7},{7,5},{8,10},{10,8},{12,... | collective-permute-start | bytes 1966088 | tf_op jit(solution)/shard_map/ppermute | solution.py:451
  134.6 2.8 %collective-permute-start.11 = (bf16[116,1,16,128]{3,2,1,0:T(8,128)(2,1)S(1)}, bf16[116,1,16,128]{3,2,1,0:T(8,128)(2,1)S(1)}, u32[]{:S(2)}, u32[]{:S(2)}) collective-permute-start(bf16[116,1,16,128]{3,2,1,0:T(8,128)(2,1)S(1)} %get-tuple-element.45), channel_id=1, source_target_pairs={{0,6},{2,4},{4,2},{6,0},{1,7},{3,5},{5,3},{7,1},{8,14},{10,12},{12... | collective-permute-start | bytes 1425416 | tf_op jit(solution)/shard_map/ppermute | solution.py:451
  139.2 6.7 %spatial.5.spatial_ref = bf16[1,4,128,512]{3,2,1,0:T(8,128)(2,1)S(1)} custom-call(bf16[6,1,4,128,2560]{4,3,2,1,0:T(8,128)(2,1)} %refs_5_.5, bf16[6,1,4,128,2560]{4,3,2,1,0:T(8,128)(2,1)} %refs_5_.5, bf16[6,1,4,128,2560]{4,3,2,1,0:T(8,128)(2,1)} %refs_5_.5), custom_call_target="tpu_custom_call" | custom-call | flops 134217728 | bytes 2097152 | tf_op jit(solution)/shard_map/spatial/pallas_call | solution.py:50
  145.9 17.3 %collective-permute-done.11.refs_5_.refs_3_ = bf16[116,1,16,128]{3,2,1,0:T(8,128)(2,1)S(1)} collective-permute-done((bf16[116,1,16,128]{3,2,1,0:T(8,128)(2,1)S(1)}, bf16[116,1,16,128]{3,2,1,0:T(8,128)(2,1)S(1)}, u32[]{:S(2)}, u32[]{:S(2)}) %collective-permute-start.11) | collective-permute-done | bytes 475168 | tf_op jit(solution)/shard_map/ppermute | solution.py:451
  163.3 3.1 %temporal.8 = (bf16[32,1,16,128]{3,2,1,0:T(8,128)(2,1)S(1)}, bf16[64,1,16,128]{3,2,1,0:T(8,128)(2,1)S(1)}, bf16[32,1,16,128]{3,2,1,0:T(8,128)(2,1)S(1)}, bf16[32,1,16,128]{3,2,1,0:T(8,128)(2,1)S(1)}) custom-call(s32[1]{0:T(128)} %bitcast.me_ref, s32[16]{0:T(128)S(1)} %convert_reduce_fusion.rank_ref, s32[16]{0:T(128)S(1)} %get-tuple-element.63.alone_ref, ...), custom_call_target="tpu_custom_call" | custom-call | flops 268435456 | bytes 1310720 | tf_op jit(solution)/shard_map/temporal/pallas_call | solution.py:312
  167.5 26.7 %collective-permute-done.13.refs_4_.refs_2_ = bf16[116,1,16,128]{3,2,1,0:T(8,128)(2,1)S(1)} collective-permute-done((bf16[116,1,16,128]{3,2,1,0:T(8,128)(2,1)S(1)}, bf16[116,1,16,128]{3,2,1,0:T(8,128)(2,1)S(1)}, u32[]{:S(2)}, u32[]{:S(2)}) %collective-permute-start.13) | collective-permute-done | bytes 475168 | tf_op jit(solution)/shard_map/ppermute | solution.py:451
  194.2 3.1 %temporal.9 = (bf16[32,1,16,128]{3,2,1,0:T(8,128)(2,1)S(1)}, bf16[64,1,16,128]{3,2,1,0:T(8,128)(2,1)S(1)}, bf16[32,1,16,128]{3,2,1,0:T(8,128)(2,1)S(1)}, bf16[32,1,16,128]{3,2,1,0:T(8,128)(2,1)S(1)}) custom-call(s32[1]{0:T(128)} %bitcast.me_ref, s32[16]{0:T(128)S(1)} %convert_reduce_fusion.rank_ref, s32[16]{0:T(128)S(1)} %get-tuple-element.63.alone_ref, ...), custom_call_target="tpu_custom_call" | custom-call | flops 268435456 | bytes 1310720 | tf_op jit(solution)/shard_map/temporal/pallas_call | solution.py:312
  197.4 9.8 %collective-permute-done.15.refs_2_ = bf16[32,1,16,128]{3,2,1,0:T(8,128)(2,1)S(1)} collective-permute-done((bf16[32,1,16,128]{3,2,1,0:T(8,128)(2,1)S(1)}, bf16[32,1,16,128]{3,2,1,0:T(8,128)(2,1)S(1)}, u32[]{:S(2)}, u32[]{:S(2)}) %collective-permute-start.15) | collective-permute-done | bytes 131104 | tf_op jit(solution)/shard_map/ppermute | solution.py:451
  208.2 2.8 %collective-permute-start.19 = (bf16[32,1,16,128]{3,2,1,0:T(8,128)(2,1)S(1)}, bf16[32,1,16,128]{3,2,1,0:T(8,128)(2,1)S(1)}, u32[]{:S(2)}, u32[]{:S(2)}) collective-permute-start(bf16[32,1,16,128]{3,2,1,0:T(8,128)(2,1)S(1)} %get-tuple-element.59), channel_id=1, source_target_pairs={{0,6},{2,4},{4,2},{6,0},{1,7},{3,5},{5,3},{7,1},{8,14},{10,12},{12... | collective-permute-start | bytes 393224 | tf_op jit(solution)/shard_map/ppermute | solution.py:451
  213.7 2.5 %combine.6.refs_7_ = bf16[1,4,128,2560]{3,2,1,0:T(8,128)(2,1)} custom-call(s32[1]{0:T(128)} %bitcast.me_ref, s32[16]{0:T(128)S(1)} %convert_reduce_fusion.rank_ref, s32[16]{0:T(128)S(1)} %get-tuple-element.63.alone_ref, s32[2]{0:T(128)S(1)} %add_bitcast_fusion.kept_ref, ...), custom_call_target="tpu_custom_call", output_to_operand_aliasing={{}: (12, {})} | custom-call | flops 262144 | bytes 1572864 | tf_op jit(solution)/shard_map/combine/pallas_call | solution.py:415
  (71 shorter events, 35.8 us)
Async XLA Ops:
  0.0 34.2 %copy-start = (f32[32,2560]{1,0:T(8,128)S(1)}, f32[32,2560]{1,0:T(8,128)}, u32[]{:S(2)}) copy-start(f32[32,2560]{1,0:T(8,128)} %param.8) | copy-start | bytes 983044
  1.9 39.6 %collective-permute-start.1 = (bf16[96,1,16,128]{3,2,1,0:T(8,128)(2,1)}, bf16[96,1,16,128]{3,2,1,0:T(8,128)(2,1)S(1)}, u32[]{:S(2)}, u32[]{:S(2)}) collective-permute-start(bf16[96,1,16,128]{3,2,1,0:T(8,128)(2,1)} %pack.7), channel_id=1, source_target_pairs={{0,4},{2,6},{4,0},{6,2},{1,5},{3,7},{5,1},{7,3},{8,12},{10,14},{12... | collective-permute-start | bytes 1179656 | tf_op jit(solution)/shard_map/ppermute | solution.py:451
  7.7 43.2 %collective-permute-start.2 = (bf16[96,1,16,128]{3,2,1,0:T(8,128)(2,1)}, bf16[96,1,16,128]{3,2,1,0:T(8,128)(2,1)}, u32[]{:S(2)}, u32[]{:S(2)}) collective-permute-start(bf16[96,1,16,128]{3,2,1,0:T(8,128)(2,1)} %pack.8), channel_id=1, source_target_pairs={{0,6},{2,4},{4,2},{6,0},{1,7},{3,5},{5,3},{7,1},{8,14},{10,12},{12... | collective-permute-start | bytes 1179656 | tf_op jit(solution)/shard_map/ppermute | solution.py:451
  10.9 55.9 %collective-permute-start.4 = (bf16[96,1,16,128]{3,2,1,0:T(8,128)(2,1)}, bf16[96,1,16,128]{3,2,1,0:T(8,128)(2,1)S(1)}, u32[]{:S(2)}, u32[]{:S(2)}) collective-permute-start(bf16[96,1,16,128]{3,2,1,0:T(8,128)(2,1)} %pack.10), channel_id=1, source_target_pairs={{0,4},{2,6},{4,0},{6,2},{1,5},{3,7},{5,1},{7,3},{8,12},{10,14},{12... | collective-permute-start | bytes 1179656 | tf_op jit(solution)/shard_map/ppermute | solution.py:451
  13.8 4.4 %copy-start.1 = (f32[1,16,32]{2,1,0:T(8,128)S(1)}, f32[1,16,32]{2,1,0:T(8,128)}, u32[]{:S(2)}) copy-start(f32[1,16,32]{2,1,0:T(8,128)} %param.7) | copy-start | bytes 6148
  13.8 9.6 %copy-start.2 = (s32[4]{0:T(128)S(1)}, s32[4]{0:T(128)}, u32[]{:S(2)}) copy-start(s32[4]{0:T(128)} %param.9) | copy-start | bytes 52
  13.8 37.2 %collective-permute-start = (bf16[128,1,16,128]{3,2,1,0:T(8,128)(2,1)S(1)}, bf16[128,1,16,128]{3,2,1,0:T(8,128)(2,1)S(1)}, u32[]{:S(2)}, u32[]{:S(2)}) collective-permute-start(bf16[128,1,16,128]{3,2,1,0:T(8,128)(2,1)S(1)} %pack.6), channel_id=1, source_target_pairs={{0,2},{2,0},{4,6},{6,4},{1,3},{3,1},{5,7},{7,5},{8,10},{10,8},{12,... | collective-permute-start | bytes 1572872 | tf_op jit(solution)/shard_map/ppermute | solution.py:451
  16.4 59.9 %collective-permute-start.3 = (bf16[128,1,16,128]{3,2,1,0:T(8,128)(2,1)S(1)}, bf16[128,1,16,128]{3,2,1,0:T(8,128)(2,1)S(1)}, u32[]{:S(2)}, u32[]{:S(2)}) collective-permute-start(bf16[128,1,16,128]{3,2,1,0:T(8,128)(2,1)S(1)} %pack.9), channel_id=1, source_target_pairs={{0,2},{2,0},{4,6},{6,4},{1,3},{3,1},{5,7},{7,5},{8,10},{10,8},{12,... | collective-permute-start | bytes 1572872 | tf_op jit(solution)/shard_map/ppermute | solution.py:451
  41.4 34.9 %collective-permute-start.5 = (bf16[96,1,16,128]{3,2,1,0:T(8,128)(2,1)S(1)}, bf16[96,1,16,128]{3,2,1,0:T(8,128)(2,1)S(1)}, u32[]{:S(2)}, u32[]{:S(2)}) collective-permute-start(bf16[96,1,16,128]{3,2,1,0:T(8,128)(2,1)S(1)} %pack.11), channel_id=1, source_target_pairs={{0,6},{2,4},{4,2},{6,0},{1,7},{3,5},{5,3},{7,1},{8,14},{10,12},{12... | collective-permute-start | bytes 1179656 | tf_op jit(solution)/shard_map/ppermute | solution.py:451
  58.7 57.3 %collective-permute-start.6 = (bf16[160,1,16,128]{3,2,1,0:T(8,128)(2,1)S(1)}, bf16[160,1,16,128]{3,2,1,0:T(8,128)(2,1)S(1)}, u32[]{:S(2)}, u32[]{:S(2)}) collective-permute-start(bf16[160,1,16,128]{3,2,1,0:T(8,128)(2,1)S(1)} %get-tuple-element.38), channel_id=1, source_target_pairs={{0,2},{2,0},{4,6},{6,4},{1,3},{3,1},{5,7},{7,5},{8,10},{10,8},{12,... | collective-permute-start | bytes 1966088 | tf_op jit(solution)/shard_map/ppermute | solution.py:451
  58.8 57.2 %collective-permute-start.7 = (bf16[116,1,16,128]{3,2,1,0:T(8,128)(2,1)S(1)}, bf16[116,1,16,128]{3,2,1,0:T(8,128)(2,1)S(1)}, u32[]{:S(2)}, u32[]{:S(2)}) collective-permute-start(bf16[116,1,16,128]{3,2,1,0:T(8,128)(2,1)S(1)} %get-tuple-element.39), channel_id=1, source_target_pairs={{0,4},{2,6},{4,0},{6,2},{1,5},{3,7},{5,1},{7,3},{8,12},{10,14},{12... | collective-permute-start | bytes 1425416 | tf_op jit(solution)/shard_map/ppermute | solution.py:451
  66.7 49.3 %collective-permute-start.8 = (bf16[116,1,16,128]{3,2,1,0:T(8,128)(2,1)S(1)}, bf16[116,1,16,128]{3,2,1,0:T(8,128)(2,1)S(1)}, u32[]{:S(2)}, u32[]{:S(2)}) collective-permute-start(bf16[116,1,16,128]{3,2,1,0:T(8,128)(2,1)S(1)} %get-tuple-element.40), channel_id=1, source_target_pairs={{0,6},{2,4},{4,2},{6,0},{1,7},{3,5},{5,3},{7,1},{8,14},{10,12},{12... | collective-permute-start | bytes 1425416 | tf_op jit(solution)/shard_map/ppermute | solution.py:451
  83.8 53.6 %collective-permute-start.10 = (bf16[116,1,16,128]{3,2,1,0:T(8,128)(2,1)S(1)}, bf16[116,1,16,128]{3,2,1,0:T(8,128)(2,1)S(1)}, u32[]{:S(2)}, u32[]{:S(2)}) collective-permute-start(bf16[116,1,16,128]{3,2,1,0:T(8,128)(2,1)S(1)} %get-tuple-element.44), channel_id=1, source_target_pairs={{0,4},{2,6},{4,0},{6,2},{1,5},{3,7},{5,1},{7,3},{8,12},{10,14},{12... | collective-permute-start | bytes 1425416 | tf_op jit(solution)/shard_map/ppermute | solution.py:451
  91.4 71.8 %collective-permute-start.9 = (bf16[128,1,16,128]{3,2,1,0:T(8,128)(2,1)S(1)}, bf16[128,1,16,128]{3,2,1,0:T(8,128)(2,1)S(1)}, u32[]{:S(2)}, u32[]{:S(2)}) collective-permute-start(bf16[128,1,16,128]{3,2,1,0:T(8,128)(2,1)S(1)} %get-tuple-element.43), channel_id=1, source_target_pairs={{0,2},{2,0},{4,6},{6,4},{1,3},{3,1},{5,7},{7,5},{8,10},{10,8},{12,... | collective-permute-start | bytes 1572872 | tf_op jit(solution)/shard_map/ppermute | solution.py:451
  123.8 70.5 %collective-permute-start.12 = (bf16[160,1,16,128]{3,2,1,0:T(8,128)(2,1)S(1)}, bf16[160,1,16,128]{3,2,1,0:T(8,128)(2,1)S(1)}, u32[]{:S(2)}, u32[]{:S(2)}) collective-permute-start(bf16[160,1,16,128]{3,2,1,0:T(8,128)(2,1)S(1)} %get-tuple-element.48), channel_id=1, source_target_pairs={{0,2},{2,0},{4,6},{6,4},{1,3},{3,1},{5,7},{7,5},{8,10},{10,8},{12,... | collective-permute-start | bytes 1966088 | tf_op jit(solution)/shard_map/ppermute | solution.py:451
  134.6 28.7 %collective-permute-start.11 = (bf16[116,1,16,128]{3,2,1,0:T(8,128)(2,1)S(1)}, bf16[116,1,16,128]{3,2,1,0:T(8,128)(2,1)S(1)}, u32[]{:S(2)}, u32[]{:S(2)}) collective-permute-start(bf16[116,1,16,128]{3,2,1,0:T(8,128)(2,1)S(1)} %get-tuple-element.45), channel_id=1, source_target_pairs={{0,6},{2,4},{4,2},{6,0},{1,7},{3,5},{5,3},{7,1},{8,14},{10,12},{12... | collective-permute-start | bytes 1425416 | tf_op jit(solution)/shard_map/ppermute | solution.py:451
  137.4 56.8 %collective-permute-start.13 = (bf16[116,1,16,128]{3,2,1,0:T(8,128)(2,1)S(1)}, bf16[116,1,16,128]{3,2,1,0:T(8,128)(2,1)S(1)}, u32[]{:S(2)}, u32[]{:S(2)}) collective-permute-start(bf16[116,1,16,128]{3,2,1,0:T(8,128)(2,1)S(1)} %get-tuple-element.49), channel_id=1, source_target_pairs={{0,4},{2,6},{4,0},{6,2},{1,5},{3,7},{5,1},{7,3},{8,12},{10,14},{12... | collective-permute-start | bytes 1425416 | tf_op jit(solution)/shard_map/ppermute | solution.py:451
  137.4 56.8 %collective-permute-start.14 = (bf16[116,1,16,128]{3,2,1,0:T(8,128)(2,1)S(1)}, bf16[116,1,16,128]{3,2,1,0:T(8,128)(2,1)S(1)}, u32[]{:S(2)}, u32[]{:S(2)}) collective-permute-start(bf16[116,1,16,128]{3,2,1,0:T(8,128)(2,1)S(1)} %get-tuple-element.50), channel_id=1, source_target_pairs={{0,6},{2,4},{4,2},{6,0},{1,7},{3,5},{5,3},{7,1},{8,14},{10,12},{12... | collective-permute-start | bytes 1425416 | tf_op jit(solution)/shard_map/ppermute | solution.py:451
  166.4 40.8 %collective-permute-start.15 = (bf16[32,1,16,128]{3,2,1,0:T(8,128)(2,1)S(1)}, bf16[32,1,16,128]{3,2,1,0:T(8,128)(2,1)S(1)}, u32[]{:S(2)}, u32[]{:S(2)}) collective-permute-start(bf16[32,1,16,128]{3,2,1,0:T(8,128)(2,1)S(1)} %get-tuple-element.53), channel_id=1, source_target_pairs={{0,4},{2,6},{4,0},{6,2},{1,5},{3,7},{5,1},{7,3},{8,12},{10,14},{12... | collective-permute-start | bytes 393224 | tf_op jit(solution)/shard_map/ppermute | solution.py:451
  166.5 41.7 %collective-permute-start.18 = (bf16[32,1,16,128]{3,2,1,0:T(8,128)(2,1)S(1)}, bf16[32,1,16,128]{3,2,1,0:T(8,128)(2,1)S(1)}, u32[]{:S(2)}, u32[]{:S(2)}) collective-permute-start(bf16[32,1,16,128]{3,2,1,0:T(8,128)(2,1)S(1)} %get-tuple-element.58), channel_id=1, source_target_pairs={{0,6},{2,4},{4,2},{6,0},{1,7},{3,5},{5,3},{7,1},{8,14},{10,12},{12... | collective-permute-start | bytes 393224 | tf_op jit(solution)/shard_map/ppermute | solution.py:451
  194.2 19.5 %collective-permute-start.20 = (bf16[64,1,16,128]{3,2,1,0:T(8,128)(2,1)S(1)}, bf16[64,1,16,128]{3,2,1,0:T(8,128)(2,1)S(1)}, u32[]{:S(2)}, u32[]{:S(2)}) collective-permute-start(bf16[64,1,16,128]{3,2,1,0:T(8,128)(2,1)S(1)} %get-tuple-element.60), channel_id=1, source_target_pairs={{0,2},{2,0},{4,6},{6,4},{1,3},{3,1},{5,7},{7,5},{8,10},{10,8},{12,... | collective-permute-start | bytes 786440 | tf_op jit(solution)/shard_map/ppermute | solution.py:451
  207.2 9.1 %collective-permute-start.16 = (bf16[64,1,16,128]{3,2,1,0:T(8,128)(2,1)S(1)}, bf16[64,1,16,128]{3,2,1,0:T(8,128)(2,1)S(1)}, u32[]{:S(2)}, u32[]{:S(2)}) collective-permute-start(bf16[64,1,16,128]{3,2,1,0:T(8,128)(2,1)S(1)} %get-tuple-element.54), channel_id=1, source_target_pairs={{0,2},{2,0},{4,6},{6,4},{1,3},{3,1},{5,7},{7,5},{8,10},{10,8},{12,... | collective-permute-start | bytes 786440 | tf_op jit(solution)/shard_map/ppermute | solution.py:451
  208.2 12.1 %collective-permute-start.19 = (bf16[32,1,16,128]{3,2,1,0:T(8,128)(2,1)S(1)}, bf16[32,1,16,128]{3,2,1,0:T(8,128)(2,1)S(1)}, u32[]{:S(2)}, u32[]{:S(2)}) collective-permute-start(bf16[32,1,16,128]{3,2,1,0:T(8,128)(2,1)S(1)} %get-tuple-element.59), channel_id=1, source_target_pairs={{0,6},{2,4},{4,2},{6,0},{1,7},{3,5},{5,3},{7,1},{8,14},{10,12},{12... | collective-permute-start | bytes 393224 | tf_op jit(solution)/shard_map/ppermute | solution.py:451
  211.0 11.2 %collective-permute-start.17 = (bf16[32,1,16,128]{3,2,1,0:T(8,128)(2,1)S(1)}, bf16[32,1,16,128]{3,2,1,0:T(8,128)(2,1)S(1)}, u32[]{:S(2)}, u32[]{:S(2)}) collective-permute-start(bf16[32,1,16,128]{3,2,1,0:T(8,128)(2,1)S(1)} %get-tuple-element.56), channel_id=1, source_target_pairs={{0,4},{2,6},{4,0},{6,2},{1,5},{3,7},{5,1},{7,3},{8,12},{10,14},{12... | collective-permute-start | bytes 393224 | tf_op jit(solution)/shard_map/ppermute | solution.py:451
  (2 other events, 7.3 us)

commit v8 on v7

--- a/solution.py
+++ b/solution.py
@@ -12,6 +12,7 @@
 GROUP = 16
 SHARES = (4, 4, 4, 4, 4)
 AHEAD = 2
+LATE = (2,)
 LAST = {1: (2,), 2: (2,), 3: (2, 3)}
 EPISODES = 3
 HIGHEST = lax.Precision.HIGHEST
@@ -83,22 +84,26 @@
         full = self.groups * self.frames
         sizes = {}
         if self.slotted(k) and m > 1:
+            sizes["slots"] = self.heads(k) * self.slots
             sizes["kv"] = 2 * self.heads(k) * full
-            sizes["slots"] = self.heads(k) * self.slots
         else:
+            if self.heads(k - AHEAD):
+                sizes["o"] = self.heads(k - AHEAD) * full
+            if m == 1 and self.slotted(k - AHEAD):
+                sizes["ol"] = 2 * self.heads(k - AHEAD) * self.frames
             if self.heads(k):
                 sizes["qkv"] = 3 * self.heads(k) * full
-            if self.heads(k - AHEAD):
-                sizes["o"] = self.heads(k - AHEAD) * full
             if m == 1 and self.slotted(k + AHEAD):
                 sizes["ql"] = 2 * self.heads(k + AHEAD) * self.frames
-            if m == 1 and self.slotted(k - AHEAD):
-                sizes["ol"] = 2 * self.heads(k - AHEAD) * self.frames
         at, total = {}, 0
         for name, size in sizes.items():
             at[name] = total
             total += size
         return at, total
+
+    def results(self, k, m):
+        at, total = self.parts(k, m)
+        return min([at[x] for x in ("kv", "qkv") if x in at], default=total)
 
     def tile(self, i, g):
         return (i * self.groups + g) * self.frames
@@ -399,11 +404,12 @@
     start, heads = plan.chunks[j]
     count, size, first = pieces(start, heads)
     whole = pl.BlockSpec((1, frames, patches, size * E), lambda c, i, *_: (c, 0, 0, i))
-    arrays, specs = [spatial, own, *back], [whole] + [tiles(x.shape[0]) for x in (own, *back)]
+    arrays, specs = [spatial, own, *back], [whole, tiles(own.shape[0])]
+    specs += [tiles(plan.results(j + AHEAD, m)) for m in range(1, n)]
     if plan.slotted(j + AHEAD):
         arrays += [handed, projected, action]
         specs += [
-            tiles(handed.shape[0]),
+            tiles(plan.results(j + 2 * AHEAD, 1)),
             pl.BlockSpec(
                 (1, 1, frames, patches, size * E), lambda c, i, *_: (5, c, 0, 0, first + i)
             ),
@@ -434,6 +440,51 @@
     )(me, *tables, *arrays)
 
 
+def add_rows_kernel(plan, heads, base, me_ref, spatial_ref, part_ref, *refs):
+    out_ref = refs[-1]
+    for h in range(heads):
+        cut = slice(h * E, (h + 1) * E)
+        for g in range(plan.groups):
+            rows = slice(g * GROUP, (g + 1) * GROUP)
+            to = base + plan.tile(h, g)
+            one, other = spatial_ref[0, :, rows, cut], part_ref[to : to + plan.frames, 0]
+            total = one.astype(jnp.float32) + other.astype(jnp.float32)
+            out_ref[0, :, rows, cut] = total.astype(jnp.bfloat16)
+
+
+def add_rows(plan, mixed, spatial, part, me, j, m):
+    clips, frames, patches, cols = spatial.shape
+    start, heads = plan.chunks[j]
+    rows = patches // plan.n
+    base = plan.parts(j + AHEAD, m)[0]["o"] if m else 0
+    held = base + heads * plan.groups * frames
+    return pl.pallas_call(
+        functools.partial(add_rows_kernel, plan, heads, base),
+        grid_spec=pltpu.PrefetchScalarGridSpec(
+            num_scalar_prefetch=1,
+            grid=(clips,),
+            in_specs=[
+                pl.BlockSpec((1, frames, rows, cols), lambda c, me_ref: (c, 0, me_ref[0] ^ m, 0)),
+                tiles(held),
+                pl.BlockSpec(memory_space=pl.ANY),
+            ],
+            out_specs=pl.BlockSpec(
+                (1, frames, rows, cols),
+                lambda c, me_ref: (c, 0, me_ref[0] ^ m, start // heads),
+            ),
+        ),
+        out_shape=jax.ShapeDtypeStruct(mixed.shape, mixed.dtype),
+        input_output_aliases={3: 0},
+        compiler_params=params(),
+        cost_estimate=pl.CostEstimate(
+            flops=clips * frames * rows * cols,
+            bytes_accessed=6 * clips * frames * rows * cols,
+            transcendentals=0,
+        ),
+        name="add_rows",
+    )(me, spatial, part, mixed)
+
+
 def after(x, *others):
     return lax.optimization_barrier((x, *others))[0]
 
@@ -494,12 +545,22 @@
     )
     action = jnp.einsum("csa,ad->csd", codes_slot, action_weight, precision=HIGHEST)
 
-    spatial, own = [], []
+    spatial, own, mixed = [], [], None
+
+    def add(mixed, j, late=()):
+        back = [own[j] if m in late else arrived[j + AHEAD][m - 1] for m in range(1, n)]
+        handed = arrived[j + 2 * AHEAD][0] if plan.slotted(j + AHEAD) else None
+        return combine(
+            plan, mixed, spatial[j], own[j], back, handed, projected, action, me, tables,
+            j, width,
+        )
+
     for j in range(count):
         for early in plan.chunks[len(spatial) : j + 2]:
             spatial.append(spatial_attention(projected, *early))
+        ready = [*spatial, *own]
         done = temporal_attention(
-            plan, projected, arrived[j], bias, action, after(me, *spatial, *own), tables, j
+            plan, projected, arrived[j], bias, action, after(me, *ready), tables, j
         )
         own.append(done[0])
         outgoing = done[1:]
@@ -508,13 +569,14 @@
             for m, gates in LAST.items():
                 outgoing[m - 1] = after(outgoing[m - 1], *[arrived[-1][g - 1] for g in gates])
         arrived.append(exchange(outgoing))
-    mixed = None
+    last = count - 1
+    start, heads = plan.chunks[last]
+    split = n > max(LATE) and not plan.slotted(last + AHEAD) and start % heads == 0
     for j in range(count):
-        handed = arrived[j + 2 * AHEAD][0] if plan.slotted(j + AHEAD) else None
-        mixed = combine(
-            plan, mixed, spatial[j], own[j], arrived[j + AHEAD], handed, projected, action, me, tables,
-            j, width,
-        )
+        mixed = add(mixed, j, LATE if split and j == last else ())
+    if split:
+        for m in LATE:
+            mixed = add_rows(plan, mixed, spatial[last], arrived[last + AHEAD][m - 1], me, last, m)
     return mixed
 
 

time: 224 us -> 224 us (level)
  transfers between devices with their start and end apart: 21 -> 21, of which waited for: 7 -> 7; matrix products, arithmetic and copies ran while one was open for 2% -> 2% of each run, Pallas kernels for 35% -> 36%
where the time goes in v8:
time: 224 us; the launch traced here: 223 us
  waiting for transfers between devices  91.2 us (41%)
  Pallas kernels  83.3 us (37%)
  starting transfers between devices  38.7 us (17%)
  blocking collectives  5.19 us (2%)
  other arithmetic  3.08 us (1%)
    ppermute x21, waiting for transfers between devices, send(): return lax.ppermute(x, 'frame', [(i, i ^ m) for i in range(n)])  91.2 us
    ppermute x21, starting transfers between devices, send(): return lax.ppermute(x, 'frame', [(i, i ^ m) for i in range(n)])  38.7 us
    pallas_call x5, Pallas kernels, spatial_attention(): pl.pallas_call(spatial_kernel, grid=(clips, frames, count), in_specs=[spe...  33.6 us
    pallas_call x5, Pallas kernels, temporal_attention(): pl.pallas_call(functools.partial(temporal_kernel, plan, j), grid_spec=plt...  29.3 us
    pallas_call x5, Pallas kernels, combine(): pl.pallas_call(functools.partial(combine_kernel, plan, j), grid_spec=pltp...  10.8 us
    pallas_call x6, Pallas kernels, pack(): pl.pallas_call(functools.partial(pack_kernel, plan, k, m), grid_spec=pltp...  8.93 us
    all_gather x1, blocking collectives, local(): all_codes = lax.all_gather(codes, 'dp', axis=0, tiled=True)  5.19 us
  transfers between devices with their start and end apart: 21, of which 7 were waited for; matrix products, arithmetic and copies ran while one was open for 2% of the time, Pallas kernels for 36%

profile of v8, /device:TPU:0, one launch (start us, length us, event | category | flops | bytes accessed | tf_op | source)
XLA Modules:
  0.0 222.9 jit_solution(2127422445335972776)
XLA Ops:
  1.9 4.0 %collective-permute-start.1 = (bf16[96,1,16,128]{3,2,1,0:T(8,128)(2,1)}, bf16[96,1,16,128]{3,2,1,0:T(8,128)(2,1)S(1)}, u32[]{:S(2)}, u32[]{:S(2)}) collective-permute-start(bf16[96,1,16,128]{3,2,1,0:T(8,128)(2,1)} %pack.7), channel_id=1, source_target_pairs={{0,4},{2,6},{4,0},{6,2},{1,5},{3,7},{5,1},{7,3},{8,12},{10,14},{12... | collective-permute-start | bytes 1179656 | tf_op jit(solution)/shard_map/ppermute | solution.py:502
  18.2 5.2 %all_gather.3 = f32[4,16,32]{2,1,0:T(8,128)S(1)} all-gather(f32[1,16,32]{2,1,0:T(8,128)S(1)} %copy-done.1), channel_id=1, replica_groups=mesh['dp'=4,'frame'=4,'mp'=2] {'dp'}, dimensions={0}, use_global_device_ids=true | all-gather | bytes 10240 | tf_op jit(solution)/shard_map/all_gather | solution.py:539
  26.3 6.7 %spatial.7.spatial_ref = bf16[1,4,128,512]{3,2,1,0:T(8,128)(2,1)S(1)} custom-call(bf16[6,1,4,128,2560]{4,3,2,1,0:T(8,128)(2,1)} %refs_5_.5, bf16[6,1,4,128,2560]{4,3,2,1,0:T(8,128)(2,1)} %refs_5_.5, bf16[6,1,4,128,2560]{4,3,2,1,0:T(8,128)(2,1)} %refs_5_.5), custom_call_target="tpu_custom_call" | custom-call | flops 134217728 | bytes 2097152 | tf_op jit(solution)/shard_map/spatial/pallas_call | solution.py:51
  34.5 6.9 %collective-permute-done.1.refs_4_ = bf16[96,1,16,128]{3,2,1,0:T(8,128)(2,1)S(1)} collective-permute-done((bf16[96,1,16,128]{3,2,1,0:T(8,128)(2,1)}, bf16[96,1,16,128]{3,2,1,0:T(8,128)(2,1)S(1)}, u32[]{:S(2)}, u32[]{:S(2)}) %collective-permute-start.1) | collective-permute-done | bytes 393248 | tf_op jit(solution)/shard_map/ppermute | solution.py:502
  41.4 2.8 %collective-permute-start.5 = (bf16[96,1,16,128]{3,2,1,0:T(8,128)(2,1)S(1)}, bf16[96,1,16,128]{3,2,1,0:T(8,128)(2,1)S(1)}, u32[]{:S(2)}, u32[]{:S(2)}) collective-permute-start(bf16[96,1,16,128]{3,2,1,0:T(8,128)(2,1)S(1)} %pack.11), channel_id=1, source_target_pairs={{0,6},{2,4},{4,2},{6,0},{1,7},{3,5},{5,3},{7,1},{8,14},{10,12},{12... | collective-permute-start | bytes 1179656 | tf_op jit(solution)/shard_map/ppermute | solution.py:502
  44.2 6.7 %spatial.6.spatial_ref = bf16[1,4,128,512]{3,2,1,0:T(8,128)(2,1)S(1)} custom-call(bf16[6,1,4,128,2560]{4,3,2,1,0:T(8,128)(2,1)} %refs_5_.5, bf16[6,1,4,128,2560]{4,3,2,1,0:T(8,128)(2,1)} %refs_5_.5, bf16[6,1,4,128,2560]{4,3,2,1,0:T(8,128)(2,1)} %refs_5_.5), custom_call_target="tpu_custom_call" | custom-call | flops 134217728 | bytes 2097152 | tf_op jit(solution)/shard_map/spatial/pallas_call | solution.py:51
  51.0 7.7 %temporal.5 = (bf16[32,1,16,128]{3,2,1,0:T(8,128)(2,1)S(1)}, bf16[160,1,16,128]{3,2,1,0:T(8,128)(2,1)S(1)}, bf16[116,1,16,128]{3,2,1,0:T(8,128)(2,1)S(1)}, bf16[116,1,16,128]{3,2,1,0:T(8,128)(2,1)S(1)}) custom-call(s32[1]{0:T(128)} %bitcast.me_ref, s32[16]{0:T(128)S(1)} %convert_reduce_fusion.rank_ref, s32[16]{0:T(128)S(1)} %get-tuple-element.63.alone_ref, ...), custom_call_target="tpu_custom_call" | custom-call | flops 268435456 | bytes 3473408 | tf_op jit(solution)/shard_map/temporal/pallas_call | solution.py:317
  60.4 6.4 %collective-permute-done.4.refs_4_ = bf16[96,1,16,128]{3,2,1,0:T(8,128)(2,1)S(1)} collective-permute-done((bf16[96,1,16,128]{3,2,1,0:T(8,128)(2,1)}, bf16[96,1,16,128]{3,2,1,0:T(8,128)(2,1)S(1)}, u32[]{:S(2)}, u32[]{:S(2)}) %collective-permute-start.4) | collective-permute-done | bytes 393248 | tf_op jit(solution)/shard_map/ppermute | solution.py:502
  66.7 2.8 %collective-permute-start.8 = (bf16[116,1,16,128]{3,2,1,0:T(8,128)(2,1)S(1)}, bf16[116,1,16,128]{3,2,1,0:T(8,128)(2,1)S(1)}, u32[]{:S(2)}, u32[]{:S(2)}) collective-permute-start(bf16[116,1,16,128]{3,2,1,0:T(8,128)(2,1)S(1)} %get-tuple-element.40), channel_id=1, source_target_pairs={{0,6},{2,4},{4,2},{6,0},{1,7},{3,5},{5,3},{7,1},{8,14},{10,12},{12... | collective-permute-start | bytes 1425416 | tf_op jit(solution)/shard_map/ppermute | solution.py:502
  69.6 6.7 %spatial.8.spatial_ref = bf16[1,4,128,512]{3,2,1,0:T(8,128)(2,1)S(1)} custom-call(bf16[6,1,4,128,2560]{4,3,2,1,0:T(8,128)(2,1)} %refs_5_.5, bf16[6,1,4,128,2560]{4,3,2,1,0:T(8,128)(2,1)} %refs_5_.5, bf16[6,1,4,128,2560]{4,3,2,1,0:T(8,128)(2,1)} %refs_5_.5), custom_call_target="tpu_custom_call" | custom-call | flops 134217728 | bytes 2097152 | tf_op jit(solution)/shard_map/spatial/pallas_call | solution.py:51
  76.3 7.5 %temporal.6 = (bf16[32,1,16,128]{3,2,1,0:T(8,128)(2,1)S(1)}, bf16[128,1,16,128]{3,2,1,0:T(8,128)(2,1)S(1)}, bf16[116,1,16,128]{3,2,1,0:T(8,128)(2,1)S(1)}, bf16[116,1,16,128]{3,2,1,0:T(8,128)(2,1)S(1)}) custom-call(s32[1]{0:T(128)} %bitcast.me_ref, s32[16]{0:T(128)S(1)} %convert_reduce_fusion.rank_ref, s32[16]{0:T(128)S(1)} %get-tuple-element.63.alone_ref, ...), custom_call_target="tpu_custom_call" | custom-call | flops 268435456 | bytes 3211264 | tf_op jit(solution)/shard_map/temporal/pallas_call | solution.py:317
  84.7 6.7 %spatial.9.spatial_ref = bf16[1,4,128,512]{3,2,1,0:T(8,128)(2,1)S(1)} custom-call(bf16[6,1,4,128,2560]{4,3,2,1,0:T(8,128)(2,1)} %refs_5_.5, bf16[6,1,4,128,2560]{4,3,2,1,0:T(8,128)(2,1)} %refs_5_.5, bf16[6,1,4,128,2560]{4,3,2,1,0:T(8,128)(2,1)} %refs_5_.5), custom_call_target="tpu_custom_call" | custom-call | flops 134217728 | bytes 2097152 | tf_op jit(solution)/shard_map/spatial/pallas_call | solution.py:51
  92.3 23.7 %collective-permute-done.7.refs_4_.refs_2_ = bf16[116,1,16,128]{3,2,1,0:T(8,128)(2,1)S(1)} collective-permute-done((bf16[116,1,16,128]{3,2,1,0:T(8,128)(2,1)S(1)}, bf16[116,1,16,128]{3,2,1,0:T(8,128)(2,1)S(1)}, u32[]{:S(2)}, u32[]{:S(2)}) %collective-permute-start.7) | collective-permute-done | bytes 475168 | tf_op jit(solution)/shard_map/ppermute | solution.py:502
  116.0 7.7 %temporal.7 = (bf16[32,1,16,128]{3,2,1,0:T(8,128)(2,1)S(1)}, bf16[160,1,16,128]{3,2,1,0:T(8,128)(2,1)S(1)}, bf16[116,1,16,128]{3,2,1,0:T(8,128)(2,1)S(1)}, bf16[116,1,16,128]{3,2,1,0:T(8,128)(2,1)S(1)}) custom-call(s32[1]{0:T(128)} %bitcast.me_ref, s32[16]{0:T(128)S(1)} %convert_reduce_fusion.rank_ref, s32[16]{0:T(128)S(1)} %get-tuple-element.63.alone_ref, ...), custom_call_target="tpu_custom_call" | custom-call | flops 268435456 | bytes 3473408 | tf_op jit(solution)/shard_map/temporal/pallas_call | solution.py:317
  123.8 10.8 %collective-permute-start.12 = (bf16[160,1,16,128]{3,2,1,0:T(8,128)(2,1)S(1)}, bf16[160,1,16,128]{3,2,1,0:T(8,128)(2,1)S(1)}, u32[]{:S(2)}, u32[]{:S(2)}) collective-permute-start(bf16[160,1,16,128]{3,2,1,0:T(8,128)(2,1)S(1)} %get-tuple-element.48), channel_id=1, source_target_pairs={{0,2},{2,0},{4,6},{6,4},{1,3},{3,1},{5,7},{7,5},{8,10},{10,8},{12,... | collective-permute-start | bytes 1966088 | tf_op jit(solution)/shard_map/ppermute | solution.py:502
  134.6 2.8 %collective-permute-start.11 = (bf16[116,1,16,128]{3,2,1,0:T(8,128)(2,1)S(1)}, bf16[116,1,16,128]{3,2,1,0:T(8,128)(2,1)S(1)}, u32[]{:S(2)}, u32[]{:S(2)}) collective-permute-start(bf16[116,1,16,128]{3,2,1,0:T(8,128)(2,1)S(1)} %get-tuple-element.45), channel_id=1, source_target_pairs={{0,6},{2,4},{4,2},{6,0},{1,7},{3,5},{5,3},{7,1},{8,14},{10,12},{12... | collective-permute-start | bytes 1425416 | tf_op jit(solution)/shard_map/ppermute | solution.py:502
  139.2 6.7 %spatial.5.spatial_ref = bf16[1,4,128,512]{3,2,1,0:T(8,128)(2,1)S(1)} custom-call(bf16[6,1,4,128,2560]{4,3,2,1,0:T(8,128)(2,1)} %refs_5_.5, bf16[6,1,4,128,2560]{4,3,2,1,0:T(8,128)(2,1)} %refs_5_.5, bf16[6,1,4,128,2560]{4,3,2,1,0:T(8,128)(2,1)} %refs_5_.5), custom_call_target="tpu_custom_call" | custom-call | flops 134217728 | bytes 2097152 | tf_op jit(solution)/shard_map/spatial/pallas_call | solution.py:51
  145.9 17.3 %collective-permute-done.11.refs_5_.refs_3_ = bf16[116,1,16,128]{3,2,1,0:T(8,128)(2,1)S(1)} collective-permute-done((bf16[116,1,16,128]{3,2,1,0:T(8,128)(2,1)S(1)}, bf16[116,1,16,128]{3,2,1,0:T(8,128)(2,1)S(1)}, u32[]{:S(2)}, u32[]{:S(2)}) %collective-permute-start.11) | collective-permute-done | bytes 475168 | tf_op jit(solution)/shard_map/ppermute | solution.py:502
  163.3 3.1 %temporal.8 = (bf16[32,1,16,128]{3,2,1,0:T(8,128)(2,1)S(1)}, bf16[64,1,16,128]{3,2,1,0:T(8,128)(2,1)S(1)}, bf16[32,1,16,128]{3,2,1,0:T(8,128)(2,1)S(1)}, bf16[32,1,16,128]{3,2,1,0:T(8,128)(2,1)S(1)}) custom-call(s32[1]{0:T(128)} %bitcast.me_ref, s32[16]{0:T(128)S(1)} %convert_reduce_fusion.rank_ref, s32[16]{0:T(128)S(1)} %get-tuple-element.63.alone_ref, ...), custom_call_target="tpu_custom_call" | custom-call | flops 268435456 | bytes 1310720 | tf_op jit(solution)/shard_map/temporal/pallas_call | solution.py:317
  167.5 26.7 %collective-permute-done.13.refs_4_.refs_2_ = bf16[116,1,16,128]{3,2,1,0:T(8,128)(2,1)S(1)} collective-permute-done((bf16[116,1,16,128]{3,2,1,0:T(8,128)(2,1)S(1)}, bf16[116,1,16,128]{3,2,1,0:T(8,128)(2,1)S(1)}, u32[]{:S(2)}, u32[]{:S(2)}) %collective-permute-start.13) | collective-permute-done | bytes 475168 | tf_op jit(solution)/shard_map/ppermute | solution.py:502
  194.2 3.1 %temporal.9 = (bf16[32,1,16,128]{3,2,1,0:T(8,128)(2,1)S(1)}, bf16[64,1,16,128]{3,2,1,0:T(8,128)(2,1)S(1)}, bf16[32,1,16,128]{3,2,1,0:T(8,128)(2,1)S(1)}, bf16[32,1,16,128]{3,2,1,0:T(8,128)(2,1)S(1)}) custom-call(s32[1]{0:T(128)} %bitcast.me_ref, s32[16]{0:T(128)S(1)} %convert_reduce_fusion.rank_ref, s32[16]{0:T(128)S(1)} %get-tuple-element.63.alone_ref, ...), custom_call_target="tpu_custom_call" | custom-call | flops 268435456 | bytes 1310720 | tf_op jit(solution)/shard_map/temporal/pallas_call | solution.py:317
  197.4 9.8 %collective-permute-done.15.refs_2_ = bf16[32,1,16,128]{3,2,1,0:T(8,128)(2,1)S(1)} collective-permute-done((bf16[32,1,16,128]{3,2,1,0:T(8,128)(2,1)S(1)}, bf16[32,1,16,128]{3,2,1,0:T(8,128)(2,1)S(1)}, u32[]{:S(2)}, u32[]{:S(2)}) %collective-permute-start.15) | collective-permute-done | bytes 131104 | tf_op jit(solution)/shard_map/ppermute | solution.py:502
  208.2 2.8 %collective-permute-start.19 = (bf16[32,1,16,128]{3,2,1,0:T(8,128)(2,1)S(1)}, bf16[32,1,16,128]{3,2,1,0:T(8,128)(2,1)S(1)}, u32[]{:S(2)}, u32[]{:S(2)}) collective-permute-start(bf16[32,1,16,128]{3,2,1,0:T(8,128)(2,1)S(1)} %get-tuple-element.59), channel_id=1, source_target_pairs={{0,6},{2,4},{4,2},{6,0},{1,7},{3,5},{5,3},{7,1},{8,14},{10,12},{12... | collective-permute-start | bytes 393224 | tf_op jit(solution)/shard_map/ppermute | solution.py:502
  213.8 2.6 %combine.6.refs_7_ = bf16[1,4,128,2560]{3,2,1,0:T(8,128)(2,1)} custom-call(s32[1]{0:T(128)} %bitcast.me_ref, s32[16]{0:T(128)S(1)} %convert_reduce_fusion.rank_ref, s32[16]{0:T(128)S(1)} %get-tuple-element.63.alone_ref, s32[2]{0:T(128)S(1)} %add_bitcast_fusion.kept_ref, ...), custom_call_target="tpu_custom_call", output_to_operand_aliasing={{}: (12, {})} | custom-call | flops 262144 | bytes 1572864 | tf_op jit(solution)/shard_map/combine/pallas_call | solution.py:421
  (72 shorter events, 35.0 us)
Async XLA Ops:
  0.0 34.2 %copy-start = (f32[32,2560]{1,0:T(8,128)S(1)}, f32[32,2560]{1,0:T(8,128)}, u32[]{:S(2)}) copy-start(f32[32,2560]{1,0:T(8,128)} %param.8) | copy-start | bytes 983044
  1.9 39.6 %collective-permute-start.1 = (bf16[96,1,16,128]{3,2,1,0:T(8,128)(2,1)}, bf16[96,1,16,128]{3,2,1,0:T(8,128)(2,1)S(1)}, u32[]{:S(2)}, u32[]{:S(2)}) collective-permute-start(bf16[96,1,16,128]{3,2,1,0:T(8,128)(2,1)} %pack.7), channel_id=1, source_target_pairs={{0,4},{2,6},{4,0},{6,2},{1,5},{3,7},{5,1},{7,3},{8,12},{10,14},{12... | collective-permute-start | bytes 1179656 | tf_op jit(solution)/shard_map/ppermute | solution.py:502
  7.7 43.2 %collective-permute-start.2 = (bf16[96,1,16,128]{3,2,1,0:T(8,128)(2,1)}, bf16[96,1,16,128]{3,2,1,0:T(8,128)(2,1)}, u32[]{:S(2)}, u32[]{:S(2)}) collective-permute-start(bf16[96,1,16,128]{3,2,1,0:T(8,128)(2,1)} %pack.8), channel_id=1, source_target_pairs={{0,6},{2,4},{4,2},{6,0},{1,7},{3,5},{5,3},{7,1},{8,14},{10,12},{12... | collective-permute-start | bytes 1179656 | tf_op jit(solution)/shard_map/ppermute | solution.py:502
  10.9 55.9 %collective-permute-start.4 = (bf16[96,1,16,128]{3,2,1,0:T(8,128)(2,1)}, bf16[96,1,16,128]{3,2,1,0:T(8,128)(2,1)S(1)}, u32[]{:S(2)}, u32[]{:S(2)}) collective-permute-start(bf16[96,1,16,128]{3,2,1,0:T(8,128)(2,1)} %pack.10), channel_id=1, source_target_pairs={{0,4},{2,6},{4,0},{6,2},{1,5},{3,7},{5,1},{7,3},{8,12},{10,14},{12... | collective-permute-start | bytes 1179656 | tf_op jit(solution)/shard_map/ppermute | solution.py:502
  13.8 4.4 %copy-start.1 = (f32[1,16,32]{2,1,0:T(8,128)S(1)}, f32[1,16,32]{2,1,0:T(8,128)}, u32[]{:S(2)}) copy-start(f32[1,16,32]{2,1,0:T(8,128)} %param.7) | copy-start | bytes 6148
  13.8 9.6 %copy-start.2 = (s32[4]{0:T(128)S(1)}, s32[4]{0:T(128)}, u32[]{:S(2)}) copy-start(s32[4]{0:T(128)} %param.9) | copy-start | bytes 52
  13.8 37.2 %collective-permute-start = (bf16[128,1,16,128]{3,2,1,0:T(8,128)(2,1)S(1)}, bf16[128,1,16,128]{3,2,1,0:T(8,128)(2,1)S(1)}, u32[]{:S(2)}, u32[]{:S(2)}) collective-permute-start(bf16[128,1,16,128]{3,2,1,0:T(8,128)(2,1)S(1)} %pack.6), channel_id=1, source_target_pairs={{0,2},{2,0},{4,6},{6,4},{1,3},{3,1},{5,7},{7,5},{8,10},{10,8},{12,... | collective-permute-start | bytes 1572872 | tf_op jit(solution)/shard_map/ppermute | solution.py:502
  16.4 59.9 %collective-permute-start.3 = (bf16[128,1,16,128]{3,2,1,0:T(8,128)(2,1)S(1)}, bf16[128,1,16,128]{3,2,1,0:T(8,128)(2,1)S(1)}, u32[]{:S(2)}, u32[]{:S(2)}) collective-permute-start(bf16[128,1,16,128]{3,2,1,0:T(8,128)(2,1)S(1)} %pack.9), channel_id=1, source_target_pairs={{0,2},{2,0},{4,6},{6,4},{1,3},{3,1},{5,7},{7,5},{8,10},{10,8},{12,... | collective-permute-start | bytes 1572872 | tf_op jit(solution)/shard_map/ppermute | solution.py:502
  41.4 34.9 %collective-permute-start.5 = (bf16[96,1,16,128]{3,2,1,0:T(8,128)(2,1)S(1)}, bf16[96,1,16,128]{3,2,1,0:T(8,128)(2,1)S(1)}, u32[]{:S(2)}, u32[]{:S(2)}) collective-permute-start(bf16[96,1,16,128]{3,2,1,0:T(8,128)(2,1)S(1)} %pack.11), channel_id=1, source_target_pairs={{0,6},{2,4},{4,2},{6,0},{1,7},{3,5},{5,3},{7,1},{8,14},{10,12},{12... | collective-permute-start | bytes 1179656 | tf_op jit(solution)/shard_map/ppermute | solution.py:502
  58.7 57.3 %collective-permute-start.6 = (bf16[160,1,16,128]{3,2,1,0:T(8,128)(2,1)S(1)}, bf16[160,1,16,128]{3,2,1,0:T(8,128)(2,1)S(1)}, u32[]{:S(2)}, u32[]{:S(2)}) collective-permute-start(bf16[160,1,16,128]{3,2,1,0:T(8,128)(2,1)S(1)} %get-tuple-element.38), channel_id=1, source_target_pairs={{0,2},{2,0},{4,6},{6,4},{1,3},{3,1},{5,7},{7,5},{8,10},{10,8},{12,... | collective-permute-start | bytes 1966088 | tf_op jit(solution)/shard_map/ppermute | solution.py:502
  58.8 57.2 %collective-permute-start.7 = (bf16[116,1,16,128]{3,2,1,0:T(8,128)(2,1)S(1)}, bf16[116,1,16,128]{3,2,1,0:T(8,128)(2,1)S(1)}, u32[]{:S(2)}, u32[]{:S(2)}) collective-permute-start(bf16[116,1,16,128]{3,2,1,0:T(8,128)(2,1)S(1)} %get-tuple-element.39), channel_id=1, source_target_pairs={{0,4},{2,6},{4,0},{6,2},{1,5},{3,7},{5,1},{7,3},{8,12},{10,14},{12... | collective-permute-start | bytes 1425416 | tf_op jit(solution)/shard_map/ppermute | solution.py:502
  66.7 49.3 %collective-permute-start.8 = (bf16[116,1,16,128]{3,2,1,0:T(8,128)(2,1)S(1)}, bf16[116,1,16,128]{3,2,1,0:T(8,128)(2,1)S(1)}, u32[]{:S(2)}, u32[]{:S(2)}) collective-permute-start(bf16[116,1,16,128]{3,2,1,0:T(8,128)(2,1)S(1)} %get-tuple-element.40), channel_id=1, source_target_pairs={{0,6},{2,4},{4,2},{6,0},{1,7},{3,5},{5,3},{7,1},{8,14},{10,12},{12... | collective-permute-start | bytes 1425416 | tf_op jit(solution)/shard_map/ppermute | solution.py:502
  83.8 53.6 %collective-permute-start.10 = (bf16[116,1,16,128]{3,2,1,0:T(8,128)(2,1)S(1)}, bf16[116,1,16,128]{3,2,1,0:T(8,128)(2,1)S(1)}, u32[]{:S(2)}, u32[]{:S(2)}) collective-permute-start(bf16[116,1,16,128]{3,2,1,0:T(8,128)(2,1)S(1)} %get-tuple-element.44), channel_id=1, source_target_pairs={{0,4},{2,6},{4,0},{6,2},{1,5},{3,7},{5,1},{7,3},{8,12},{10,14},{12... | collective-permute-start | bytes 1425416 | tf_op jit(solution)/shard_map/ppermute | solution.py:502
  91.4 71.8 %collective-permute-start.9 = (bf16[128,1,16,128]{3,2,1,0:T(8,128)(2,1)S(1)}, bf16[128,1,16,128]{3,2,1,0:T(8,128)(2,1)S(1)}, u32[]{:S(2)}, u32[]{:S(2)}) collective-permute-start(bf16[128,1,16,128]{3,2,1,0:T(8,128)(2,1)S(1)} %get-tuple-element.43), channel_id=1, source_target_pairs={{0,2},{2,0},{4,6},{6,4},{1,3},{3,1},{5,7},{7,5},{8,10},{10,8},{12,... | collective-permute-start | bytes 1572872 | tf_op jit(solution)/shard_map/ppermute | solution.py:502
  123.8 70.5 %collective-permute-start.12 = (bf16[160,1,16,128]{3,2,1,0:T(8,128)(2,1)S(1)}, bf16[160,1,16,128]{3,2,1,0:T(8,128)(2,1)S(1)}, u32[]{:S(2)}, u32[]{:S(2)}) collective-permute-start(bf16[160,1,16,128]{3,2,1,0:T(8,128)(2,1)S(1)} %get-tuple-element.48), channel_id=1, source_target_pairs={{0,2},{2,0},{4,6},{6,4},{1,3},{3,1},{5,7},{7,5},{8,10},{10,8},{12,... | collective-permute-start | bytes 1966088 | tf_op jit(solution)/shard_map/ppermute | solution.py:502
  134.6 28.7 %collective-permute-start.11 = (bf16[116,1,16,128]{3,2,1,0:T(8,128)(2,1)S(1)}, bf16[116,1,16,128]{3,2,1,0:T(8,128)(2,1)S(1)}, u32[]{:S(2)}, u32[]{:S(2)}) collective-permute-start(bf16[116,1,16,128]{3,2,1,0:T(8,128)(2,1)S(1)} %get-tuple-element.45), channel_id=1, source_target_pairs={{0,6},{2,4},{4,2},{6,0},{1,7},{3,5},{5,3},{7,1},{8,14},{10,12},{12... | collective-permute-start | bytes 1425416 | tf_op jit(solution)/shard_map/ppermute | solution.py:502
  137.4 56.8 %collective-permute-start.13 = (bf16[116,1,16,128]{3,2,1,0:T(8,128)(2,1)S(1)}, bf16[116,1,16,128]{3,2,1,0:T(8,128)(2,1)S(1)}, u32[]{:S(2)}, u32[]{:S(2)}) collective-permute-start(bf16[116,1,16,128]{3,2,1,0:T(8,128)(2,1)S(1)} %get-tuple-element.49), channel_id=1, source_target_pairs={{0,4},{2,6},{4,0},{6,2},{1,5},{3,7},{5,1},{7,3},{8,12},{10,14},{12... | collective-permute-start | bytes 1425416 | tf_op jit(solution)/shard_map/ppermute | solution.py:502
  137.4 56.8 %collective-permute-start.14 = (bf16[116,1,16,128]{3,2,1,0:T(8,128)(2,1)S(1)}, bf16[116,1,16,128]{3,2,1,0:T(8,128)(2,1)S(1)}, u32[]{:S(2)}, u32[]{:S(2)}) collective-permute-start(bf16[116,1,16,128]{3,2,1,0:T(8,128)(2,1)S(1)} %get-tuple-element.50), channel_id=1, source_target_pairs={{0,6},{2,4},{4,2},{6,0},{1,7},{3,5},{5,3},{7,1},{8,14},{10,12},{12... | collective-permute-start | bytes 1425416 | tf_op jit(solution)/shard_map/ppermute | solution.py:502
  166.4 40.8 %collective-permute-start.15 = (bf16[32,1,16,128]{3,2,1,0:T(8,128)(2,1)S(1)}, bf16[32,1,16,128]{3,2,1,0:T(8,128)(2,1)S(1)}, u32[]{:S(2)}, u32[]{:S(2)}) collective-permute-start(bf16[32,1,16,128]{3,2,1,0:T(8,128)(2,1)S(1)} %get-tuple-element.52), channel_id=1, source_target_pairs={{0,4},{2,6},{4,0},{6,2},{1,5},{3,7},{5,1},{7,3},{8,12},{10,14},{12... | collective-permute-start | bytes 393224 | tf_op jit(solution)/shard_map/ppermute | solution.py:502
  166.5 41.7 %collective-permute-start.18 = (bf16[32,1,16,128]{3,2,1,0:T(8,128)(2,1)S(1)}, bf16[32,1,16,128]{3,2,1,0:T(8,128)(2,1)S(1)}, u32[]{:S(2)}, u32[]{:S(2)}) collective-permute-start(bf16[32,1,16,128]{3,2,1,0:T(8,128)(2,1)S(1)} %get-tuple-element.58), channel_id=1, source_target_pairs={{0,6},{2,4},{4,2},{6,0},{1,7},{3,5},{5,3},{7,1},{8,14},{10,12},{12... | collective-permute-start | bytes 393224 | tf_op jit(solution)/shard_map/ppermute | solution.py:502
  194.2 19.6 %collective-permute-start.20 = (bf16[64,1,16,128]{3,2,1,0:T(8,128)(2,1)S(1)}, bf16[64,1,16,128]{3,2,1,0:T(8,128)(2,1)S(1)}, u32[]{:S(2)}, u32[]{:S(2)}) collective-permute-start(bf16[64,1,16,128]{3,2,1,0:T(8,128)(2,1)S(1)} %get-tuple-element.60), channel_id=1, source_target_pairs={{0,2},{2,0},{4,6},{6,4},{1,3},{3,1},{5,7},{7,5},{8,10},{10,8},{12,... | collective-permute-start | bytes 786440 | tf_op jit(solution)/shard_map/ppermute | solution.py:502
  207.2 9.2 %collective-permute-start.17 = (bf16[64,1,16,128]{3,2,1,0:T(8,128)(2,1)S(1)}, bf16[64,1,16,128]{3,2,1,0:T(8,128)(2,1)S(1)}, u32[]{:S(2)}, u32[]{:S(2)}) collective-permute-start(bf16[64,1,16,128]{3,2,1,0:T(8,128)(2,1)S(1)} %get-tuple-element.56), channel_id=1, source_target_pairs={{0,2},{2,0},{4,6},{6,4},{1,3},{3,1},{5,7},{7,5},{8,10},{10,8},{12,... | collective-permute-start | bytes 786440 | tf_op jit(solution)/shard_map/ppermute | solution.py:502
  208.2 12.3 %collective-permute-start.19 = (bf16[32,1,16,128]{3,2,1,0:T(8,128)(2,1)S(1)}, bf16[32,1,16,128]{3,2,1,0:T(8,128)(2,1)S(1)}, u32[]{:S(2)}, u32[]{:S(2)}) collective-permute-start(bf16[32,1,16,128]{3,2,1,0:T(8,128)(2,1)S(1)} %get-tuple-element.59), channel_id=1, source_target_pairs={{0,6},{2,4},{4,2},{6,0},{1,7},{3,5},{5,3},{7,1},{8,14},{10,12},{12... | collective-permute-start | bytes 393224 | tf_op jit(solution)/shard_map/ppermute | solution.py:502
  211.0 11.2 %collective-permute-start.16 = (bf16[32,1,16,128]{3,2,1,0:T(8,128)(2,1)S(1)}, bf16[32,1,16,128]{3,2,1,0:T(8,128)(2,1)S(1)}, u32[]{:S(2)}, u32[]{:S(2)}) collective-permute-start(bf16[32,1,16,128]{3,2,1,0:T(8,128)(2,1)S(1)} %get-tuple-element.53), channel_id=1, source_target_pairs={{0,4},{2,6},{4,0},{6,2},{1,5},{3,7},{5,1},{7,3},{8,12},{10,14},{12... | collective-permute-start | bytes 393224 | tf_op jit(solution)/shard_map/ppermute | solution.py:502
  (2 other events, 7.3 us)

commit v9 on v8

--- a/solution.py
+++ b/solution.py
@@ -13,7 +13,7 @@
 SHARES = (4, 4, 4, 4, 4)
 AHEAD = 2
 LATE = (2,)
-LAST = {1: (2,), 2: (2,), 3: (2, 3)}
+LAST = {1: (2,), 3: (2, 3)}
 EPISODES = 3
 HIGHEST = lax.Precision.HIGHEST
 VMEM = 48 * 1024 * 1024

time: 224 us -> 224 us (level)
  no operation moved by 1% of the time
where the time goes in v9:
time: 224 us; the launch traced here: 223 us
  waiting for transfers between devices  91.3 us (41%)
  Pallas kernels  83.1 us (37%)
  starting transfers between devices  38.8 us (17%)
  blocking collectives  5.19 us (2%)
  other arithmetic  3.08 us (1%)
    ppermute x21, waiting for transfers between devices, send(): return lax.ppermute(x, 'frame', [(i, i ^ m) for i in range(n)])  91.3 us
    ppermute x21, starting transfers between devices, send(): return lax.ppermute(x, 'frame', [(i, i ^ m) for i in range(n)])  38.8 us
    pallas_call x5, Pallas kernels, spatial_attention(): pl.pallas_call(spatial_kernel, grid=(clips, frames, count), in_specs=[spe...  33.6 us
    pallas_call x5, Pallas kernels, temporal_attention(): pl.pallas_call(functools.partial(temporal_kernel, plan, j), grid_spec=plt...  29.2 us
    pallas_call x5, Pallas kernels, combine(): pl.pallas_call(functools.partial(combine_kernel, plan, j), grid_spec=pltp...  10.6 us
    pallas_call x6, Pallas kernels, pack(): pl.pallas_call(functools.partial(pack_kernel, plan, k, m), grid_spec=pltp...  8.93 us
    all_gather x1, blocking collectives, local(): all_codes = lax.all_gather(codes, 'dp', axis=0, tiled=True)  5.19 us
  transfers between devices with their start and end apart: 21, of which 7 were waited for; matrix products, arithmetic and copies ran while one was open for 2% of the time, Pallas kernels for 36%

profile of v9, /device:TPU:0, one launch (start us, length us, event | category | flops | bytes accessed | tf_op | source)
XLA Modules:
  0.0 222.9 jit_solution(2127422445335972776)
XLA Ops:
  1.9 4.0 %collective-permute-start.1 = (bf16[96,1,16,128]{3,2,1,0:T(8,128)(2,1)}, bf16[96,1,16,128]{3,2,1,0:T(8,128)(2,1)S(1)}, u32[]{:S(2)}, u32[]{:S(2)}) collective-permute-start(bf16[96,1,16,128]{3,2,1,0:T(8,128)(2,1)} %pack.7), channel_id=1, source_target_pairs={{0,4},{2,6},{4,0},{6,2},{1,5},{3,7},{5,1},{7,3},{8,12},{10,14},{12... | collective-permute-start | bytes 1179656 | tf_op jit(solution)/shard_map/ppermute | solution.py:502
  18.2 5.2 %all_gather.3 = f32[4,16,32]{2,1,0:T(8,128)S(1)} all-gather(f32[1,16,32]{2,1,0:T(8,128)S(1)} %copy-done.1), channel_id=1, replica_groups=mesh['dp'=4,'frame'=4,'mp'=2] {'dp'}, dimensions={0}, use_global_device_ids=true | all-gather | bytes 10240 | tf_op jit(solution)/shard_map/all_gather | solution.py:539
  26.3 6.7 %spatial.7.spatial_ref = bf16[1,4,128,512]{3,2,1,0:T(8,128)(2,1)S(1)} custom-call(bf16[6,1,4,128,2560]{4,3,2,1,0:T(8,128)(2,1)} %refs_5_.5, bf16[6,1,4,128,2560]{4,3,2,1,0:T(8,128)(2,1)} %refs_5_.5, bf16[6,1,4,128,2560]{4,3,2,1,0:T(8,128)(2,1)} %refs_5_.5), custom_call_target="tpu_custom_call" | custom-call | flops 134217728 | bytes 2097152 | tf_op jit(solution)/shard_map/spatial/pallas_call | solution.py:51
  34.5 6.9 %collective-permute-done.1.refs_4_ = bf16[96,1,16,128]{3,2,1,0:T(8,128)(2,1)S(1)} collective-permute-done((bf16[96,1,16,128]{3,2,1,0:T(8,128)(2,1)}, bf16[96,1,16,128]{3,2,1,0:T(8,128)(2,1)S(1)}, u32[]{:S(2)}, u32[]{:S(2)}) %collective-permute-start.1) | collective-permute-done | bytes 393248 | tf_op jit(solution)/shard_map/ppermute | solution.py:502
  41.4 2.8 %collective-permute-start.5 = (bf16[96,1,16,128]{3,2,1,0:T(8,128)(2,1)S(1)}, bf16[96,1,16,128]{3,2,1,0:T(8,128)(2,1)S(1)}, u32[]{:S(2)}, u32[]{:S(2)}) collective-permute-start(bf16[96,1,16,128]{3,2,1,0:T(8,128)(2,1)S(1)} %pack.11), channel_id=1, source_target_pairs={{0,6},{2,4},{4,2},{6,0},{1,7},{3,5},{5,3},{7,1},{8,14},{10,12},{12... | collective-permute-start | bytes 1179656 | tf_op jit(solution)/shard_map/ppermute | solution.py:502
  44.2 6.7 %spatial.6.spatial_ref = bf16[1,4,128,512]{3,2,1,0:T(8,128)(2,1)S(1)} custom-call(bf16[6,1,4,128,2560]{4,3,2,1,0:T(8,128)(2,1)} %refs_5_.5, bf16[6,1,4,128,2560]{4,3,2,1,0:T(8,128)(2,1)} %refs_5_.5, bf16[6,1,4,128,2560]{4,3,2,1,0:T(8,128)(2,1)} %refs_5_.5), custom_call_target="tpu_custom_call" | custom-call | flops 134217728 | bytes 2097152 | tf_op jit(solution)/shard_map/spatial/pallas_call | solution.py:51
  51.0 7.7 %temporal.5 = (bf16[32,1,16,128]{3,2,1,0:T(8,128)(2,1)S(1)}, bf16[160,1,16,128]{3,2,1,0:T(8,128)(2,1)S(1)}, bf16[116,1,16,128]{3,2,1,0:T(8,128)(2,1)S(1)}, bf16[116,1,16,128]{3,2,1,0:T(8,128)(2,1)S(1)}) custom-call(s32[1]{0:T(128)} %bitcast.me_ref, s32[16]{0:T(128)S(1)} %convert_reduce_fusion.rank_ref, s32[16]{0:T(128)S(1)} %get-tuple-element.61.alone_ref, ...), custom_call_target="tpu_custom_call" | custom-call | flops 268435456 | bytes 3473408 | tf_op jit(solution)/shard_map/temporal/pallas_call | solution.py:317
  60.4 6.4 %collective-permute-done.4.refs_4_ = bf16[96,1,16,128]{3,2,1,0:T(8,128)(2,1)S(1)} collective-permute-done((bf16[96,1,16,128]{3,2,1,0:T(8,128)(2,1)}, bf16[96,1,16,128]{3,2,1,0:T(8,128)(2,1)S(1)}, u32[]{:S(2)}, u32[]{:S(2)}) %collective-permute-start.4) | collective-permute-done | bytes 393248 | tf_op jit(solution)/shard_map/ppermute | solution.py:502
  66.7 2.8 %collective-permute-start.8 = (bf16[116,1,16,128]{3,2,1,0:T(8,128)(2,1)S(1)}, bf16[116,1,16,128]{3,2,1,0:T(8,128)(2,1)S(1)}, u32[]{:S(2)}, u32[]{:S(2)}) collective-permute-start(bf16[116,1,16,128]{3,2,1,0:T(8,128)(2,1)S(1)} %get-tuple-element.39), channel_id=1, source_target_pairs={{0,6},{2,4},{4,2},{6,0},{1,7},{3,5},{5,3},{7,1},{8,14},{10,12},{12... | collective-permute-start | bytes 1425416 | tf_op jit(solution)/shard_map/ppermute | solution.py:502
  69.6 6.7 %spatial.8.spatial_ref = bf16[1,4,128,512]{3,2,1,0:T(8,128)(2,1)S(1)} custom-call(bf16[6,1,4,128,2560]{4,3,2,1,0:T(8,128)(2,1)} %refs_5_.5, bf16[6,1,4,128,2560]{4,3,2,1,0:T(8,128)(2,1)} %refs_5_.5, bf16[6,1,4,128,2560]{4,3,2,1,0:T(8,128)(2,1)} %refs_5_.5), custom_call_target="tpu_custom_call" | custom-call | flops 134217728 | bytes 2097152 | tf_op jit(solution)/shard_map/spatial/pallas_call | solution.py:51
  76.3 7.5 %temporal.6 = (bf16[32,1,16,128]{3,2,1,0:T(8,128)(2,1)S(1)}, bf16[128,1,16,128]{3,2,1,0:T(8,128)(2,1)S(1)}, bf16[116,1,16,128]{3,2,1,0:T(8,128)(2,1)S(1)}, bf16[116,1,16,128]{3,2,1,0:T(8,128)(2,1)S(1)}) custom-call(s32[1]{0:T(128)} %bitcast.me_ref, s32[16]{0:T(128)S(1)} %convert_reduce_fusion.rank_ref, s32[16]{0:T(128)S(1)} %get-tuple-element.61.alone_ref, ...), custom_call_target="tpu_custom_call" | custom-call | flops 268435456 | bytes 3211264 | tf_op jit(solution)/shard_map/temporal/pallas_call | solution.py:317
  84.7 6.7 %spatial.9.spatial_ref = bf16[1,4,128,512]{3,2,1,0:T(8,128)(2,1)S(1)} custom-call(bf16[6,1,4,128,2560]{4,3,2,1,0:T(8,128)(2,1)} %refs_5_.5, bf16[6,1,4,128,2560]{4,3,2,1,0:T(8,128)(2,1)} %refs_5_.5, bf16[6,1,4,128,2560]{4,3,2,1,0:T(8,128)(2,1)} %refs_5_.5), custom_call_target="tpu_custom_call" | custom-call | flops 134217728 | bytes 2097152 | tf_op jit(solution)/shard_map/spatial/pallas_call | solution.py:51
  92.3 23.7 %collective-permute-done.7.refs_4_.refs_2_ = bf16[116,1,16,128]{3,2,1,0:T(8,128)(2,1)S(1)} collective-permute-done((bf16[116,1,16,128]{3,2,1,0:T(8,128)(2,1)S(1)}, bf16[116,1,16,128]{3,2,1,0:T(8,128)(2,1)S(1)}, u32[]{:S(2)}, u32[]{:S(2)}) %collective-permute-start.7) | collective-permute-done | bytes 475168 | tf_op jit(solution)/shard_map/ppermute | solution.py:502
  116.0 7.7 %temporal.7 = (bf16[32,1,16,128]{3,2,1,0:T(8,128)(2,1)S(1)}, bf16[160,1,16,128]{3,2,1,0:T(8,128)(2,1)S(1)}, bf16[116,1,16,128]{3,2,1,0:T(8,128)(2,1)S(1)}, bf16[116,1,16,128]{3,2,1,0:T(8,128)(2,1)S(1)}) custom-call(s32[1]{0:T(128)} %bitcast.me_ref, s32[16]{0:T(128)S(1)} %convert_reduce_fusion.rank_ref, s32[16]{0:T(128)S(1)} %get-tuple-element.61.alone_ref, ...), custom_call_target="tpu_custom_call" | custom-call | flops 268435456 | bytes 3473408 | tf_op jit(solution)/shard_map/temporal/pallas_call | solution.py:317
  123.8 10.8 %collective-permute-start.12 = (bf16[160,1,16,128]{3,2,1,0:T(8,128)(2,1)S(1)}, bf16[160,1,16,128]{3,2,1,0:T(8,128)(2,1)S(1)}, u32[]{:S(2)}, u32[]{:S(2)}) collective-permute-start(bf16[160,1,16,128]{3,2,1,0:T(8,128)(2,1)S(1)} %get-tuple-element.47), channel_id=1, source_target_pairs={{0,2},{2,0},{4,6},{6,4},{1,3},{3,1},{5,7},{7,5},{8,10},{10,8},{12,... | collective-permute-start | bytes 1966088 | tf_op jit(solution)/shard_map/ppermute | solution.py:502
  134.6 2.8 %collective-permute-start.11 = (bf16[116,1,16,128]{3,2,1,0:T(8,128)(2,1)S(1)}, bf16[116,1,16,128]{3,2,1,0:T(8,128)(2,1)S(1)}, u32[]{:S(2)}, u32[]{:S(2)}) collective-permute-start(bf16[116,1,16,128]{3,2,1,0:T(8,128)(2,1)S(1)} %get-tuple-element.44), channel_id=1, source_target_pairs={{0,6},{2,4},{4,2},{6,0},{1,7},{3,5},{5,3},{7,1},{8,14},{10,12},{12... | collective-permute-start | bytes 1425416 | tf_op jit(solution)/shard_map/ppermute | solution.py:502
  139.2 6.7 %spatial.5.spatial_ref = bf16[1,4,128,512]{3,2,1,0:T(8,128)(2,1)S(1)} custom-call(bf16[6,1,4,128,2560]{4,3,2,1,0:T(8,128)(2,1)} %refs_5_.5, bf16[6,1,4,128,2560]{4,3,2,1,0:T(8,128)(2,1)} %refs_5_.5, bf16[6,1,4,128,2560]{4,3,2,1,0:T(8,128)(2,1)} %refs_5_.5), custom_call_target="tpu_custom_call" | custom-call | flops 134217728 | bytes 2097152 | tf_op jit(solution)/shard_map/spatial/pallas_call | solution.py:51
  145.9 17.3 %collective-permute-done.11.refs_5_.refs_3_ = bf16[116,1,16,128]{3,2,1,0:T(8,128)(2,1)S(1)} collective-permute-done((bf16[116,1,16,128]{3,2,1,0:T(8,128)(2,1)S(1)}, bf16[116,1,16,128]{3,2,1,0:T(8,128)(2,1)S(1)}, u32[]{:S(2)}, u32[]{:S(2)}) %collective-permute-start.11) | collective-permute-done | bytes 475168 | tf_op jit(solution)/shard_map/ppermute | solution.py:502
  163.3 3.1 %temporal.8 = (bf16[32,1,16,128]{3,2,1,0:T(8,128)(2,1)S(1)}, bf16[64,1,16,128]{3,2,1,0:T(8,128)(2,1)S(1)}, bf16[32,1,16,128]{3,2,1,0:T(8,128)(2,1)S(1)}, bf16[32,1,16,128]{3,2,1,0:T(8,128)(2,1)S(1)}) custom-call(s32[1]{0:T(128)} %bitcast.me_ref, s32[16]{0:T(128)S(1)} %convert_reduce_fusion.rank_ref, s32[16]{0:T(128)S(1)} %get-tuple-element.61.alone_ref, ...), custom_call_target="tpu_custom_call" | custom-call | flops 268435456 | bytes 1310720 | tf_op jit(solution)/shard_map/temporal/pallas_call | solution.py:317
  167.5 26.7 %collective-permute-done.13.refs_4_.refs_2_ = bf16[116,1,16,128]{3,2,1,0:T(8,128)(2,1)S(1)} collective-permute-done((bf16[116,1,16,128]{3,2,1,0:T(8,128)(2,1)S(1)}, bf16[116,1,16,128]{3,2,1,0:T(8,128)(2,1)S(1)}, u32[]{:S(2)}, u32[]{:S(2)}) %collective-permute-start.13) | collective-permute-done | bytes 475168 | tf_op jit(solution)/shard_map/ppermute | solution.py:502
  194.2 3.1 %temporal.9 = (bf16[32,1,16,128]{3,2,1,0:T(8,128)(2,1)S(1)}, bf16[64,1,16,128]{3,2,1,0:T(8,128)(2,1)S(1)}, bf16[32,1,16,128]{3,2,1,0:T(8,128)(2,1)S(1)}, bf16[32,1,16,128]{3,2,1,0:T(8,128)(2,1)S(1)}) custom-call(s32[1]{0:T(128)} %bitcast.me_ref, s32[16]{0:T(128)S(1)} %convert_reduce_fusion.rank_ref, s32[16]{0:T(128)S(1)} %get-tuple-element.61.alone_ref, ...), custom_call_target="tpu_custom_call" | custom-call | flops 268435456 | bytes 1310720 | tf_op jit(solution)/shard_map/temporal/pallas_call | solution.py:317
  197.4 9.8 %collective-permute-done.16.refs_2_ = bf16[32,1,16,128]{3,2,1,0:T(8,128)(2,1)S(1)} collective-permute-done((bf16[32,1,16,128]{3,2,1,0:T(8,128)(2,1)S(1)}, bf16[32,1,16,128]{3,2,1,0:T(8,128)(2,1)S(1)}, u32[]{:S(2)}, u32[]{:S(2)}) %collective-permute-start.16) | collective-permute-done | bytes 131104 | tf_op jit(solution)/shard_map/ppermute | solution.py:502
  208.2 2.8 %collective-permute-start.19 = (bf16[32,1,16,128]{3,2,1,0:T(8,128)(2,1)S(1)}, bf16[32,1,16,128]{3,2,1,0:T(8,128)(2,1)S(1)}, u32[]{:S(2)}, u32[]{:S(2)}) collective-permute-start(bf16[32,1,16,128]{3,2,1,0:T(8,128)(2,1)S(1)} %get-tuple-element.57), channel_id=1, source_target_pairs={{0,6},{2,4},{4,2},{6,0},{1,7},{3,5},{5,3},{7,1},{8,14},{10,12},{12... | collective-permute-start | bytes 393224 | tf_op jit(solution)/shard_map/ppermute | solution.py:502
  213.7 2.5 %combine.6.refs_7_ = bf16[1,4,128,2560]{3,2,1,0:T(8,128)(2,1)} custom-call(s32[1]{0:T(128)} %bitcast.me_ref, s32[16]{0:T(128)S(1)} %convert_reduce_fusion.rank_ref, s32[16]{0:T(128)S(1)} %get-tuple-element.61.alone_ref, s32[2]{0:T(128)S(1)} %add_bitcast_fusion.kept_ref, ...), custom_call_target="tpu_custom_call", output_to_operand_aliasing={{}: (12, {})} | custom-call | flops 262144 | bytes 1572864 | tf_op jit(solution)/shard_map/combine/pallas_call | solution.py:421
  (72 shorter events, 35.1 us)
Async XLA Ops:
  0.0 34.2 %copy-start = (f32[32,2560]{1,0:T(8,128)S(1)}, f32[32,2560]{1,0:T(8,128)}, u32[]{:S(2)}) copy-start(f32[32,2560]{1,0:T(8,128)} %param.8) | copy-start | bytes 983044
  1.9 39.6 %collective-permute-start.1 = (bf16[96,1,16,128]{3,2,1,0:T(8,128)(2,1)}, bf16[96,1,16,128]{3,2,1,0:T(8,128)(2,1)S(1)}, u32[]{:S(2)}, u32[]{:S(2)}) collective-permute-start(bf16[96,1,16,128]{3,2,1,0:T(8,128)(2,1)} %pack.7), channel_id=1, source_target_pairs={{0,4},{2,6},{4,0},{6,2},{1,5},{3,7},{5,1},{7,3},{8,12},{10,14},{12... | collective-permute-start | bytes 1179656 | tf_op jit(solution)/shard_map/ppermute | solution.py:502
  7.7 43.2 %collective-permute-start.2 = (bf16[96,1,16,128]{3,2,1,0:T(8,128)(2,1)}, bf16[96,1,16,128]{3,2,1,0:T(8,128)(2,1)}, u32[]{:S(2)}, u32[]{:S(2)}) collective-permute-start(bf16[96,1,16,128]{3,2,1,0:T(8,128)(2,1)} %pack.8), channel_id=1, source_target_pairs={{0,6},{2,4},{4,2},{6,0},{1,7},{3,5},{5,3},{7,1},{8,14},{10,12},{12... | collective-permute-start | bytes 1179656 | tf_op jit(solution)/shard_map/ppermute | solution.py:502
  10.9 55.9 %collective-permute-start.4 = (bf16[96,1,16,128]{3,2,1,0:T(8,128)(2,1)}, bf16[96,1,16,128]{3,2,1,0:T(8,128)(2,1)S(1)}, u32[]{:S(2)}, u32[]{:S(2)}) collective-permute-start(bf16[96,1,16,128]{3,2,1,0:T(8,128)(2,1)} %pack.10), channel_id=1, source_target_pairs={{0,4},{2,6},{4,0},{6,2},{1,5},{3,7},{5,1},{7,3},{8,12},{10,14},{12... | collective-permute-start | bytes 1179656 | tf_op jit(solution)/shard_map/ppermute | solution.py:502
  13.8 4.4 %copy-start.1 = (f32[1,16,32]{2,1,0:T(8,128)S(1)}, f32[1,16,32]{2,1,0:T(8,128)}, u32[]{:S(2)}) copy-start(f32[1,16,32]{2,1,0:T(8,128)} %param.7) | copy-start | bytes 6148
  13.8 9.6 %copy-start.2 = (s32[4]{0:T(128)S(1)}, s32[4]{0:T(128)}, u32[]{:S(2)}) copy-start(s32[4]{0:T(128)} %param.9) | copy-start | bytes 52
  13.8 37.2 %collective-permute-start = (bf16[128,1,16,128]{3,2,1,0:T(8,128)(2,1)S(1)}, bf16[128,1,16,128]{3,2,1,0:T(8,128)(2,1)S(1)}, u32[]{:S(2)}, u32[]{:S(2)}) collective-permute-start(bf16[128,1,16,128]{3,2,1,0:T(8,128)(2,1)S(1)} %pack.6), channel_id=1, source_target_pairs={{0,2},{2,0},{4,6},{6,4},{1,3},{3,1},{5,7},{7,5},{8,10},{10,8},{12,... | collective-permute-start | bytes 1572872 | tf_op jit(solution)/shard_map/ppermute | solution.py:502
  16.4 59.9 %collective-permute-start.3 = (bf16[128,1,16,128]{3,2,1,0:T(8,128)(2,1)S(1)}, bf16[128,1,16,128]{3,2,1,0:T(8,128)(2,1)S(1)}, u32[]{:S(2)}, u32[]{:S(2)}) collective-permute-start(bf16[128,1,16,128]{3,2,1,0:T(8,128)(2,1)S(1)} %pack.9), channel_id=1, source_target_pairs={{0,2},{2,0},{4,6},{6,4},{1,3},{3,1},{5,7},{7,5},{8,10},{10,8},{12,... | collective-permute-start | bytes 1572872 | tf_op jit(solution)/shard_map/ppermute | solution.py:502
  41.4 34.9 %collective-permute-start.5 = (bf16[96,1,16,128]{3,2,1,0:T(8,128)(2,1)S(1)}, bf16[96,1,16,128]{3,2,1,0:T(8,128)(2,1)S(1)}, u32[]{:S(2)}, u32[]{:S(2)}) collective-permute-start(bf16[96,1,16,128]{3,2,1,0:T(8,128)(2,1)S(1)} %pack.11), channel_id=1, source_target_pairs={{0,6},{2,4},{4,2},{6,0},{1,7},{3,5},{5,3},{7,1},{8,14},{10,12},{12... | collective-permute-start | bytes 1179656 | tf_op jit(solution)/shard_map/ppermute | solution.py:502
  58.7 57.3 %collective-permute-start.6 = (bf16[160,1,16,128]{3,2,1,0:T(8,128)(2,1)S(1)}, bf16[160,1,16,128]{3,2,1,0:T(8,128)(2,1)S(1)}, u32[]{:S(2)}, u32[]{:S(2)}) collective-permute-start(bf16[160,1,16,128]{3,2,1,0:T(8,128)(2,1)S(1)} %get-tuple-element.37), channel_id=1, source_target_pairs={{0,2},{2,0},{4,6},{6,4},{1,3},{3,1},{5,7},{7,5},{8,10},{10,8},{12,... | collective-permute-start | bytes 1966088 | tf_op jit(solution)/shard_map/ppermute | solution.py:502
  58.8 57.2 %collective-permute-start.7 = (bf16[116,1,16,128]{3,2,1,0:T(8,128)(2,1)S(1)}, bf16[116,1,16,128]{3,2,1,0:T(8,128)(2,1)S(1)}, u32[]{:S(2)}, u32[]{:S(2)}) collective-permute-start(bf16[116,1,16,128]{3,2,1,0:T(8,128)(2,1)S(1)} %get-tuple-element.38), channel_id=1, source_target_pairs={{0,4},{2,6},{4,0},{6,2},{1,5},{3,7},{5,1},{7,3},{8,12},{10,14},{12... | collective-permute-start | bytes 1425416 | tf_op jit(solution)/shard_map/ppermute | solution.py:502
  66.7 49.3 %collective-permute-start.8 = (bf16[116,1,16,128]{3,2,1,0:T(8,128)(2,1)S(1)}, bf16[116,1,16,128]{3,2,1,0:T(8,128)(2,1)S(1)}, u32[]{:S(2)}, u32[]{:S(2)}) collective-permute-start(bf16[116,1,16,128]{3,2,1,0:T(8,128)(2,1)S(1)} %get-tuple-element.39), channel_id=1, source_target_pairs={{0,6},{2,4},{4,2},{6,0},{1,7},{3,5},{5,3},{7,1},{8,14},{10,12},{12... | collective-permute-start | bytes 1425416 | tf_op jit(solution)/shard_map/ppermute | solution.py:502
  83.8 53.6 %collective-permute-start.10 = (bf16[116,1,16,128]{3,2,1,0:T(8,128)(2,1)S(1)}, bf16[116,1,16,128]{3,2,1,0:T(8,128)(2,1)S(1)}, u32[]{:S(2)}, u32[]{:S(2)}) collective-permute-start(bf16[116,1,16,128]{3,2,1,0:T(8,128)(2,1)S(1)} %get-tuple-element.43), channel_id=1, source_target_pairs={{0,4},{2,6},{4,0},{6,2},{1,5},{3,7},{5,1},{7,3},{8,12},{10,14},{12... | collective-permute-start | bytes 1425416 | tf_op jit(solution)/shard_map/ppermute | solution.py:502
  91.4 71.8 %collective-permute-start.9 = (bf16[128,1,16,128]{3,2,1,0:T(8,128)(2,1)S(1)}, bf16[128,1,16,128]{3,2,1,0:T(8,128)(2,1)S(1)}, u32[]{:S(2)}, u32[]{:S(2)}) collective-permute-start(bf16[128,1,16,128]{3,2,1,0:T(8,128)(2,1)S(1)} %get-tuple-element.42), channel_id=1, source_target_pairs={{0,2},{2,0},{4,6},{6,4},{1,3},{3,1},{5,7},{7,5},{8,10},{10,8},{12,... | collective-permute-start | bytes 1572872 | tf_op jit(solution)/shard_map/ppermute | solution.py:502
  123.8 70.5 %collective-permute-start.12 = (bf16[160,1,16,128]{3,2,1,0:T(8,128)(2,1)S(1)}, bf16[160,1,16,128]{3,2,1,0:T(8,128)(2,1)S(1)}, u32[]{:S(2)}, u32[]{:S(2)}) collective-permute-start(bf16[160,1,16,128]{3,2,1,0:T(8,128)(2,1)S(1)} %get-tuple-element.47), channel_id=1, source_target_pairs={{0,2},{2,0},{4,6},{6,4},{1,3},{3,1},{5,7},{7,5},{8,10},{10,8},{12,... | collective-permute-start | bytes 1966088 | tf_op jit(solution)/shard_map/ppermute | solution.py:502
  134.6 28.7 %collective-permute-start.11 = (bf16[116,1,16,128]{3,2,1,0:T(8,128)(2,1)S(1)}, bf16[116,1,16,128]{3,2,1,0:T(8,128)(2,1)S(1)}, u32[]{:S(2)}, u32[]{:S(2)}) collective-permute-start(bf16[116,1,16,128]{3,2,1,0:T(8,128)(2,1)S(1)} %get-tuple-element.44), channel_id=1, source_target_pairs={{0,6},{2,4},{4,2},{6,0},{1,7},{3,5},{5,3},{7,1},{8,14},{10,12},{12... | collective-permute-start | bytes 1425416 | tf_op jit(solution)/shard_map/ppermute | solution.py:502
  137.4 56.8 %collective-permute-start.13 = (bf16[116,1,16,128]{3,2,1,0:T(8,128)(2,1)S(1)}, bf16[116,1,16,128]{3,2,1,0:T(8,128)(2,1)S(1)}, u32[]{:S(2)}, u32[]{:S(2)}) collective-permute-start(bf16[116,1,16,128]{3,2,1,0:T(8,128)(2,1)S(1)} %get-tuple-element.48), channel_id=1, source_target_pairs={{0,4},{2,6},{4,0},{6,2},{1,5},{3,7},{5,1},{7,3},{8,12},{10,14},{12... | collective-permute-start | bytes 1425416 | tf_op jit(solution)/shard_map/ppermute | solution.py:502
  137.4 56.8 %collective-permute-start.14 = (bf16[116,1,16,128]{3,2,1,0:T(8,128)(2,1)S(1)}, bf16[116,1,16,128]{3,2,1,0:T(8,128)(2,1)S(1)}, u32[]{:S(2)}, u32[]{:S(2)}) collective-permute-start(bf16[116,1,16,128]{3,2,1,0:T(8,128)(2,1)S(1)} %get-tuple-element.49), channel_id=1, source_target_pairs={{0,6},{2,4},{4,2},{6,0},{1,7},{3,5},{5,3},{7,1},{8,14},{10,12},{12... | collective-permute-start | bytes 1425416 | tf_op jit(solution)/shard_map/ppermute | solution.py:502
  166.4 40.8 %collective-permute-start.16 = (bf16[32,1,16,128]{3,2,1,0:T(8,128)(2,1)S(1)}, bf16[32,1,16,128]{3,2,1,0:T(8,128)(2,1)S(1)}, u32[]{:S(2)}, u32[]{:S(2)}) collective-permute-start(bf16[32,1,16,128]{3,2,1,0:T(8,128)(2,1)S(1)} %get-tuple-element.53), channel_id=1, source_target_pairs={{0,4},{2,6},{4,0},{6,2},{1,5},{3,7},{5,1},{7,3},{8,12},{10,14},{12... | collective-permute-start | bytes 393224 | tf_op jit(solution)/shard_map/ppermute | solution.py:502
  166.5 41.7 %collective-permute-start.18 = (bf16[32,1,16,128]{3,2,1,0:T(8,128)(2,1)S(1)}, bf16[32,1,16,128]{3,2,1,0:T(8,128)(2,1)S(1)}, u32[]{:S(2)}, u32[]{:S(2)}) collective-permute-start(bf16[32,1,16,128]{3,2,1,0:T(8,128)(2,1)S(1)} %get-tuple-element.56), channel_id=1, source_target_pairs={{0,6},{2,4},{4,2},{6,0},{1,7},{3,5},{5,3},{7,1},{8,14},{10,12},{12... | collective-permute-start | bytes 393224 | tf_op jit(solution)/shard_map/ppermute | solution.py:502
  194.2 19.5 %collective-permute-start.20 = (bf16[64,1,16,128]{3,2,1,0:T(8,128)(2,1)S(1)}, bf16[64,1,16,128]{3,2,1,0:T(8,128)(2,1)S(1)}, u32[]{:S(2)}, u32[]{:S(2)}) collective-permute-start(bf16[64,1,16,128]{3,2,1,0:T(8,128)(2,1)S(1)} %get-tuple-element.58), channel_id=1, source_target_pairs={{0,2},{2,0},{4,6},{6,4},{1,3},{3,1},{5,7},{7,5},{8,10},{10,8},{12,... | collective-permute-start | bytes 786440 | tf_op jit(solution)/shard_map/ppermute | solution.py:502
  207.2 9.1 %collective-permute-start.17 = (bf16[64,1,16,128]{3,2,1,0:T(8,128)(2,1)S(1)}, bf16[64,1,16,128]{3,2,1,0:T(8,128)(2,1)S(1)}, u32[]{:S(2)}, u32[]{:S(2)}) collective-permute-start(bf16[64,1,16,128]{3,2,1,0:T(8,128)(2,1)S(1)} %get-tuple-element.54), channel_id=1, source_target_pairs={{0,2},{2,0},{4,6},{6,4},{1,3},{3,1},{5,7},{7,5},{8,10},{10,8},{12,... | collective-permute-start | bytes 786440 | tf_op jit(solution)/shard_map/ppermute | solution.py:502
  208.2 12.1 %collective-permute-start.19 = (bf16[32,1,16,128]{3,2,1,0:T(8,128)(2,1)S(1)}, bf16[32,1,16,128]{3,2,1,0:T(8,128)(2,1)S(1)}, u32[]{:S(2)}, u32[]{:S(2)}) collective-permute-start(bf16[32,1,16,128]{3,2,1,0:T(8,128)(2,1)S(1)} %get-tuple-element.57), channel_id=1, source_target_pairs={{0,6},{2,4},{4,2},{6,0},{1,7},{3,5},{5,3},{7,1},{8,14},{10,12},{12... | collective-permute-start | bytes 393224 | tf_op jit(solution)/shard_map/ppermute | solution.py:502
  211.0 11.2 %collective-permute-start.15 = (bf16[32,1,16,128]{3,2,1,0:T(8,128)(2,1)S(1)}, bf16[32,1,16,128]{3,2,1,0:T(8,128)(2,1)S(1)}, u32[]{:S(2)}, u32[]{:S(2)}) collective-permute-start(bf16[32,1,16,128]{3,2,1,0:T(8,128)(2,1)S(1)} %get-tuple-element.50), channel_id=1, source_target_pairs={{0,4},{2,6},{4,0},{6,2},{1,5},{3,7},{5,1},{7,3},{8,12},{10,14},{12... | collective-permute-start | bytes 393224 | tf_op jit(solution)/shard_map/ppermute | solution.py:502
  (2 other events, 7.3 us)
